TPU v7x, 256 devices: a whole 4x4x8 slice. The times are simulated.
256 devices in a mesh: rows: 128 (over z, x, y), cols: 2 (over core).
Axes of the slice: x: 4, y: 4, z: 8, core: 2. Of those that a mesh axis runs over, the one named last changes fastest.
Arguments:
- vectors: float32 [64, 393216], P('cols', 'rows'), may hold values from -45 to 45
- directions: float32 [64, 393216], P('cols', 'rows'), may hold values from -6 to 6
- affinity: float32 [3072, 6, 128, 128], P('rows'), may hold values from 0.01 to 1, as said below
- pattern: int32 [3072, 6], P('rows'), may hold values from 0 to 3071, as said below
- rotation: float32 [192, 64], replicated, may hold values from -0.4375 to 0.4375
Outputs:
- new_vectors: float32 [64, 393216], P('cols', 'rows')
- new_directions: float32 [64, 393216], P('cols', 'rows')
- ritz_matrix: float32 [192, 192], replicated
Inputs may be any that keep to these rules, and one draw needn't show every extreme that they name: Block row i has pattern[i, 0] = i; its 6 indices are distinct, block j appears in row i exactly when block i appears in row j, and each lies, modulo 3072, among the block rows of its own index of rows and of the two indices beside it (the first and last indices count as beside each other). The affinity matrix is symmetric as the steps state.
All inputs are finite; a program needn't handle non-finite values.
Results may differ from a plain program's by a relative error of at most 0.0015.
Values sent between devices are 32-bit elements; how exact they have to be, the bound alone decides.
No kernel may reach another device: no remote copies, remote signals or barrier semaphores. Data moves between devices by JAX's collectives and lax.ppermute only.
A program may use at most 64 MiB of HBM per device.

v0:
```python
import math

import jax
import jax.numpy as jnp
import numpy as np
from jax import lax
from jax.sharding import PartitionSpec as P

BLK = 128


def with_halo(x, sides, width):
    for axis, dim in sides:
        devices, length = (lax.axis_size(axis), x.shape[dim])
        up = [(i, (i + 1) % devices) for i in range(devices)]
        down = [(j, i) for i, j in up]
        last = lax.slice_in_dim(x, length - width, length, axis=dim)
        initial = lax.slice_in_dim(x, 0, width, axis=dim)
        before = lax.ppermute(last, axis, up)
        after = lax.ppermute(initial, axis, down)
        x = jnp.concatenate([before, x, after], axis=dim)
    return x


def exact_dot(left, right):
    return jnp.dot(left, right, precision=lax.Precision.HIGHEST)


def block_image(extended, panel, affinity, pattern, scale):
    count = panel.shape[0]
    local_blocks = affinity.shape[0]
    all_blocks = local_blocks * lax.axis_size("rows")
    first_block = (lax.axis_index("rows") - 1) * local_blocks
    local_index = (pattern - first_block + all_blocks) % all_blocks
    blocks = extended.reshape(count, 3 * local_blocks, BLK)
    picked = jnp.take(blocks, local_index, axis=1)
    image = jnp.einsum("cikn,ikmn->cim", picked, affinity, precision=lax.Precision.HIGHEST)
    return panel - scale[None, :] * image.reshape(count, -1)


def canonical_order(parts, width):
    total = width * parts
    listed = [
        panel_id * total + owner * width + column
        for owner in range(parts)
        for panel_id in range(3)
        for column in range(width)
    ]
    return np.array(listed, dtype=np.int32)


def local(vectors, directions, affinity, pattern, rotation):
    width = vectors.shape[0]
    rows_dev = vectors.shape[1]
    parts = lax.axis_size("cols")
    owner = lax.axis_index("cols")
    total = width * parts
    nodes = rows_dev * lax.axis_size("rows")
    scale = lax.rsqrt(jnp.sum(affinity, axis=(1, 3)).reshape(-1))
    paired = jnp.concatenate([vectors, directions], axis=0)
    spread = with_halo(scale[None, :] * paired, (("rows", 1),), rows_dev)
    paired_image = block_image(spread, paired, affinity, pattern, scale)
    image_x = paired_image[:width]
    image_p = paired_image[width:]
    sums = lax.psum(
        (jnp.sum(vectors * image_x, axis=1), jnp.sum(vectors * vectors, axis=1)), "rows"
    )
    quotient = sums[0] / sums[1]
    second = image_x - quotient[:, None] * vectors
    beyond = with_halo(scale[None, :] * second, (("rows", 1),), rows_dev)
    second_image = block_image(beyond, second, affinity, pattern, scale)
    local_panel = jnp.concatenate([second, vectors, directions], axis=0)
    local_image = jnp.concatenate([second_image, image_x, image_p], axis=0)
    whole_panel, whole_image = (
        lax.all_gather(local_panel, "cols", axis=0, tiled=True),
        lax.all_gather(local_image, "cols", axis=0, tiled=True),
    )
    half_gram = exact_dot(local_panel, whole_panel.T)
    half_raw = exact_dot(local_panel, whole_image.T)
    summed_gram, summed_raw = lax.psum((half_gram, half_raw), "rows")
    gram_g, raw_g = (
        lax.all_gather(summed_gram, "cols", axis=0, tiled=True),
        lax.all_gather(summed_raw, "cols", axis=0, tiled=True),
    )
    order = canonical_order(parts, width)
    position = np.argsort(order).astype(np.int32)
    gram = gram_g[position][:, position]
    raw = raw_g[position][:, position]
    identity = jnp.eye(3 * total, dtype=jnp.float32)
    lower = jnp.linalg.cholesky(gram)
    inverse = jax.scipy.linalg.solve_triangular(lower, identity, lower=True)
    ritz_matrix = exact_dot(exact_dot(inverse, raw), inverse.T)
    kept = jnp.concatenate(
        [rotation[:total], jnp.zeros((total, total), jnp.float32), rotation[2 * total :]], axis=0
    )
    mixing = exact_dot(inverse.T, rotation)
    trailing = exact_dot(inverse.T, kept)
    combined = jnp.concatenate([mixing, trailing], axis=1)
    gathered_rows = combined[order]
    own_vectors = lax.dynamic_slice_in_dim(gathered_rows, owner * width, width, 1)
    own_directions = lax.dynamic_slice_in_dim(gathered_rows, total + owner * width, width, 1)
    selected = jnp.concatenate([own_vectors, own_directions], axis=1)
    result = math.sqrt(nodes) * exact_dot(selected.T, whole_panel)
    return (result[:width], result[width:], ritz_matrix)


def solution(mesh):
    in_specs = (
        P("cols", "rows"),
        P("cols", "rows"),
        P("rows", None, None, None),
        P("rows", None),
        P(),
    )
    out_specs = (P("cols", "rows"), P("cols", "rows"), P())
    return jax.shard_map(local, mesh=mesh, in_specs=in_specs, out_specs=out_specs, check_vma=False)
```

profile of v0, /device:TPU:1, one launch (start us, length us, event | category | flops | bytes accessed | tf_op | source)
XLA Modules:
  0.0 747.2 jit_solution(9850285343485458750)
XLA Ops:
  7.2 4.2 reduce_sum.27
  11.7 2.2 collective-permute-start
  13.9 9.0 %collective-permute-start.1 = (f32[64,3072]{1,0:T(8,128)S(1)}, f32[64,3072]{1,0:T(8,128)}, u32[]{:S(2)}, u32[]{:S(2)}) collective-permute-start(f32[64,3072]{1,0:T(8,128)S(1)} %broadcast_multiply_fusion), channel_id=1, source_target_pairs={{2,0},{4,2},{6,4},{8,6},{10,8},{12,10},{14,12},{16,14},{18,16},{20... | collective-permute-start | bytes 2359304 | tf_op jit(solution)/shard_map/ppermute | solution.py:20
  23.2 16.9 %collective-permute-done = f32[64,3072]{1,0:T(8,128)S(1)} collective-permute-done((f32[64,3072]{1,0:T(8,128)S(1)}, f32[64,3072]{1,0:T(8,128)S(1)}, u32[]{:S(2)}, u32[]{:S(2)}) %collective-permute-start) | collective-permute-done | bytes 786464 | tf_op jit(solution)/shard_map/ppermute | solution.py:19
  40.1 0.9 copy-done.6
  40.9 1.9 copy_bitcast_fusion
  42.9 3.0 gather_fusion
  45.9 13.5 %fusion.8 = f32[24,8,8,128]{3,2,1,0:T(8,128)S(1)} fusion(f32[24,6,128,128]{3,2,1,0:T(8,128)} %param.14, f32[24,6,64,128]{3,2,1,0:T(8,128)} %bitcast.77, pred[24,6]{1,0:T(8,128)(4,1)S(1)} %copy.38), kind=kOutput, calls=%fused_computation.18 | convolution fusion | flops 1813118976 | bytes 14942352 | tf_op jit(solution)/shard_map/cikn,ikmn->cim/dot_general | solution.py:37
  59.6 293.1 %all-reduce.3 = (f32[32]{0:T(128)S(1)}, f32[32]{0:T(128)S(1)}) all-reduce(f32[32]{0:T(128)S(1)} %get-tuple-element.24, f32[32]{0:T(128)S(1)} %get-tuple-element.23), channel_id=1, replica_groups=mesh['rows'=128,'cols'=2] {'rows'}, use_global_device_ids=true, to_apply=%region_2.3 | all-reduce | flops 64 | bytes 512 | tf_op jit(solution)/shard_map/psum | solution.py:65
  352.9 1.1 pad_maximum_fusion
  354.2 6.9 collective-permute-start.3
  361.1 5.2 collective-permute-done.2
  366.4 2.2 gather_fusion.4
  368.7 12.4 %fusion.11 = f32[24,4,8,128]{3,2,1,0:T(8,128)S(1)} fusion(f32[24,6,128,128]{3,2,1,0:T(8,128)} %param.14, f32[24,6,32,128]{3,2,1,0:T(8,128)} %bitcast.78, pred[24,6]{1,0:T(8,128)(4,1)S(1)} %copy-done.10), kind=kOutput, calls=%fused_computation.19 | convolution fusion | flops 906559488 | bytes 12189840 | tf_op jit(solution)/shard_map/cikn,ikmn->cim/dot_general | solution.py:37
  381.2 1.1 pad_maximum_fusion.1
  382.5 39.4 %all-gather.3.cloned.1.call-done = f32[192,3072]{1,0:T(8,128)} async-done(((f32[96,3072]{1,0:T(8,128)}), f32[192,3072]{1,0:T(8,128)}) %all-gather.3.cloned.1.call-update) | async-done | bytes 2359312 | tf_op jit(solution)/shard_map/all_gather | solution.py:75
  421.9 4.7 fusion.47
  426.6 29.5 %all-gather.5.cloned.1.call-done = f32[192,3072]{1,0:T(8,128)} async-done(((f32[96,3072]{1,0:T(8,128)}), f32[192,3072]{1,0:T(8,128)}) %all-gather.5.cloned.1.call-update) | async-done | bytes 2359312 | tf_op jit(solution)/shard_map/all_gather | solution.py:76
  456.1 4.7 fusion.46
  461.0 209.3 %all-reduce.7.cloned.1.call-done = (f32[96,192]{1,0:T(8,128)}, f32[96,192]{1,0:T(8,128)}) async-done(((f32[96,192]{1,0:T(8,128)}, f32[96,192]{1,0:T(8,128)}), (f32[96,192]{1,0:T(8,128)}, f32[96,192]{1,0:T(8,128)})) %all-reduce.7.cloned.1.call-update) | async-done | bytes 147472 | tf_op jit(solution)/shard_map/psum | solution.py:80
  670.4 7.2 all_gather.13
  677.5 0.9 gather_fusion.1
  678.5 0.9 gather_fusion.2
  679.5 11.7 %cholesky.51 = f32[128,128]{1,0:T(8,128)S(1)} custom-call(f32[128,128]{1,0:T(8,128)S(1)} %cholesky.124), custom_call_target="Cholesky" | custom-call | tf_op jit(solution)/shard_map/jit(cholesky)/cholesky | solution.py:90
  691.3 9.8 %custom-call.15 = f32[1,128,128]{1,2,0:T(8,128)S(1)} custom-call(f32[1,128,128]{2,1,0:T(8,128)S(1)} %get-tuple-element.38), custom_call_target="InvertDiagBlocksLowerTriangular" | custom-call | tf_op jit(solution)/shard_map/jit(cholesky)/cholesky | solution.py:90
  701.5 5.8 cholesky.110
  710.1 19.7 %custom-call.16 = f32[2,128,128]{1,2,0:T(8,128)S(1)} custom-call(f32[2,128,128]{2,1,0:T(8,128)S(1)} %pad_maximum_fusion.3), custom_call_target="InvertDiagBlocksLowerTriangular" | custom-call | tf_op jit(solution)/shard_map/jit(_solve_triangular)/triangular_solve | solution.py:91
  730.8 2.2 all_gather.15
  734.0 0.9 gather_fusion.6
  735.8 1.0 fusion.30
  738.1 1.6 convolution_multiply_fusion
  739.7 0.9 fusion.48
  (87 shorter events, 7.8 us)
Async XLA Ops:
  7.2 4.3 copy-start
  7.2 4.4 copy-start.2
  7.2 414.7 %all-gather.3.cloned.1.call-start = ((), (), s32[]{:S(2)}) async-start(), calls=%async_computation | async-start | bytes 3538944 | tf_op jit(solution)/shard_map/all_gather | solution.py:75
  11.5 11.4 %copy-start.11 = (s32[24,6]{0,1:T(8,128)S(1)}, s32[24,6]{0,1:T(8,128)}, u32[]{:S(2)}) copy-start(s32[24,6]{0,1:T(8,128)} %param.15) | copy-start | bytes 1732
  11.6 28.5 %copy-start.3 = (f32[64,3072]{1,0:T(8,128)}, f32[64,3072]{1,0:T(8,128)S(1)}, u32[]{:S(2)}) copy-start(f32[64,3072]{1,0:T(8,128)S(1)} %constant_dynamic-update-slice_fusion) | copy-start | bytes 2359300
  11.7 28.4 %copy-start.5 = (f32[64,3072]{1,0:T(8,128)}, f32[64,3072]{1,0:T(8,128)S(1)}, u32[]{:S(2)}) copy-start(f32[64,3072]{1,0:T(8,128)S(1)} %broadcast_multiply_fusion) | copy-start | bytes 2359300
  11.7 28.4 %collective-permute-start = (f32[64,3072]{1,0:T(8,128)S(1)}, f32[64,3072]{1,0:T(8,128)S(1)}, u32[]{:S(2)}, u32[]{:S(2)}) collective-permute-start(f32[64,3072]{1,0:T(8,128)S(1)} %broadcast_multiply_fusion), channel_id=1, source_target_pairs={{0,2},{2,4},{4,6},{6,8},{8,10},{10,12},{12,14},{14,16},{16,18},{18... | collective-permute-start | bytes 2359304 | tf_op jit(solution)/shard_map/ppermute | solution.py:19
  13.9 27.1 %collective-permute-start.1 = (f32[64,3072]{1,0:T(8,128)S(1)}, f32[64,3072]{1,0:T(8,128)}, u32[]{:S(2)}, u32[]{:S(2)}) collective-permute-start(f32[64,3072]{1,0:T(8,128)S(1)} %broadcast_multiply_fusion), channel_id=1, source_target_pairs={{2,0},{4,2},{6,4},{8,6},{10,8},{12,10},{14,12},{16,14},{18,16},{20... | collective-permute-start | bytes 2359304 | tf_op jit(solution)/shard_map/ppermute | solution.py:20
  23.2 22.7 %copy-start.9 = (pred[24,6]{1,0:T(8,128)(4,1)}, pred[24,6]{1,0:T(8,128)(4,1)S(1)}, u32[]{:S(2)}) copy-start(pred[24,6]{1,0:T(8,128)(4,1)S(1)} %copy.38) | copy-start | bytes 436
  40.1 0.9 copy-start.6
  45.9 13.5 %copy-start.4 = (f32[64,3072]{1,0:T(8,128)S(1)}, f32[64,3072]{1,0:T(8,128)}, u32[]{:S(2)}) copy-start(f32[64,3072]{1,0:T(8,128)} %copy-done.3) | copy-start | bytes 2359300
  354.0 102.0 %all-gather.5.cloned.1.call-start = ((), (), s32[]{:S(2)}) async-start(), calls=%async_computation.1 | async-start | bytes 3538944 | tf_op jit(solution)/shard_map/all_gather | solution.py:76
  354.1 12.2 %collective-permute-start.2 = (f32[32,3072]{1,0:T(8,128)S(1)}, f32[32,3072]{1,0:T(8,128)S(1)}, u32[]{:S(2)}, u32[]{:S(2)}) collective-permute-start(f32[32,3072]{1,0:T(8,128)S(1)} %get-tuple-element.29), channel_id=1, source_target_pairs={{0,2},{2,4},{4,6},{6,8},{8,10},{10,12},{12,14},{14,16},{16,18},{18... | collective-permute-start | bytes 1179656 | tf_op jit(solution)/shard_map/ppermute | solution.py:19
  354.2 12.1 %collective-permute-start.3 = (f32[32,3072]{1,0:T(8,128)S(1)}, f32[32,3072]{1,0:T(8,128)S(1)}, u32[]{:S(2)}, u32[]{:S(2)}) collective-permute-start(f32[32,3072]{1,0:T(8,128)S(1)} %get-tuple-element.29), channel_id=1, source_target_pairs={{2,0},{4,2},{6,4},{8,6},{10,8},{12,10},{14,12},{16,14},{18,16},{20... | collective-permute-start | bytes 1179656 | tf_op jit(solution)/shard_map/ppermute | solution.py:20
  366.4 2.3 copy-start.10
  381.1 1.3 copy-start.13
  381.1 1.4 copy-start.7
  382.3 288.0 %all-reduce.7.cloned.1.call-start = ((), (), s32[]{:S(2)}) async-start(), calls=%async_computation.2 | async-start | bytes 393216 | tf_op jit(solution)/shard_map/psum | solution.py:80
  426.6 34.2 %copy-start.12 = (s32[192]{0:T(256)S(1)}, s32[192]{0:T(256)}, u32[]{:S(2)}) copy-start(s32[192]{0:T(256)} %constant.201) | copy-start | bytes 2308
  678.5 52.3 %copy-start.8 = (f32[96,192]{1,0:T(8,128)S(1)}, f32[96,192]{1,0:T(8,128)}, u32[]{:S(2)}) copy-start(f32[96,192]{1,0:T(8,128)} %get-tuple-element.28) | copy-start | bytes 221188
  734.0 4.1 copy-start.1
Sparse Core Ops, SparseCore 0:
  354.2 67.6 all-gather.2
  423.7 32.3 all-gather.4
  462.2 208.1 all-reduce.6
where the time goes:
time: 747 us
  blocking collectives  302 us (40%)
  waiting for transfers between devices  300 us (40%)
  other arithmetic  57.7 us (8%)
  matrix products  40.5 us (5%)
  starting transfers between devices  18.3 us (2%)
  between operations  15.5 us (2%)
  local copies, waits for them, and re-layouts  12.3 us (2%)
    psum x1, blocking collectives, local(): lax.psum((jnp.sum(vectors * image_x, axis=1), jnp.sum(vectors * vectors,...  293 us
    psum x1, waiting for transfers between devices, local(): summed_gram, summed_raw = lax.psum((half_gram, half_raw), 'rows')  209 us
    all_gather x1, waiting for transfers between devices, local(): lax.all_gather(local_panel, 'cols', axis=0, tiled=True)  39.4 us
    all_gather x1, waiting for transfers between devices, local(): lax.all_gather(local_image, 'cols', axis=0, tiled=True)  29.5 us
    another operation x7, other arithmetic, local(): lower = jnp.linalg.cholesky(gram)  28.7 us
    dot_general x2, matrix products, block_image(): jnp.einsum('cikn,ikmn->cim', picked, affinity, precision=lax.Precision.HI...  25.9 us
    ppermute x2, waiting for transfers between devices, with_halo(): before = lax.ppermute(last, axis, up)  22.1 us
    another operation x6, other arithmetic, local(): inverse = jax.scipy.linalg.solve_triangular(lower, identity, lower=True)  19.8 us
  transfers between devices with their start and end apart: 7, of which 5 were waited for; matrix products, arithmetic and copies ran while one was open for 3% of the time, Pallas kernels for 0%

commit v1 on v0

--- a/solution.py
+++ b/solution.py
@@ -38,6 +38,30 @@
     return panel - scale[None, :] * image.reshape(count, -1)
 
 
+def plane_groups():
+    return [[z * 16 + i for i in range(16)] for z in range(8)]
+
+
+def column_groups():
+    return [[z * 16 + i for z in range(8)] for i in range(16)]
+
+
+def exchange(x, groups):
+    return lax.all_to_all(x, "rows", 0, 0, axis_index_groups=groups)
+
+
+def sum_small(x):
+    everyone = lax.all_to_all(jnp.broadcast_to(x[None], (128,) + x.shape), "rows", 0, 0)
+    return jnp.sum(everyone, axis=0)
+
+
+def sum_large(x):
+    plane, column = plane_groups(), column_groups()
+    part = jnp.sum(exchange(x, plane), axis=0)
+    part = jnp.sum(exchange(jnp.broadcast_to(part[None], (8,) + part.shape), column), axis=0)
+    return exchange(jnp.broadcast_to(part[None], (16,) + part.shape), plane)
+
+
 def canonical_order(parts, width):
     total = width * parts
     listed = [
@@ -62,9 +86,9 @@
     paired_image = block_image(spread, paired, affinity, pattern, scale)
     image_x = paired_image[:width]
     image_p = paired_image[width:]
-    sums = lax.psum(
-        (jnp.sum(vectors * image_x, axis=1), jnp.sum(vectors * vectors, axis=1)), "rows"
-    )
+    sums = sum_small(
+        jnp.concatenate([jnp.sum(vectors * image_x, axis=1), jnp.sum(vectors * vectors, axis=1)]).reshape(1, 2 * width)
+    ).reshape(2, width)
     quotient = sums[0] / sums[1]
     second = image_x - quotient[:, None] * vectors
     beyond = with_halo(scale[None, :] * second, (("rows", 1),), rows_dev)
@@ -77,7 +101,9 @@
     )
     half_gram = exact_dot(local_panel, whole_panel.T)
     half_raw = exact_dot(local_panel, whole_image.T)
-    summed_gram, summed_raw = lax.psum((half_gram, half_raw), "rows")
+    both = jnp.concatenate([half_gram, half_raw], axis=0).reshape(16, 12, 6 * width)
+    both = sum_large(both).reshape(6 * width, 6 * width)
+    summed_gram, summed_raw = both[: 3 * width], both[3 * width :]
     gram_g, raw_g = (
         lax.all_gather(summed_gram, "cols", axis=0, tiled=True),
         lax.all_gather(summed_raw, "cols", axis=0, tiled=True),

time: 747 us -> 252 us (0.34)
  blocking collectives: 302 us -> 28.9 us
  waiting for transfers between devices: 300 us -> 60 us
  starting transfers between devices: 18.3 us -> 34.9 us
    psum x1 -> x0, blocking collectives: 293 us -> none  [local(): lax.psum((jnp.sum(vectors * image_x, axis=1), jnp.sum(vectors * vectors,...]
    psum x1 -> x0, waiting for transfers between devices: 209 us -> none  [local(): summed_gram, summed_raw = lax.psum((half_gram, half_raw), 'rows')]
    all_gather x1, waiting for transfers between devices: 39.4 us -> 0.02 us  [local(): lax.all_gather(local_panel, 'cols', axis=0, tiled=True)]
    all_to_all x0 -> x3, waiting for transfers between devices: none -> 22.8 us  [exchange(): return lax.all_to_all(x, 'rows', 0, 0, axis_index_groups=groups)]
    all_to_all x0 -> x1, blocking collectives: none -> 20.7 us  [sum_small(): lax.all_to_all(jnp.broadcast_to(x[None], (128,) + x.shape), 'rows', 0, 0)]
    all_to_all x0 -> x3, starting transfers between devices: none -> 16.6 us  [exchange(): return lax.all_to_all(x, 'rows', 0, 0, axis_index_groups=groups)]
    all_gather x1, waiting for transfers between devices: 29.5 us -> 14.5 us  [local(): lax.all_gather(local_image, 'cols', axis=0, tiled=True)]
  transfers between devices with their start and end apart: 7 -> 9, of which waited for: 5 -> 6; matrix products, arithmetic and copies ran while one was open for 3% -> 8% of each run, Pallas kernels for 0% -> 0%
where the time goes in v1:
time: 252 us
  waiting for transfers between devices  60 us (24%)
  other arithmetic  58.1 us (23%)
  matrix products  39.2 us (16%)
  starting transfers between devices  34.9 us (14%)
  blocking collectives  28.9 us (11%)
  between operations  15.9 us (6%)
  local copies, waits for them, and re-layouts  14.6 us (6%)
    another operation x7, other arithmetic, local(): lower = jnp.linalg.cholesky(gram)  28.7 us
    dot_general x2, matrix products, block_image(): jnp.einsum('cikn,ikmn->cim', picked, affinity, precision=lax.Precision.HI...  25.9 us
    all_to_all x3, waiting for transfers between devices, exchange(): return lax.all_to_all(x, 'rows', 0, 0, axis_index_groups=groups)  22.8 us
    ppermute x2, waiting for transfers between devices, with_halo(): before = lax.ppermute(last, axis, up)  22.7 us
    all_to_all x1, blocking collectives, sum_small(): lax.all_to_all(jnp.broadcast_to(x[None], (128,) + x.shape), 'rows', 0, 0)  20.7 us
    another operation x6, other arithmetic, local(): inverse = jax.scipy.linalg.solve_triangular(lower, identity, lower=True)  19.8 us
    all_to_all x3, starting transfers between devices, exchange(): return lax.all_to_all(x, 'rows', 0, 0, axis_index_groups=groups)  16.6 us
    ppermute x2, starting transfers between devices, with_halo(): after = lax.ppermute(initial, axis, down)  15.6 us
  transfers between devices with their start and end apart: 9, of which 6 were waited for; matrix products, arithmetic and copies ran while one was open for 8% of the time, Pallas kernels for 0%

profile of v1, /device:TPU:1, one launch (start us, length us, event | category | flops | bytes accessed | tf_op | source)
XLA Modules:
  0.0 251.6 jit_solution(2049715893752065225)
XLA Ops:
  7.2 4.2 %reduce_sum.56 = f32[24,128]{1,0:T(8,128)S(1)} reduce(f32[24,6,128,128]{3,2,1,0:T(8,128)} %param.14, f32[]{:T(128)} %constant.144.clone.1), dimensions={1,3}, to_apply=%region_0.0 | reduce | flops 2356224 | bytes 9449476 | tf_op jit(solution)/shard_map/reduce_sum | solution.py:83
  11.7 2.2 collective-permute-start
  13.9 9.0 %collective-permute-start.1 = (f32[64,3072]{1,0:T(8,128)S(1)}, f32[64,3072]{1,0:T(8,128)}, u32[]{:S(2)}, u32[]{:S(2)}) collective-permute-start(f32[64,3072]{1,0:T(8,128)S(1)} %broadcast_multiply_fusion), channel_id=1, source_target_pairs={{2,0},{4,2},{6,4},{8,6},{10,8},{12,10},{14,12},{16,14},{18,16},{20... | collective-permute-start | bytes 2359304 | tf_op jit(solution)/shard_map/ppermute | solution.py:20
  23.2 16.9 %collective-permute-done = f32[64,3072]{1,0:T(8,128)S(1)} collective-permute-done((f32[64,3072]{1,0:T(8,128)S(1)}, f32[64,3072]{1,0:T(8,128)S(1)}, u32[]{:S(2)}, u32[]{:S(2)}) %collective-permute-start) | collective-permute-done | bytes 786464 | tf_op jit(solution)/shard_map/ppermute | solution.py:19
  40.9 1.9 copy_bitcast_fusion
  42.9 3.0 %gather_fusion = f32[144,64,128]{2,1,0:T(8,128)} fusion(f32[64,72,128]{2,0,1:T(8,128)S(1)} %copy_bitcast_fusion, s32[1024]{0:T(1024)S(1)} %pad_clamp_fusion.2), kind=kCustom, calls=%fused_computation | custom fusion | bytes 9437760 | tf_op jit(solution)/shard_map/jit(_take)/gather | solution.py:36
  45.9 13.5 %fusion.8 = f32[24,8,8,128]{3,2,1,0:T(8,128)S(1)} fusion(f32[24,6,128,128]{3,2,1,0:T(8,128)} %param.14, f32[24,6,64,128]{3,2,1,0:T(8,128)} %bitcast.80, pred[24,6]{1,0:T(8,128)(4,1)S(1)} %copy.66), kind=kOutput, calls=%fused_computation.18 | convolution fusion | flops 1813118976 | bytes 14942352 | tf_op jit(solution)/shard_map/cikn,ikmn->cim/dot_general | solution.py:37
  59.8 20.7 %all_to_all.20 = f32[128,1,64]{2,1,0:T(1,128)S(1)} all-to-all(f32[128,1,64]{2,1,0:T(1,128)S(1)} %broadcast_in_dim.65), channel_id=1, replica_groups=mesh['rows'=128,'cols'=2] {'rows'}, dimensions={0} | all-to-all | bytes 65536 | tf_op jit(solution)/shard_map/all_to_all | solution.py:54
  80.9 1.2 pad_maximum_fusion
  82.5 6.6 %collective-permute-start.3 = (f32[32,3072]{1,0:T(8,128)S(1)}, f32[32,3072]{1,0:T(8,128)S(1)}, u32[]{:S(2)}, u32[]{:S(2)}) collective-permute-start(f32[32,3072]{1,0:T(8,128)S(1)} %get-tuple-element.25), channel_id=1, source_target_pairs={{2,0},{4,2},{6,4},{8,6},{10,8},{12,10},{14,12},{16,14},{18,16},{20... | collective-permute-start | bytes 1179656 | tf_op jit(solution)/shard_map/ppermute | solution.py:20
  89.1 5.8 %collective-permute-done.2 = f32[32,3072]{1,0:T(8,128)S(1)} collective-permute-done((f32[32,3072]{1,0:T(8,128)S(1)}, f32[32,3072]{1,0:T(8,128)S(1)}, u32[]{:S(2)}, u32[]{:S(2)}) %collective-permute-start.2) | collective-permute-done | bytes 393248 | tf_op jit(solution)/shard_map/ppermute | solution.py:19
  95.1 2.2 gather_fusion.1
  97.3 12.4 %fusion.11 = f32[24,4,8,128]{3,2,1,0:T(8,128)S(1)} fusion(f32[24,6,128,128]{3,2,1,0:T(8,128)} %param.14, f32[24,6,32,128]{3,2,1,0:T(8,128)} %bitcast.81, pred[24,6]{1,0:T(8,128)(4,1)S(1)} %copy-done.9), kind=kOutput, calls=%fused_computation.19 | convolution fusion | flops 906559488 | bytes 12189840 | tf_op jit(solution)/shard_map/cikn,ikmn->cim/dot_general | solution.py:37
  109.8 1.1 pad_maximum_fusion.1
  111.0 4.1 %fusion.48 = f32[96,192]{1,0:T(8,128)S(1)} fusion(f32[192,3072]{1,0:T(8,128)} %all-gather.3.cloned.1.call-done, f32[32,3072]{1,0:T(8,128)S(1)} %copy-done.2, f32[32,3072]{1,0:T(8,128)S(1)} %copy-done, f32[32,3072]{1,0:T(8,128)S(1)} %get-tuple-element.26), kind=kOutput, calls=%fused_computation.106 | convolution fusion | flops 680067072 | bytes 3612672 | tf_op jit(solution)/shard_map/dot_general | solution.py:26
  115.1 14.5 %all-gather.5.cloned.1.call-done = f32[192,3072]{1,0:T(8,128)} async-done(((f32[96,3072]{1,0:T(8,128)}), f32[192,3072]{1,0:T(8,128)}) %all-gather.5.cloned.1.call-update) | async-done | bytes 2359312 | tf_op jit(solution)/shard_map/all_gather | solution.py:100
  129.5 4.1 %fusion.47 = f32[96,192]{1,0:T(8,128)S(1)} fusion(f32[192,3072]{1,0:T(8,128)} %all-gather.5.cloned.1.call-done, f32[32,3072]{1,0:T(8,128)S(1)} %copy-done.2, f32[32,3072]{1,0:T(8,128)S(1)} %copy-done, f32[32,3072]{1,0:T(8,128)S(1)} %get-tuple-element.26), kind=kOutput, calls=%fused_computation.105 | convolution fusion | flops 680067072 | bytes 3612672 | tf_op jit(solution)/shard_map/dot_general | solution.py:26
  134.4 6.3 %all-to-all-start.1 = ((f32[16,12,192]{2,1,0:T(8,128)}), f32[16,12,192]{2,1,0:T(8,128)S(1)}, u32[]{:S(2)}, u32[]{:S(2)}) async-start(f32[16,12,192]{2,1,0:T(8,128)} %reshape.84), calls=%async_computation.1 | async-start | bytes 524288 | tf_op jit(solution)/shard_map/all_to_all | solution.py:50
  140.7 7.7 %all-to-all-done.1 = f32[16,12,192]{2,1,0:T(8,128)S(1)} async-done(((f32[16,12,192]{2,1,0:T(8,128)}), f32[16,12,192]{2,1,0:T(8,128)S(1)}, u32[]{:S(2)}, u32[]{:S(2)}) %all-to-all-start.1) | async-done | bytes 147488 | tf_op jit(solution)/shard_map/all_to_all | solution.py:50
  149.1 6.7 %all-to-all-start.2 = ((f32[8,12,192]{2,1,0:T(8,128)}), f32[8,12,192]{2,1,0:T(8,128)S(1)}, u32[]{:S(2)}, u32[]{:S(2)}) async-start(f32[8,12,192]{2,1,0:T(8,128)} %broadcast_in_dim.68), calls=%async_computation.2 | async-start | bytes 262144 | tf_op jit(solution)/shard_map/all_to_all | solution.py:50
  155.9 8.0 %all-to-all-done.2 = f32[8,12,192]{2,1,0:T(8,128)S(1)} async-done(((f32[8,12,192]{2,1,0:T(8,128)}), f32[8,12,192]{2,1,0:T(8,128)S(1)}, u32[]{:S(2)}, u32[]{:S(2)}) %all-to-all-start.2) | async-done | bytes 73760 | tf_op jit(solution)/shard_map/all_to_all | solution.py:50
  164.6 3.7 %all-to-all-start.3 = ((f32[16,12,192]{2,1,0:T(8,128)}), f32[16,12,192]{2,1,0:T(8,128)S(1)}, u32[]{:S(2)}, u32[]{:S(2)}) async-start(f32[16,12,192]{2,1,0:T(8,128)} %broadcast_in_dim.69), calls=%async_computation.3 | async-start | bytes 524288 | tf_op jit(solution)/shard_map/all_to_all | solution.py:50
  168.5 7.1 %all-to-all-done.3 = f32[16,12,192]{2,1,0:T(8,128)S(1)} async-done(((f32[16,12,192]{2,1,0:T(8,128)}), f32[16,12,192]{2,1,0:T(8,128)S(1)}, u32[]{:S(2)}, u32[]{:S(2)}) %all-to-all-start.3) | async-done | bytes 147488 | tf_op jit(solution)/shard_map/all_to_all | solution.py:50
  175.6 6.0 %all_gather.14 = f32[192,192]{1,0:T(8,128)S(1)} all-gather(f32[96,192]{1,0:T(8,128)S(1)} %slice.92), channel_id=1, replica_groups=mesh['rows'=128,'cols'=2] {'cols'}, dimensions={0}, use_global_device_ids=true | all-gather | bytes 221184 | tf_op jit(solution)/shard_map/all_gather | solution.py:108
  183.6 11.7 %cholesky.51 = f32[128,128]{1,0:T(8,128)S(1)} custom-call(f32[128,128]{1,0:T(8,128)S(1)} %cholesky.124), custom_call_target="Cholesky" | custom-call | tf_op jit(solution)/shard_map/jit(cholesky)/cholesky | solution.py:116
  195.4 9.8 %custom-call.15 = f32[1,128,128]{1,2,0:T(8,128)S(1)} custom-call(f32[1,128,128]{2,1,0:T(8,128)S(1)} %get-tuple-element.36), custom_call_target="InvertDiagBlocksLowerTriangular" | custom-call | tf_op jit(solution)/shard_map/jit(cholesky)/cholesky | solution.py:116
  205.6 5.8 %cholesky.110 = f32[64,64]{1,0:T(8,128)S(1)} custom-call(f32[64,64]{1,0:T(8,128)S(1)} %convolution_subtract_fusion.1), custom_call_target="Cholesky" | custom-call | tf_op jit(solution)/shard_map/jit(cholesky)/cholesky | solution.py:116
  214.2 19.7 %custom-call.16 = f32[2,128,128]{1,2,0:T(8,128)S(1)} custom-call(f32[2,128,128]{2,1,0:T(8,128)S(1)} %pad_maximum_fusion.4), custom_call_target="InvertDiagBlocksLowerTriangular" | custom-call | tf_op jit(solution)/shard_map/jit(_solve_triangular)/triangular_solve | solution.py:117
  234.9 2.2 all_gather.15
  239.9 1.0 fusion.30
  242.2 1.6 convolution_multiply_fusion
  243.8 0.9 fusion.49
  (100 shorter events, 14.1 us)
Async XLA Ops:
  7.2 4.3 %copy-start = (f32[32,3072]{1,0:T(8,128)S(1)}, f32[32,3072]{1,0:T(8,128)}, u32[]{:S(2)}) copy-start(f32[32,3072]{1,0:T(8,128)} %param.12) | copy-start | bytes 1179652
  7.2 4.4 %copy-start.2 = (f32[32,3072]{1,0:T(8,128)S(1)}, f32[32,3072]{1,0:T(8,128)}, u32[]{:S(2)}) copy-start(f32[32,3072]{1,0:T(8,128)} %param.13) | copy-start | bytes 1179652
  7.2 103.8 %all-gather.3.cloned.1.call-start = ((), (), s32[]{:S(2)}) async-start(), calls=%async_computation.4 | async-start | bytes 3538944 | tf_op jit(solution)/shard_map/all_gather | solution.py:99
  11.5 11.4 %copy-start.10 = (s32[24,6]{0,1:T(8,128)S(1)}, s32[24,6]{0,1:T(8,128)}, u32[]{:S(2)}) copy-start(s32[24,6]{0,1:T(8,128)} %param.15) | copy-start | bytes 1732
  11.6 28.5 %copy-start.3 = (f32[64,3072]{1,0:T(8,128)}, f32[64,3072]{1,0:T(8,128)S(1)}, u32[]{:S(2)}) copy-start(f32[64,3072]{1,0:T(8,128)S(1)} %constant_dynamic-update-slice_fusion) | copy-start | bytes 2359300
  11.7 28.4 %copy-start.5 = (f32[64,3072]{1,0:T(8,128)}, f32[64,3072]{1,0:T(8,128)S(1)}, u32[]{:S(2)}) copy-start(f32[64,3072]{1,0:T(8,128)S(1)} %broadcast_multiply_fusion) | copy-start | bytes 2359300
  11.7 28.4 %collective-permute-start = (f32[64,3072]{1,0:T(8,128)S(1)}, f32[64,3072]{1,0:T(8,128)S(1)}, u32[]{:S(2)}, u32[]{:S(2)}) collective-permute-start(f32[64,3072]{1,0:T(8,128)S(1)} %broadcast_multiply_fusion), channel_id=1, source_target_pairs={{0,2},{2,4},{4,6},{6,8},{8,10},{10,12},{12,14},{14,16},{16,18},{18... | collective-permute-start | bytes 2359304 | tf_op jit(solution)/shard_map/ppermute | solution.py:19
  13.9 27.1 %collective-permute-start.1 = (f32[64,3072]{1,0:T(8,128)S(1)}, f32[64,3072]{1,0:T(8,128)}, u32[]{:S(2)}, u32[]{:S(2)}) collective-permute-start(f32[64,3072]{1,0:T(8,128)S(1)} %broadcast_multiply_fusion), channel_id=1, source_target_pairs={{2,0},{4,2},{6,4},{8,6},{10,8},{12,10},{14,12},{16,14},{18,16},{20... | collective-permute-start | bytes 2359304 | tf_op jit(solution)/shard_map/ppermute | solution.py:20
  23.2 22.7 %copy-start.8 = (pred[24,6]{1,0:T(8,128)(4,1)}, pred[24,6]{1,0:T(8,128)(4,1)S(1)}, u32[]{:S(2)}) copy-start(pred[24,6]{1,0:T(8,128)(4,1)S(1)} %copy.66) | copy-start | bytes 436
  40.1 0.9 copy-start.6
  45.9 13.5 %copy-start.4 = (f32[64,3072]{1,0:T(8,128)S(1)}, f32[64,3072]{1,0:T(8,128)}, u32[]{:S(2)}) copy-start(f32[64,3072]{1,0:T(8,128)} %copy-done.3) | copy-start | bytes 2359300
  82.0 47.5 %all-gather.5.cloned.1.call-start = ((), (), s32[]{:S(2)}) async-start(), calls=%async_computation.5 | async-start | bytes 3538944 | tf_op jit(solution)/shard_map/all_gather | solution.py:100
  82.1 12.8 %collective-permute-start.2 = (f32[32,3072]{1,0:T(8,128)S(1)}, f32[32,3072]{1,0:T(8,128)S(1)}, u32[]{:S(2)}, u32[]{:S(2)}) collective-permute-start(f32[32,3072]{1,0:T(8,128)S(1)} %get-tuple-element.25), channel_id=1, source_target_pairs={{0,2},{2,4},{4,6},{6,8},{8,10},{10,12},{12,14},{14,16},{16,18},{18... | collective-permute-start | bytes 1179656 | tf_op jit(solution)/shard_map/ppermute | solution.py:19
  82.5 12.5 %collective-permute-start.3 = (f32[32,3072]{1,0:T(8,128)S(1)}, f32[32,3072]{1,0:T(8,128)S(1)}, u32[]{:S(2)}, u32[]{:S(2)}) collective-permute-start(f32[32,3072]{1,0:T(8,128)S(1)} %get-tuple-element.25), channel_id=1, source_target_pairs={{2,0},{4,2},{6,4},{8,6},{10,8},{12,10},{14,12},{16,14},{18,16},{20... | collective-permute-start | bytes 1179656 | tf_op jit(solution)/shard_map/ppermute | solution.py:20
  95.1 2.3 copy-start.9
  115.1 25.6 %copy-start.7 = (f32[192,64]{0,1:T(8,128)S(1)}, f32[192,64]{0,1:T(8,128)}, u32[]{:S(2)}) copy-start(f32[192,64]{0,1:T(8,128)} %param.16) | copy-start | bytes 147460
  115.1 40.7 %copy-start.12 = (s32[192]{0:T(256)S(1)}, s32[192]{0:T(256)}, u32[]{:S(2)}) copy-start(s32[192]{0:T(256)} %constant.199) | copy-start | bytes 2308
  133.6 34.6 %copy-start.11 = (s32[192]{0:T(256)S(1)}, s32[192]{0:T(256)}, u32[]{:S(2)}) copy-start(s32[192]{0:T(256)} %constant.201) | copy-start | bytes 2308
  134.4 14.0 %all-to-all-start.1 = ((f32[16,12,192]{2,1,0:T(8,128)}), f32[16,12,192]{2,1,0:T(8,128)S(1)}, u32[]{:S(2)}, u32[]{:S(2)}) async-start(f32[16,12,192]{2,1,0:T(8,128)} %reshape.84), calls=%async_computation.1 | async-start | bytes 524288 | tf_op jit(solution)/shard_map/all_to_all | solution.py:50
  149.1 14.8 %all-to-all-start.2 = ((f32[8,12,192]{2,1,0:T(8,128)}), f32[8,12,192]{2,1,0:T(8,128)S(1)}, u32[]{:S(2)}, u32[]{:S(2)}) async-start(f32[8,12,192]{2,1,0:T(8,128)} %broadcast_in_dim.68), calls=%async_computation.2 | async-start | bytes 262144 | tf_op jit(solution)/shard_map/all_to_all | solution.py:50
  164.6 11.0 %all-to-all-start.3 = ((f32[16,12,192]{2,1,0:T(8,128)}), f32[16,12,192]{2,1,0:T(8,128)S(1)}, u32[]{:S(2)}, u32[]{:S(2)}) async-start(f32[16,12,192]{2,1,0:T(8,128)} %broadcast_in_dim.69), calls=%async_computation.3 | async-start | bytes 524288 | tf_op jit(solution)/shard_map/all_to_all | solution.py:50
  238.1 4.1 %copy-start.1 = (f32[192,3072]{1,0:T(8,128)S(1)}, f32[192,3072]{1,0:T(8,128)}, u32[]{:S(2)}) copy-start(f32[192,3072]{1,0:T(8,128)} %all-gather.3.cloned.1.call-done) | copy-start | bytes 7077892
Sparse Core Ops, SparseCore 0:
  82.2 12.3 all-gather.2
  111.1 18.4 all-gather.4

commit v2 on v1

v2 whole, which is shorter than its diff:
```python
import functools
import math

import jax
import jax.numpy as jnp
from jax import lax
from jax.experimental import pallas as pl
from jax.experimental.pallas import tpu as pltpu
from jax.sharding import PartitionSpec as P

BLK = 128
F32 = jnp.float32
BF16 = jnp.bfloat16
ROWS_PER_STEP = 4
VMEM_LIMIT = 60 * 2**20
PIVOTS = 16
EXACT = lax.Precision.HIGHEST


def halves(v):
    high = v.astype(BF16)
    return high, (v - high.astype(F32)).astype(BF16)


def ring(devices, step):
    return [(i, (i + step) % devices) for i in range(devices)]


def plane_groups():
    return [[z * 16 + i for i in range(16)] for z in range(8)]


def column_groups():
    return [[z * 16 + i for z in range(8)] for i in range(16)]


def exchange(x, groups):
    return lax.all_to_all(x, "rows", 0, 0, axis_index_groups=groups)


def repeated(x, count):
    return jnp.broadcast_to(x[None], (count,) + x.shape)


def sum_large(x):
    plane, column = plane_groups(), column_groups()
    part = jnp.sum(exchange(x, plane), axis=0)
    part = jnp.sum(exchange(repeated(part, 8), column), axis=0)
    return exchange(repeated(part, 16), plane)


def prepare_kernel(a_ref, split_ref, scale_ref):
    step = pl.program_id(0)
    for r in range(ROWS_PER_STEP):
        total = a_ref[r, 0]
        for k in range(6):
            a = a_ref[r, k]
            if k:
                total = total + a
            high, low = halves(a)
            split_ref[r, 0:BLK, k * BLK : (k + 1) * BLK] = high
            split_ref[r, BLK : 2 * BLK, k * BLK : (k + 1) * BLK] = low
        degree = jnp.sum(total.T, axis=0, keepdims=True)
        scale_ref[pl.ds(step * ROWS_PER_STEP + r, 1), :] = lax.rsqrt(degree)


def prepare(affinity):
    n = affinity.shape[0]
    return pl.pallas_call(
        prepare_kernel,
        grid=(n // ROWS_PER_STEP,),
        in_specs=[pl.BlockSpec((ROWS_PER_STEP, 6, BLK, BLK), lambda i: (i, 0, 0, 0))],
        out_specs=[
            pl.BlockSpec((ROWS_PER_STEP, 2 * BLK, 6 * BLK), lambda i: (i, 0, 0)),
            pl.BlockSpec((n, BLK), lambda i: (0, 0)),
        ],
        out_shape=[
            jax.ShapeDtypeStruct((n, 2 * BLK, 6 * BLK), BF16),
            jax.ShapeDtypeStruct((n, BLK), F32),
        ],
        compiler_params=pltpu.CompilerParams(vmem_limit_bytes=VMEM_LIMIT),
        cost_estimate=pl.CostEstimate(flops=10**7, bytes_accessed=19 * 10**6, transcendentals=3072),
        name="prepare",
    )(affinity)


def block_of(ref, i):
    return ref[:, pl.ds(pl.multiple_of(i * BLK, BLK), BLK)]


def local_place(index, first, total):
    place = index - first
    place = jnp.where(place < 0, place + total, place)
    return jnp.where(place >= total, place - total, place)


def gathered(info, pat, turned, i):
    places = [local_place(pat[i, k], info[1], info[2]) for k in range(6)]
    return jnp.concatenate([turned[place] for place in places], axis=0)


def first_kernel(info, pat, a_ref, x_ref, xb_ref, xa_ref, s_ref, sb_ref, sa_ref, y_ref, sums_ref, turned, acc):
    step = pl.program_id(0)
    count = s_ref.shape[0]

    @pl.when(step == 0)
    def _():
        acc[...] = jnp.zeros_like(acc)
        for part, (v_ref, t_ref) in enumerate(((xb_ref, sb_ref), (x_ref, s_ref), (xa_ref, sa_ref))):

            @pl.loop(0, count)
            def _(j):
                v = block_of(v_ref, j) * t_ref[pl.ds(j, 1), :]
                high = v.astype(BF16).astype(F32)
                stack = jnp.concatenate([high, v - high, jnp.zeros((64, BLK), F32)], axis=0)
                turned[part * count + j] = stack.T.astype(BF16)

    for r in range(ROWS_PER_STEP):
        i = step * ROWS_PER_STEP + r
        weights = gathered(info, pat, turned, i)
        product = jnp.dot(a_ref[r], weights, preferred_element_type=F32)
        image = (product[:BLK] + product[BLK:]).T
        x = block_of(x_ref, i)
        y = x - s_ref[pl.ds(i, 1), :] * (image[0:32] + image[32:64])
        y_ref[:, pl.ds(pl.multiple_of(i * BLK, BLK), BLK)] = y
        acc[0:32, :] += x * y
        acc[32:64, :] += x * x

    @pl.when(step == pl.num_programs(0) - 1)
    def _():
        stack = jnp.concatenate([acc[...], jnp.zeros((64, BLK), F32)], axis=0)
        sums_ref[...] = jnp.sum(stack.T, axis=0, keepdims=True)


def whole(shape):
    return pl.BlockSpec(shape, lambda i, *_: (0,) * len(shape))


def first_image(info, pattern, split, x, xb, xa, s, sb, sa):
    n = s.shape[0]
    return pl.pallas_call(
        first_kernel,
        grid_spec=pltpu.PrefetchScalarGridSpec(
            num_scalar_prefetch=2,
            grid=(n // ROWS_PER_STEP,),
            in_specs=[pl.BlockSpec((ROWS_PER_STEP, 2 * BLK, 6 * BLK), lambda i, *_: (i, 0, 0))]
            + [whole(x.shape)] * 3
            + [whole(s.shape)] * 3,
            out_specs=[whole(x.shape), whole((1, BLK))],
            scratch_shapes=[pltpu.VMEM((3 * n, BLK, BLK), BF16), pltpu.VMEM((64, BLK), F32)],
        ),
        out_shape=[jax.ShapeDtypeStruct(x.shape, F32), jax.ShapeDtypeStruct((1, BLK), F32)],
        compiler_params=pltpu.CompilerParams(vmem_limit_bytes=VMEM_LIMIT),
        cost_estimate=pl.CostEstimate(flops=4 * 10**9, bytes_accessed=11 * 10**6, transcendentals=0),
        name="first_image",
    )(info, pattern, split, x, xb, xa, s, sb, sa)


def second_kernel(
    info, pat, a_ref, sums_ref, y_ref, yb_ref, ya_ref, p_ref, pb_ref, pa_ref, s_ref, sb_ref, sa_ref,
    x_ref, xo_ref, yo_ref, po_ref, high_ref, low_ref, out_ref, turned, quotients, left_high, left_low, acc,
):
    step = pl.program_id(0)
    count = s_ref.shape[0]
    core = info[0]
    own = pl.multiple_of(core * 32, 32)
    other = pl.multiple_of((1 - core) * 32, 32)

    @pl.when(step == 0)
    def _():
        acc[...] = jnp.zeros_like(acc)
        sums = jnp.sum(sums_ref[...], axis=0, keepdims=True)
        column = jnp.broadcast_to(sums, (BLK, BLK)).T
        quotients[0:32] = column[0:32] / column[32:64]
        quotients[32:64] = column[64:96] / column[96:128]
        triples = ((yb_ref, pb_ref, sb_ref), (y_ref, p_ref, s_ref), (ya_ref, pa_ref, sa_ref))
        for part, (v_ref, w_ref, t_ref) in enumerate(triples):

            @pl.loop(0, count)
            def _(j):
                t = t_ref[pl.ds(j, 1), :]
                v = block_of(v_ref, j) * t
                w = block_of(w_ref, j) * t
                v_high = v.astype(BF16).astype(F32)
                w_high = w.astype(BF16).astype(F32)
                stack = jnp.concatenate([v_high, v - v_high, w_high, w - w_high], axis=0)
                turned[part * count + j] = stack.T.astype(BF16)

    q_own = quotients[pl.ds(own, 32), :]
    q_other = quotients[pl.ds(other, 32), :]
    for r in range(ROWS_PER_STEP):
        i = step * ROWS_PER_STEP + r
        lanes = slice(r * BLK, (r + 1) * BLK)
        weights = gathered(info, pat, turned, i)
        product = jnp.dot(a_ref[r], weights, preferred_element_type=F32)
        image = (product[:BLK] + product[BLK:]).T
        s = s_ref[pl.ds(i, 1), :]
        x, y, p = block_of(x_ref, i), block_of(y_ref, i), block_of(p_ref, i)
        z = y - s * (image[0:32] + image[32:64])
        p_image = p - s * (image[64:96] + image[96:128])
        residual = y - q_own * x
        for at, v in enumerate((residual, x, p, z - q_own * y, y, p_image)):
            high, low = halves(v)
            left_high[32 * at : 32 * at + 32, lanes] = high
            left_low[32 * at : 32 * at + 32, lanes] = low
            if at < 3:
                high_ref[pl.ds(64 * at + own, 32), lanes] = high
                low_ref[pl.ds(64 * at + own, 32), lanes] = low
        xo = block_of(xo_ref, i)
        for at, v in enumerate((block_of(yo_ref, i) - q_other * xo, xo, block_of(po_ref, i))):
            high, low = halves(v)
            high_ref[pl.ds(64 * at + other, 32), lanes] = high
            low_ref[pl.ds(64 * at + other, 32), lanes] = low

    left = jnp.concatenate([left_high[...], left_low[...]], axis=0)
    dims = (((1,), (1,)), ((), ()))
    acc[...] += lax.dot_general(left, high_ref[...], dims, preferred_element_type=F32) + lax.dot_general(
        left, low_ref[...], dims, preferred_element_type=F32
    )

    @pl.when(step == pl.num_programs(0) - 1)
    def _():
        total = acc[0:192] + acc[192:384]
        out_ref[0:192, :] = total[:, 0:BLK]
        out_ref[192:384, :] = jnp.concatenate([total[:, BLK:192], jnp.zeros((192, 64), F32)], axis=1)


def second_image(info, pattern, split, sums, y, yb, ya, p, pb, pa, s, sb, sa, x, xo, yo, po):
    n = s.shape[0]
    chunk = ROWS_PER_STEP * BLK
    return pl.pallas_call(
        second_kernel,
        grid_spec=pltpu.PrefetchScalarGridSpec(
            num_scalar_prefetch=2,
            grid=(n // ROWS_PER_STEP,),
            in_specs=[pl.BlockSpec((ROWS_PER_STEP, 2 * BLK, 6 * BLK), lambda i, *_: (i, 0, 0)), whole(sums.shape)]
            + [whole(x.shape)] * 6
            + [whole(s.shape)] * 3
            + [whole(x.shape)] * 4,
            out_specs=[pl.BlockSpec((192, chunk), lambda i, *_: (0, i))] * 2 + [whole((384, BLK))],
            scratch_shapes=[
                pltpu.VMEM((3 * n, BLK, BLK), BF16),
                pltpu.VMEM((64, BLK), F32),
                pltpu.VMEM((192, chunk), BF16),
                pltpu.VMEM((192, chunk), BF16),
                pltpu.VMEM((384, 192), F32),
            ],
        ),
        out_shape=[jax.ShapeDtypeStruct((192, x.shape[1]), BF16)] * 2 + [jax.ShapeDtypeStruct((384, BLK), F32)],
        compiler_params=pltpu.CompilerParams(vmem_limit_bytes=VMEM_LIMIT),
        cost_estimate=pl.CostEstimate(flops=8 * 10**9, bytes_accessed=18 * 10**6, transcendentals=0),
        name="second_image",
    )(info, pattern, split, sums, y, yb, ya, p, pb, pa, s, sb, sa, x, xo, yo, po)


def picked_row(groups, at):
    return jnp.broadcast_to(groups[at // 8][at % 8 : at % 8 + 1, :], (8, BLK))


def inverse_factor(block):
    lane = lax.broadcasted_iota(jnp.int32, (8, BLK), 1)
    sub = lax.broadcasted_iota(jnp.int32, (8, BLK), 0)
    a = []
    for g in range(4):
        unit = jnp.where(lane - 32 == sub + 8 * g, 1.0, 0.0)
        a.append(jnp.where(lane < 32, block[8 * g : 8 * g + 8, :], unit))
    for start in range(0, 32, PIVOTS):
        columns = [
            [jnp.broadcast_to(a[g][:, start + k : start + k + 1], (8, BLK)) if g >= start // 8 else None for g in range(4)]
            for k in range(PIVOTS)
        ]
        for k in range(PIVOTS):
            at = start + k
            own = at // 8
            pivot = 1.0 / picked_row(columns[k], at)
            factor = [columns[k][g] * pivot if g >= own else None for g in range(4)]
            factor[own] = jnp.where(sub > at % 8, factor[own], 0.0)
            for other in columns[k + 1 :]:
                e = picked_row(other, at)
                for g in range(own, 4):
                    other[g] = other[g] - factor[g] * e
            row = picked_row(a, at)
            for g in range(own, 4):
                a[g] = a[g] - factor[g] * row
    scaled = []
    for g in range(4):
        diagonal = jnp.sum(jnp.where(lane == sub + 8 * g, a[g], 0.0), axis=1, keepdims=True)
        scaled.append(a[g] * lax.rsqrt(diagonal))
    return jnp.concatenate(scaled, axis=0)[:, 32:64]


def exact(left, right, dims):
    return lax.dot_general(left, right, (dims, ((), ())), precision=EXACT, preferred_element_type=F32)


def inverse_cholesky(work, inverse):
    lane = lax.broadcasted_iota(jnp.int32, (32, 192), 1)
    sub = lax.broadcasted_iota(jnp.int32, (32, 192), 0)
    for at in range(0, 192, 32):
        rows = work[at : at + 32, :]
        if at < BLK:
            piece = rows[:, 0:BLK]
        else:
            piece = jnp.concatenate([rows[:, BLK:192], jnp.zeros((32, 64), F32)], axis=1)
        if at % BLK:
            piece = pltpu.roll(piece, BLK - at % BLK, 1)
        small = inverse_factor(piece)
        unit = jnp.where(lane - at == sub, 1.0, 0.0)
        rows = jnp.where((lane >= at) & (lane < at + 32), unit, rows)
        new = exact(small, rows, ((1,), (0,)))
        inverse[at : at + 32, :] = jnp.where(lane < at + 32, new, 0.0)
        if at < 160:
            update = exact(new, new, ((0,), (0,)))
            wide = lax.broadcasted_iota(jnp.int32, (160 - at, 192), 1)
            old = jnp.where((wide >= at) & (wide < at + 32), 0.0, work[at + 32 : 192, :])
            work[at + 32 : 192, :] = old - update[at + 32 : 192, :]


def final_kernel(
    info, mine_ref, theirs_ref, chosen_ref, high_ref, low_ref, vectors_ref, directions_ref, ritz_ref, work, raw, inverse, *, factor
):
    first = info[0] == 0
    for at in range(6):
        low_row = 32 * (at // 2)
        own = (at % 2 == 0) == first
        for base, target in ((0, work), (96, raw)):
            rows = slice(base + low_row, base + low_row + 32)
            lower_rows = slice(192 + base + low_row, 192 + base + low_row + 32)
            target[32 * at : 32 * at + 32, 0:BLK] = jnp.where(own, mine_ref[rows, :], theirs_ref[rows, :])
            tail = jnp.where(own, mine_ref[lower_rows, :], theirs_ref[lower_rows, :])
            target[32 * at : 32 * at + 32, BLK:192] = tail[:, 0:64]
    inverse_cholesky(work, inverse)
    whole_inverse = inverse[...]
    half = exact(whole_inverse, raw[...], ((1,), (1,)))
    ritz_ref[...] = exact(half, whole_inverse, ((1,), (1,)))
    mix = factor * exact(chosen_ref[...], whole_inverse, ((1,), (0,)))
    left = jnp.concatenate(halves(mix), axis=0)
    for at in range(0, high_ref.shape[1], 512):
        lanes = slice(at, at + 512)
        product = jnp.dot(left, high_ref[:, lanes], preferred_element_type=F32)
        product = product + jnp.dot(left, low_ref[:, lanes], preferred_element_type=F32)
        product = product[0:64] + product[64:128]
        vectors_ref[:, lanes] = product[0:32]
        directions_ref[:, lanes] = product[32:64]


def final(info, mine, theirs, chosen, high, low, factor):
    return pl.pallas_call(
        functools.partial(final_kernel, factor=factor),
        in_specs=[pl.BlockSpec(memory_space=pltpu.SMEM)] + [pl.BlockSpec(memory_space=pltpu.VMEM)] * 5,
        out_shape=[jax.ShapeDtypeStruct((32, high.shape[1]), F32)] * 2 + [jax.ShapeDtypeStruct((192, 192), F32)],
        scratch_shapes=[pltpu.VMEM((192, 192), F32)] * 3,
        compiler_params=pltpu.CompilerParams(vmem_limit_bytes=VMEM_LIMIT),
        cost_estimate=pl.CostEstimate(flops=4 * 10**8, bytes_accessed=4 * 10**6, transcendentals=0),
        name="final",
    )(info, mine, theirs, chosen, high, low)


def other_core(x):
    return lax.ppermute(x, "cols", [(0, 1), (1, 0)])


def local(vectors, directions, affinity, pattern, rotation):
    width, rows_dev = vectors.shape
    devices = lax.axis_size("rows")
    core = lax.axis_index("cols")
    total = 2 * width
    nodes = rows_dev * devices
    local_blocks = affinity.shape[0]
    all_blocks = local_blocks * devices
    first_block = (lax.axis_index("rows") - 1) * local_blocks
    info = jnp.stack([core, first_block, jnp.int32(all_blocks)]).astype(jnp.int32)
    up, down = ring(devices, 1), ring(devices, -1)

    x_before = lax.ppermute(vectors, "rows", up)
    x_after = lax.ppermute(vectors, "rows", down)
    split, scale = prepare(affinity)
    s_before = lax.ppermute(scale, "rows", up)
    s_after = lax.ppermute(scale, "rows", down)
    p_early, _ = lax.optimization_barrier((directions, scale))
    p_before = lax.ppermute(p_early, "rows", up)
    p_after = lax.ppermute(p_early, "rows", down)
    x_other = other_core(vectors)
    p_other = other_core(directions)
    y, sums = first_image(info, pattern, split, vectors, x_before, x_after, scale, s_before, s_after)
    y_before = lax.ppermute(y, "rows", up)
    y_after = lax.ppermute(y, "rows", down)
    y_other = other_core(y)
    half = sums[:, 0:64]
    blank = jnp.zeros_like(half)
    row = jnp.where(core == 0, jnp.concatenate([half, blank], axis=1), jnp.concatenate([blank, half], axis=1))
    all_sums = lax.all_to_all(repeated(row, 2 * devices), ("rows", "cols"), 0, 0).reshape(2 * devices, BLK)
    high, low, part = second_image(
        info, pattern, split, all_sums, y, y_before, y_after, directions, p_before, p_after,
        scale, s_before, s_after, vectors, x_other, y_other, p_other,
    )
    summed = sum_large(part.reshape(16, 24, BLK)).reshape(384, BLK)
    theirs = other_core(summed)
    mine = lambda m: lax.dynamic_slice_in_dim(m, core * width, width, 1)
    kept = jnp.concatenate([rotation[:total], jnp.zeros((total, total), F32), rotation[2 * total :]], axis=0)
    chosen = jnp.concatenate([mine(rotation), mine(kept)], axis=1).T
    new_vectors, new_directions, ritz_matrix = final(info, summed, theirs, chosen, high, low, math.sqrt(nodes))
    return new_vectors, new_directions, ritz_matrix


def solution(mesh):
    in_specs = (P("cols", "rows"), P("cols", "rows"), P("rows", None, None, None), P("rows", None), P())
    out_specs = (P("cols", "rows"), P("cols", "rows"), P())
    return jax.shard_map(local, mesh=mesh, in_specs=in_specs, out_specs=out_specs, check_vma=False)
```

time: 252 us -> 156 us (0.62)
  Pallas kernels: 0 us -> 57.1 us
  other arithmetic: 58.1 us -> 2.15 us
  matrix products: 39.2 us -> 0 us
  waiting for transfers between devices: 60 us -> 29 us
  blocking collectives: 28.9 us -> 10.4 us
  starting transfers between devices: 34.9 us -> 51 us
  between operations: 15.9 us -> 0.85 us
  local copies, waits for them, and re-layouts: 14.6 us -> 5.13 us
    pallas_call x0 -> x4, Pallas kernels: none -> 57.1 us  [the longest x1 19.2 us: second_image(): pl.pallas_call(second_kernel, grid_spec=pltpu.PrefetchScalarGridSpec(num_...]
    another operation x13 -> x1, other arithmetic: 48.5 us -> 0.66 us  [local(): jnp.stack([core, first_block, jnp.int32(all_blocks)]).astype(jnp.int32)]
    dot_general x9 -> x0, matrix products: 37.9 us -> none  [the longest x2 25.9 us: block_image(): jnp.einsum('cikn,ikmn->cim', picked, affinity, precision=lax.Precision.HI...]
    ppermute x4 -> x12, waiting for transfers between devices: 22.7 us -> 1.73 us  [the longest x1 1.28 us: local(): s_before = lax.ppermute(scale, 'rows', up)]
    ppermute x4 -> x12, starting transfers between devices: 18.2 us -> 37.8 us  [the longest x1 9.02 us: local(): x_after = lax.ppermute(vectors, 'rows', down)]
    all_gather x2 -> x0, waiting for transfers between devices: 14.5 us -> none  [the longest x1 14.5 us: local(): lax.all_gather(local_image, 'cols', axis=0, tiled=True)]
    all_to_all x0 -> x1, waiting for transfers between devices: none -> 12.9 us  [local(): lax.all_to_all(repeated(row, 2 * devices), ('rows', 'cols'), 0, 0)]
    all_to_all x1, blocking collectives: 20.7 us -> 10.4 us  [exchange(): return lax.all_to_all(x, 'rows', 0, 0, axis_index_groups=groups)]
  transfers between devices with their start and end apart: 9 -> 15, of which waited for: 6 -> 5; matrix products, arithmetic and copies ran while one was open for 8% -> 2% of each run, Pallas kernels for 0% -> 17%
where the time goes in v2:
time: 156 us
  Pallas kernels  57.1 us (37%)
  starting transfers between devices  51 us (33%)
  waiting for transfers between devices  29 us (19%)
  blocking collectives  10.4 us (7%)
  local copies, waits for them, and re-layouts  5.13 us (3%)
  other arithmetic  2.15 us (1%)
    pallas_call x1, Pallas kernels, second_image(): pl.pallas_call(second_kernel, grid_spec=pltpu.PrefetchScalarGridSpec(num_...  19.2 us
    pallas_call x1, Pallas kernels, first_image(): pl.pallas_call(first_kernel, grid_spec=pltpu.PrefetchScalarGridSpec(num_s...  16.7 us
    all_to_all x2, waiting for transfers between devices, exchange(): return lax.all_to_all(x, 'rows', 0, 0, axis_index_groups=groups)  14.4 us
    all_to_all x1, waiting for transfers between devices, local(): lax.all_to_all(repeated(row, 2 * devices), ('rows', 'cols'), 0, 0)  12.9 us
    pallas_call x1, Pallas kernels, final(): pl.pallas_call(functools.partial(final_kernel, factor=factor), in_specs=[...  12 us
    all_to_all x1, blocking collectives, exchange(): return lax.all_to_all(x, 'rows', 0, 0, axis_index_groups=groups)  10.4 us
    pallas_call x1, Pallas kernels, prepare(): pl.pallas_call(prepare_kernel, grid=(n // ROWS_PER_STEP,), in_specs=[pl.B...  9.18 us
    ppermute x1, starting transfers between devices, local(): x_after = lax.ppermute(vectors, 'rows', down)  9.02 us
  transfers between devices with their start and end apart: 15, of which 5 were waited for; matrix products, arithmetic and copies ran while one was open for 2% of the time, Pallas kernels for 17%

profile of v2, /device:TPU:1, one launch (start us, length us, event | category | flops | bytes accessed | tf_op | source)
XLA Modules:
  0.0 155.6 jit_solution(7131758726586915681)
XLA Ops:
  0.7 2.2 %collective-permute-start = (f32[32,3072]{1,0:T(8,128)}, f32[32,3072]{1,0:T(8,128)S(1)}, u32[]{:S(2)}, u32[]{:S(2)}) collective-permute-start(f32[32,3072]{1,0:T(8,128)} %x_ref.3), channel_id=1, source_target_pairs={{0,2},{2,4},{4,6},{6,8},{8,10},{10,12},{12,14},{14,16},{16,18},{18... | collective-permute-start | bytes 1179656 | tf_op jit(solution)/shard_map/ppermute | solution.py:375
  2.9 9.0 %collective-permute-start.1 = (f32[32,3072]{1,0:T(8,128)}, f32[32,3072]{1,0:T(8,128)S(1)}, u32[]{:S(2)}, u32[]{:S(2)}) collective-permute-start(f32[32,3072]{1,0:T(8,128)} %x_ref.3), channel_id=1, source_target_pairs={{0,254},{2,0},{4,2},{6,4},{8,6},{10,8},{12,10},{14,12},{16,14},{18... | collective-permute-start | bytes 1179656 | tf_op jit(solution)/shard_map/ppermute | solution.py:376
  11.9 9.2 %prepare.1 = (bf16[24,256,768]{2,1,0:T(8,128)(2,1)}, f32[24,128]{1,0:T(8,128)}) custom-call(f32[24,6,128,128]{3,2,1,0:T(8,128)} %a_ref.1), custom_call_target="tpu_custom_call" | custom-call | flops 10000000 | bytes 19000000 | tf_op jit(solution)/shard_map/prepare/pallas_call | solution.py:69
  21.1 6.9 %collective-permute-start.3 = (f32[24,128]{1,0:T(8,128)}, f32[24,128]{1,0:T(8,128)S(1)}, u32[]{:S(2)}, u32[]{:S(2)}) collective-permute-start(f32[24,128]{1,0:T(8,128)} %get-tuple-element.12.s_ref), channel_id=1, source_target_pairs={{0,254},{2,0},{4,2},{6,4},{8,6},{10,8},{12,10},{14,12},{16,14},{18... | collective-permute-start | bytes 36872 | tf_op jit(solution)/shard_map/ppermute | solution.py:379
  28.0 1.3 collective-permute-done.2.sb_ref
  29.3 5.6 %collective-permute-start.7 = (f32[32,3072]{1,0:T(8,128)S(1)}, f32[32,3072]{1,0:T(8,128)S(1)}, u32[]{:S(2)}, u32[]{:S(2)}) collective-permute-start(f32[32,3072]{1,0:T(8,128)S(1)} %copy-done.7), channel_id=1, source_target_pairs={{0,254},{2,0},{4,2},{6,4},{8,6},{10,8},{12,10},{14,12},{16,14},{18... | collective-permute-start | bytes 1179656 | tf_op jit(solution)/shard_map/ppermute | solution.py:382
  34.9 0.7 pad_add_fusion.info
  35.5 0.7 copy.13.pat
  36.2 2.1 %collective-permute-start.10 = (f32[32,3072]{1,0:T(8,128)S(1)}, f32[32,3072]{1,0:T(8,128)S(1)}, u32[]{:S(2)}, u32[]{:S(2)}) collective-permute-start(f32[32,3072]{1,0:T(8,128)S(1)} %copy-done.7), channel_id=1, source_target_pairs={{0,1},{1,0},{2,3},{3,2},{4,5},{5,4},{6,7},{7,6},{8,9},{9,8},{10,11... | collective-permute-start | bytes 1179656 | tf_op jit(solution)/shard_map/ppermute | solution.py:360
  38.4 0.6 copy-done.12
  39.0 0.1 copy-done.13
  39.2 16.7 %first_image.1 = (f32[32,3072]{1,0:T(8,128)}, f32[1,128]{1,0:T(1,128)}) custom-call(s32[3]{0:T(128)} %pad_add_fusion.info, s32[24,6]{1,0:T(8,128)} %copy.13.pat, bf16[24,256,768]{2,1,0:T(8,128)(2,1)} %get-tuple-element.11.a_ref, f32[32,3072]{1,0:T(8,128)} %x_ref.3, f32[32,3072]{1,0:T(8,128)} %copy-done.12, f32[32,3072]{1,0:T(8,128)} %copy-done.13, ...), custom_call_target="tpu_custom_call" | custom-call | flops 4000000000 | bytes 11000000 | tf_op jit(solution)/shard_map/first_image/pallas_call | solution.py:141
  55.9 6.9 %collective-permute-start.5 = (f32[32,3072]{1,0:T(8,128)}, f32[32,3072]{1,0:T(8,128)S(1)}, u32[]{:S(2)}, u32[]{:S(2)}) collective-permute-start(f32[32,3072]{1,0:T(8,128)} %get-tuple-element.14.y_ref), channel_id=1, source_target_pairs={{0,254},{2,0},{4,2},{6,4},{8,6},{10,8},{12,10},{14,12},{16,14},{18... | collective-permute-start | bytes 1179656 | tf_op jit(solution)/shard_map/ppermute | solution.py:387
  62.8 1.0 collective-permute-start.9
  63.8 0.8 fusion.2
  64.6 0.7 broadcast_in_dim.11
  65.3 6.0 %all-to-all-start = ((f32[256,1,128]{2,1,0:T(1,128)}), f32[256,1,128]{2,1,0:T(1,128)S(1)}, u32[]{:S(2)}, u32[]{:S(2)}) async-start(f32[256,1,128]{2,1,0:T(1,128)} %broadcast_in_dim.11), calls=%async_computation | async-start | bytes 262144 | tf_op jit(solution)/shard_map/all_to_all | solution.py:392
  71.4 12.9 %all-to-all-done = f32[256,1,128]{2,1,0:T(1,128)S(1)} async-done(((f32[256,1,128]{2,1,0:T(1,128)}), f32[256,1,128]{2,1,0:T(1,128)S(1)}, u32[]{:S(2)}, u32[]{:S(2)}) %all-to-all-start) | async-done | bytes 131104 | tf_op jit(solution)/shard_map/all_to_all | solution.py:392
  84.4 0.6 copy-done.3
  85.2 19.2 %second_image.1 = (bf16[192,3072]{1,0:T(8,128)(2,1)}, bf16[192,3072]{1,0:T(8,128)(2,1)}, f32[384,128]{1,0:T(8,128)}) custom-call(s32[3]{0:T(128)} %pad_add_fusion.info, s32[24,6]{1,0:T(8,128)} %copy.13.pat, bf16[24,256,768]{2,1,0:T(8,128)(2,1)} %get-tuple-element.11.a_ref, f32[256,128]{1,0:T(8,128)} %bitcast.13, f32[32,3072]{1,0:T(8,128)} %get-tuple-element.14.y_ref, ...), custom_call_target="tpu_custom_call" | custom-call | flops 8000000000 | bytes 18000000 | tf_op jit(solution)/shard_map/second_image/pallas_call | solution.py:231
  104.5 10.4 %all_to_all.20 = f32[16,24,128]{2,1,0:T(8,128)S(1)} all-to-all(f32[16,24,128]{2,1,0:T(8,128)} %bitcast.12), channel_id=1, replica_groups={{0,2,4,6,8,10,12,14,16,18,20,22,24,26,28,30},{32,34,36,38,40,42,44,46,4..., dimensions={0} | all-to-all | bytes 393216 | tf_op jit(solution)/shard_map/all_to_all | solution.py:38
  114.9 0.6 broadcast_in_dim.12
  115.6 3.4 %all-to-all-start.2 = ((f32[8,24,128]{2,1,0:T(8,128)}), f32[8,24,128]{2,1,0:T(8,128)S(1)}, u32[]{:S(2)}, u32[]{:S(2)}) async-start(f32[8,24,128]{2,1,0:T(8,128)} %broadcast_in_dim.12), calls=%async_computation.2 | async-start | bytes 196608 | tf_op jit(solution)/shard_map/all_to_all | solution.py:38
  119.0 7.5 %all-to-all-done.2 = f32[8,24,128]{2,1,0:T(8,128)S(1)} async-done(((f32[8,24,128]{2,1,0:T(8,128)}), f32[8,24,128]{2,1,0:T(8,128)S(1)}, u32[]{:S(2)}, u32[]{:S(2)}) %all-to-all-start.2) | async-done | bytes 98336 | tf_op jit(solution)/shard_map/all_to_all | solution.py:38
  126.5 0.7 broadcast_in_dim.13
  127.2 3.7 %all-to-all-start.3 = ((f32[16,24,128]{2,1,0:T(8,128)}), f32[16,24,128]{2,1,0:T(8,128)S(1)}, u32[]{:S(2)}, u32[]{:S(2)}) async-start(f32[16,24,128]{2,1,0:T(8,128)} %broadcast_in_dim.13), calls=%async_computation.3 | async-start | bytes 393216 | tf_op jit(solution)/shard_map/all_to_all | solution.py:38
  131.0 6.9 %all-to-all-done.3 = f32[16,24,128]{2,1,0:T(8,128)S(1)} async-done(((f32[16,24,128]{2,1,0:T(8,128)}), f32[16,24,128]{2,1,0:T(8,128)S(1)}, u32[]{:S(2)}, u32[]{:S(2)}) %all-to-all-start.3) | async-done | bytes 196640 | tf_op jit(solution)/shard_map/all_to_all | solution.py:38
  137.9 4.0 %collective-permute-start.11 = (f32[384,128]{1,0:T(8,128)S(1)}, f32[384,128]{1,0:T(8,128)S(1)}, u32[]{:S(2)}, u32[]{:S(2)}) collective-permute-start(f32[384,128]{1,0:T(8,128)S(1)} %bitcast.10), channel_id=1, source_target_pairs={{0,1},{1,0},{2,3},{3,2},{4,5},{5,4},{6,7},{7,6},{8,9},{9,8},{10,11... | collective-permute-start | bytes 589832 | tf_op jit(solution)/shard_map/ppermute | solution.py:360
  141.9 0.6 maximum_bitcast_fusion.chosen_ref
  142.5 0.4 collective-permute-done.11.theirs_ref
  143.0 0.7 copy-done.1
  143.6 12.0 %final.1 = (f32[32,3072]{1,0:T(8,128)}, f32[32,3072]{1,0:T(8,128)}, f32[192,192]{1,0:T(8,128)}) custom-call(s32[3]{0:T(128)} %pad_add_fusion.info, f32[384,128]{1,0:T(8,128)} %bitcast.11, f32[384,128]{1,0:T(8,128)} %copy-done.1, f32[64,192]{1,0:T(8,128)} %maximum_bitcast_fusion.chosen_ref, bf16[192,3072]{1,0:T(8,128)(2,1)} %get-tuple-element.17.high_ref, ...), custom_call_target="tpu_custom_call" | custom-call | flops 400000000 | bytes 4000000 | tf_op jit(solution)/shard_map/final/pallas_call | solution.py:348
  (52 shorter events, 0.6 us)
Async XLA Ops:
  0.6 37.7 %copy-start.6 = (f32[32,3072]{1,0:T(8,128)S(1)}, f32[32,3072]{1,0:T(8,128)}, u32[]{:S(2)}) copy-start(f32[32,3072]{1,0:T(8,128)} %x_ref.3) | copy-start | bytes 1179652
  0.6 27.3 %copy-start.7 = (f32[32,3072]{1,0:T(8,128)S(1)}, f32[32,3072]{1,0:T(8,128)}, u32[]{:S(2)}) copy-start(f32[32,3072]{1,0:T(8,128)} %p_ref.1) | copy-start | bytes 1179652
  0.7 34.9 %copy-start.4 = (s32[24,6]{0,1:T(8,128)S(1)}, s32[24,6]{0,1:T(8,128)}, u32[]{:S(2)}) copy-start(s32[24,6]{0,1:T(8,128)} %param.8) | copy-start | bytes 1732
  0.7 37.6 %collective-permute-start = (f32[32,3072]{1,0:T(8,128)}, f32[32,3072]{1,0:T(8,128)S(1)}, u32[]{:S(2)}, u32[]{:S(2)}) collective-permute-start(f32[32,3072]{1,0:T(8,128)} %x_ref.3), channel_id=1, source_target_pairs={{0,2},{2,4},{4,6},{6,8},{8,10},{10,12},{12,14},{14,16},{16,18},{18... | collective-permute-start | bytes 1179656 | tf_op jit(solution)/shard_map/ppermute | solution.py:375
  2.9 35.6 %collective-permute-start.1 = (f32[32,3072]{1,0:T(8,128)}, f32[32,3072]{1,0:T(8,128)S(1)}, u32[]{:S(2)}, u32[]{:S(2)}) collective-permute-start(f32[32,3072]{1,0:T(8,128)} %x_ref.3), channel_id=1, source_target_pairs={{0,254},{2,0},{4,2},{6,4},{8,6},{10,8},{12,10},{14,12},{16,14},{18... | collective-permute-start | bytes 1179656 | tf_op jit(solution)/shard_map/ppermute | solution.py:376
  21.1 42.7 %copy-start.5 = (pred[1,128]{1,0:T(4,128)(4,1)S(1)}, pred[1,128]{1,0:T(4,128)(4,1)}, u32[]{:S(2)}) copy-start(pred[1,128]{1,0:T(4,128)(4,1)} %constant.24.clone.1) | copy-start | bytes 388
  21.1 8.2 %collective-permute-start.2 = (f32[24,128]{1,0:T(8,128)}, f32[24,128]{1,0:T(8,128)S(1)}, u32[]{:S(2)}, u32[]{:S(2)}) collective-permute-start(f32[24,128]{1,0:T(8,128)} %get-tuple-element.12.s_ref), channel_id=1, source_target_pairs={{0,2},{2,4},{4,6},{6,8},{8,10},{10,12},{12,14},{14,16},{16,18},{18... | collective-permute-start | bytes 36872 | tf_op jit(solution)/shard_map/ppermute | solution.py:378
  21.1 15.1 %collective-permute-start.3 = (f32[24,128]{1,0:T(8,128)}, f32[24,128]{1,0:T(8,128)S(1)}, u32[]{:S(2)}, u32[]{:S(2)}) collective-permute-start(f32[24,128]{1,0:T(8,128)} %get-tuple-element.12.s_ref), channel_id=1, source_target_pairs={{0,254},{2,0},{4,2},{6,4},{8,6},{10,8},{12,10},{14,12},{16,14},{18... | collective-permute-start | bytes 36872 | tf_op jit(solution)/shard_map/ppermute | solution.py:379
  28.0 27.9 %collective-permute-start.6 = (f32[32,3072]{1,0:T(8,128)S(1)}, f32[32,3072]{1,0:T(8,128)S(1)}, u32[]{:S(2)}, u32[]{:S(2)}) collective-permute-start(f32[32,3072]{1,0:T(8,128)S(1)} %copy-done.7), channel_id=1, source_target_pairs={{0,2},{2,4},{4,6},{6,8},{8,10},{10,12},{12,14},{14,16},{16,18},{18... | collective-permute-start | bytes 1179656 | tf_op jit(solution)/shard_map/ppermute | solution.py:381
  29.3 9.2 %copy-start.16 = (f32[24,128]{1,0:T(8,128)}, f32[24,128]{1,0:T(8,128)S(1)}, u32[]{:S(2)}) copy-start(f32[24,128]{1,0:T(8,128)S(1)} %collective-permute-done.2.sb_ref) | copy-start | bytes 36868
  29.3 33.5 %collective-permute-start.7 = (f32[32,3072]{1,0:T(8,128)S(1)}, f32[32,3072]{1,0:T(8,128)S(1)}, u32[]{:S(2)}, u32[]{:S(2)}) collective-permute-start(f32[32,3072]{1,0:T(8,128)S(1)} %copy-done.7), channel_id=1, source_target_pairs={{0,254},{2,0},{4,2},{6,4},{8,6},{10,8},{12,10},{14,12},{16,14},{18... | collective-permute-start | bytes 1179656 | tf_op jit(solution)/shard_map/ppermute | solution.py:382
  36.2 2.2 %copy-start.17 = (f32[24,128]{1,0:T(8,128)}, f32[24,128]{1,0:T(8,128)S(1)}, u32[]{:S(2)}) copy-start(f32[24,128]{1,0:T(8,128)S(1)} %collective-permute-done.3.sa_ref) | copy-start | bytes 36868
  36.2 35.2 %collective-permute-start.10 = (f32[32,3072]{1,0:T(8,128)S(1)}, f32[32,3072]{1,0:T(8,128)S(1)}, u32[]{:S(2)}, u32[]{:S(2)}) collective-permute-start(f32[32,3072]{1,0:T(8,128)S(1)} %copy-done.7), channel_id=1, source_target_pairs={{0,1},{1,0},{2,3},{3,2},{4,5},{5,4},{6,7},{7,6},{8,9},{9,8},{10,11... | collective-permute-start | bytes 1179656 | tf_op jit(solution)/shard_map/ppermute | solution.py:360
  38.3 0.7 copy-start.12
  38.3 33.1 %collective-permute-start.8 = (f32[32,3072]{1,0:T(8,128)S(1)}, f32[32,3072]{1,0:T(8,128)S(1)}, u32[]{:S(2)}, u32[]{:S(2)}) collective-permute-start(f32[32,3072]{1,0:T(8,128)S(1)} %copy-done.6), channel_id=1, source_target_pairs={{0,1},{1,0},{2,3},{3,2},{4,5},{5,4},{6,7},{7,6},{8,9},{9,8},{10,11... | collective-permute-start | bytes 1179656 | tf_op jit(solution)/shard_map/ppermute | solution.py:360
  38.4 0.8 copy-start.13
  55.9 28.4 %collective-permute-start.4 = (f32[32,3072]{1,0:T(8,128)}, f32[32,3072]{1,0:T(8,128)S(1)}, u32[]{:S(2)}, u32[]{:S(2)}) collective-permute-start(f32[32,3072]{1,0:T(8,128)} %get-tuple-element.14.y_ref), channel_id=1, source_target_pairs={{0,2},{2,4},{4,6},{6,8},{8,10},{10,12},{12,14},{14,16},{16,18},{18... | collective-permute-start | bytes 1179656 | tf_op jit(solution)/shard_map/ppermute | solution.py:386
  55.9 28.5 %copy-start.8 = (f32[32,3072]{1,0:T(8,128)}, f32[32,3072]{1,0:T(8,128)S(1)}, u32[]{:S(2)}) copy-start(f32[32,3072]{1,0:T(8,128)S(1)} %collective-permute-done.6.pb_ref) | copy-start | bytes 1179652
  55.9 28.4 %collective-permute-start.5 = (f32[32,3072]{1,0:T(8,128)}, f32[32,3072]{1,0:T(8,128)S(1)}, u32[]{:S(2)}, u32[]{:S(2)}) collective-permute-start(f32[32,3072]{1,0:T(8,128)} %get-tuple-element.14.y_ref), channel_id=1, source_target_pairs={{0,254},{2,0},{4,2},{6,4},{8,6},{10,8},{12,10},{14,12},{16,14},{18... | collective-permute-start | bytes 1179656 | tf_op jit(solution)/shard_map/ppermute | solution.py:387
  62.8 21.6 %copy-start.9 = (f32[32,3072]{1,0:T(8,128)}, f32[32,3072]{1,0:T(8,128)S(1)}, u32[]{:S(2)}) copy-start(f32[32,3072]{1,0:T(8,128)S(1)} %collective-permute-done.7.pa_ref) | copy-start | bytes 1179652
  62.8 21.6 %collective-permute-start.9 = (f32[32,3072]{1,0:T(8,128)}, f32[32,3072]{1,0:T(8,128)}, u32[]{:S(2)}, u32[]{:S(2)}) collective-permute-start(f32[32,3072]{1,0:T(8,128)} %get-tuple-element.14.y_ref), channel_id=1, source_target_pairs={{0,1},{1,0},{2,3},{3,2},{4,5},{5,4},{6,7},{7,6},{8,9},{9,8},{10,11... | collective-permute-start | bytes 1179656 | tf_op jit(solution)/shard_map/ppermute | solution.py:360
  65.3 19.0 %all-to-all-start = ((f32[256,1,128]{2,1,0:T(1,128)}), f32[256,1,128]{2,1,0:T(1,128)S(1)}, u32[]{:S(2)}, u32[]{:S(2)}) async-start(f32[256,1,128]{2,1,0:T(1,128)} %broadcast_in_dim.11), calls=%async_computation | async-start | bytes 262144 | tf_op jit(solution)/shard_map/all_to_all | solution.py:392
  71.4 13.0 %copy-start.10 = (f32[32,3072]{1,0:T(8,128)}, f32[32,3072]{1,0:T(8,128)S(1)}, u32[]{:S(2)}) copy-start(f32[32,3072]{1,0:T(8,128)S(1)} %collective-permute-done.10.po_ref) | copy-start | bytes 1179652
  71.4 13.0 %copy-start.11 = (f32[32,3072]{1,0:T(8,128)}, f32[32,3072]{1,0:T(8,128)S(1)}, u32[]{:S(2)}) copy-start(f32[32,3072]{1,0:T(8,128)S(1)} %collective-permute-done.8.xo_ref) | copy-start | bytes 1179652
  84.3 0.8 copy-start.14
  84.3 0.9 copy-start.15
  85.2 45.7 %copy-start.2 = (f32[192,64]{0,1:T(8,128)S(1)}, f32[192,64]{0,1:T(8,128)}, u32[]{:S(2)}) copy-start(f32[192,64]{0,1:T(8,128)} %param.9) | copy-start | bytes 147460
  115.6 11.0 %all-to-all-start.2 = ((f32[8,24,128]{2,1,0:T(8,128)}), f32[8,24,128]{2,1,0:T(8,128)S(1)}, u32[]{:S(2)}, u32[]{:S(2)}) async-start(f32[8,24,128]{2,1,0:T(8,128)} %broadcast_in_dim.12), calls=%async_computation.2 | async-start | bytes 196608 | tf_op jit(solution)/shard_map/all_to_all | solution.py:38
  127.2 10.7 %all-to-all-start.3 = ((f32[16,24,128]{2,1,0:T(8,128)}), f32[16,24,128]{2,1,0:T(8,128)S(1)}, u32[]{:S(2)}, u32[]{:S(2)}) async-start(f32[16,24,128]{2,1,0:T(8,128)} %broadcast_in_dim.13), calls=%async_computation.3 | async-start | bytes 393216 | tf_op jit(solution)/shard_map/all_to_all | solution.py:38
  137.9 5.1 %copy-start = (f32[16,24,128]{2,1,0:T(8,128)}, f32[16,24,128]{2,1,0:T(8,128)S(1)}, u32[]{:S(2)}) copy-start(f32[16,24,128]{2,1,0:T(8,128)S(1)} %all-to-all-done.3) | copy-start | bytes 589828
  137.9 5.1 %collective-permute-start.11 = (f32[384,128]{1,0:T(8,128)S(1)}, f32[384,128]{1,0:T(8,128)S(1)}, u32[]{:S(2)}, u32[]{:S(2)}) collective-permute-start(f32[384,128]{1,0:T(8,128)S(1)} %bitcast.10), channel_id=1, source_target_pairs={{0,1},{1,0},{2,3},{3,2},{4,5},{5,4},{6,7},{7,6},{8,9},{9,8},{10,11... | collective-permute-start | bytes 589832 | tf_op jit(solution)/shard_map/ppermute | solution.py:360
  143.0 0.7 copy-start.1
  (1 other events, 0.7 us)

commit v3 on v2

v3 whole, which is shorter than its diff:
```python
import functools
import math

import jax
import jax.numpy as jnp
from jax import lax
from jax.experimental import pallas as pl
from jax.experimental.pallas import tpu as pltpu
from jax.sharding import PartitionSpec as P

BLK = 128
F32 = jnp.float32
BF16 = jnp.bfloat16
UNROLL = 24
GROUP = 6
CHUNK = 8
VMEM_LIMIT = 60 * 2**20
PIVOTS = 16
EXACT = lax.Precision.HIGHEST


def halves(v):
    high = v.astype(BF16)
    return high, (v - high.astype(F32)).astype(BF16)


def ring(devices, step):
    return [(i, (i + step) % devices) for i in range(devices)]


def row_of(z, x, y):
    return z * 16 + x * 4 + y


def plane_groups():
    return [[row_of(z, x, y) for x in range(4) for y in range(4)] for z in range(8)]


def column_groups():
    return [[row_of(z, x, y) for z in range(8)] for x in range(4) for y in range(4)]


def sheet_groups():
    return [[row_of(z, x, y) for z in range(8) for x in range(4)] for y in range(4)]


def line_groups():
    return [[row_of(z, x, y) for y in range(4)] for z in range(8) for x in range(4)]


def with_cores(groups):
    return [[2 * i + core for core in range(2) for i in group] for group in groups]


def exchange(x, groups):
    return lax.all_to_all(x, "rows", 0, 0, axis_index_groups=groups)


def exchange_cores(x, groups):
    return lax.all_to_all(x, ("rows", "cols"), 0, 0, axis_index_groups=with_cores(groups))


def repeated(x, count):
    return jnp.broadcast_to(x[None], (count,) + x.shape)


def sum_large(x):
    part = jnp.sum(exchange(x, plane_groups()), axis=0)
    part = jnp.sum(exchange(repeated(part, 8), column_groups()), axis=0)
    return exchange_cores(repeated(part, 32), plane_groups())


def prepare_kernel(a_hbm, split_hbm, scale_ref, a_ref, split_ref, arrived, sent):
    count = a_ref.shape[0]
    arrivals = [pltpu.make_async_copy(a_hbm.at[i], a_ref.at[i], arrived.at[i]) for i in range(count)]
    sends = [pltpu.make_async_copy(split_ref.at[i], split_hbm.at[i], sent.at[i]) for i in range(count)]
    for copy in arrivals:
        copy.start()
    for i in range(count):
        if i % GROUP == 0:
            for copy in arrivals[i : i + GROUP]:
                copy.wait()
        total = a_ref[i, 0]
        for k in range(6):
            a = a_ref[i, k]
            if k:
                total = total + a
            high, low = halves(a)
            split_ref[i, 0:BLK, k * BLK : (k + 1) * BLK] = high
            split_ref[i, BLK : 2 * BLK, k * BLK : (k + 1) * BLK] = low
        scale_ref[i : i + 1, :] = lax.rsqrt(jnp.sum(total.T, axis=0, keepdims=True))
        if i % GROUP == GROUP - 1:
            for copy in sends[i + 1 - GROUP : i + 1]:
                copy.start()
    for copy in sends:
        copy.wait()


def prepare(affinity):
    n = affinity.shape[0]
    split = (n, 2 * BLK, 6 * BLK)
    return pl.pallas_call(
        prepare_kernel,
        in_specs=[pl.BlockSpec(memory_space=pl.ANY)],
        out_specs=[pl.BlockSpec(memory_space=pl.ANY), pl.BlockSpec(memory_space=pltpu.VMEM)],
        out_shape=[jax.ShapeDtypeStruct(split, BF16), jax.ShapeDtypeStruct((n, BLK), F32)],
        scratch_shapes=[
            pltpu.VMEM((n, 6, BLK, BLK), F32),
            pltpu.VMEM(split, BF16),
            pltpu.SemaphoreType.DMA((n,)),
            pltpu.SemaphoreType.DMA((n,)),
        ],
        compiler_params=pltpu.CompilerParams(vmem_limit_bytes=VMEM_LIMIT),
        cost_estimate=pl.CostEstimate(flops=10**7, bytes_accessed=19 * 10**6, transcendentals=3072),
        name="prepare",
    )(affinity)


def block_of(ref, i):
    return ref[:, pl.ds(pl.multiple_of(i * BLK, BLK), BLK)]


def local_place(index, first, total):
    place = index - first
    place = jnp.where(place < 0, place + total, place)
    return jnp.where(place >= total, place - total, place)


def gathered(info, pat, turned, i):
    places = [local_place(pat[i, k], info[1], info[2]) for k in range(6)]
    return jnp.concatenate([turned[place] for place in places], axis=0)


def loads(a_hbm, split_ref, arrived):
    copies = [pltpu.make_async_copy(a_hbm.at[i], split_ref.at[i], arrived.at[i]) for i in range(a_hbm.shape[0])]
    for copy in copies:
        copy.start()
    return copies


def turn(turned, place, v):
    turned[place] = v.T.astype(BF16)


def first_kernel(
    info, pat, a_hbm, x_ref, xb_ref, xa_ref, p_ref, s_ref, sb_ref, sa_ref, yp_ref, sums_ref, split_ref, turned, arrived
):
    count = s_ref.shape[0]
    copies = loads(a_hbm, split_ref, arrived)
    for part, (v_ref, t_ref) in enumerate(((xb_ref, sb_ref), (x_ref, s_ref), (xa_ref, sa_ref))):

        @pl.loop(0, count, unroll=UNROLL)
        def _(j):
            v = block_of(v_ref, j) * t_ref[pl.ds(j, 1), :]
            high = v.astype(BF16).astype(F32)
            turn(turned, part * count + j, jnp.concatenate([high, v - high, jnp.zeros((64, BLK), F32)], axis=0))

    yp_ref[32:64, :] = p_ref[...]
    xy = jnp.zeros((32, BLK), F32)
    xx = jnp.zeros((32, BLK), F32)
    for i in range(count):
        lanes = slice(i * BLK, (i + 1) * BLK)
        if i % GROUP == 0:
            for copy in copies[i : i + GROUP]:
                copy.wait()
        weights = gathered(info, pat, turned, i)
        product = jnp.dot(split_ref[i], weights, preferred_element_type=F32)
        image = (product[:BLK] + product[BLK:]).T
        x = x_ref[:, lanes]
        y = x - s_ref[i : i + 1, :] * (image[0:32] + image[32:64])
        yp_ref[0:32, lanes] = y
        xy += x * y
        xx += x * x
    stack = jnp.concatenate([xy, xx, jnp.zeros((64, BLK), F32)], axis=0)
    sums_ref[...] = jnp.sum(stack.T, axis=0, keepdims=True)


def memory(*spaces):
    return [pl.BlockSpec(memory_space=space) for space in spaces]


def first_image(info, pattern, split, x, xb, xa, p, s, sb, sa):
    n = s.shape[0]
    return pl.pallas_call(
        first_kernel,
        in_specs=memory(pltpu.SMEM, pltpu.SMEM, pl.ANY, *[pltpu.VMEM] * 7),
        out_shape=[jax.ShapeDtypeStruct((64, x.shape[1]), F32), jax.ShapeDtypeStruct((1, BLK), F32)],
        scratch_shapes=[
            pltpu.VMEM(split.shape, BF16),
            pltpu.VMEM((3 * n, BLK, BLK), BF16),
            pltpu.SemaphoreType.DMA((n,)),
        ],
        compiler_params=pltpu.CompilerParams(vmem_limit_bytes=VMEM_LIMIT),
        cost_estimate=pl.CostEstimate(flops=4 * 10**9, bytes_accessed=11 * 10**6, transcendentals=0),
        name="first_image",
    )(info, pattern, split, x, xb, xa, p, s, sb, sa)


def second_kernel(
    info, pat, a_hbm, sums_ref, yp_ref, before_ref, after_ref, s_ref, sb_ref, sa_ref, x_ref, xo_ref, ypo_ref,
    high_ref, low_ref, out_ref, split_ref, turned, quotients, left_ref, acc, arrived,
):
    count = s_ref.shape[0]
    core = info[0]
    own = pl.multiple_of(core * 32, 32)
    other = pl.multiple_of((1 - core) * 32, 32)
    copies = loads(a_hbm, split_ref, arrived)

    sums = jnp.sum(sums_ref[...], axis=0, keepdims=True)
    column = jnp.broadcast_to(sums, (BLK, BLK)).T
    quotients[0:32] = column[0:32] / column[32:64]
    quotients[32:64] = column[64:96] / column[96:128]
    q_own = quotients[pl.ds(own, 32), :]
    q_other = quotients[pl.ds(other, 32), :]
    for part, (v_ref, t_ref) in enumerate(((before_ref, sb_ref), (yp_ref, s_ref), (after_ref, sa_ref))):

        @pl.loop(0, count, unroll=UNROLL)
        def _(j):
            v = block_of(v_ref, j) * t_ref[pl.ds(j, 1), :]
            high = v.astype(BF16).astype(F32)
            turn(turned, part * count + j, jnp.concatenate([high, v - high], axis=0))

    for i in range(count):
        lanes = slice(i * BLK, (i + 1) * BLK)
        place = slice(i % CHUNK * BLK, (i % CHUNK + 1) * BLK)
        if i % GROUP == 0:
            for copy in copies[i : i + GROUP]:
                copy.wait()
        weights = gathered(info, pat, turned, i)
        product = jnp.dot(split_ref[i], weights, preferred_element_type=F32)
        image = (product[:BLK] + product[BLK:]).T
        image = yp_ref[:, lanes] - s_ref[i : i + 1, :] * (image[0:64] + image[64:128])
        x, y, p = x_ref[:, lanes], yp_ref[0:32, lanes], yp_ref[32:64, lanes]
        for at, v in enumerate((y - q_own * x, x, p, image[0:32] - q_own * y, y, image[32:64])):
            high, low = halves(v)
            left_ref[32 * at : 32 * at + 32, place] = high
            left_ref[192 + 32 * at : 224 + 32 * at, place] = low
            if at < 3:
                high_ref[pl.ds(64 * at + own, 32), lanes] = high
                low_ref[pl.ds(64 * at + own, 32), lanes] = low
        xo = xo_ref[:, lanes]
        for at, v in enumerate((ypo_ref[0:32, lanes] - q_other * xo, xo, ypo_ref[32:64, lanes])):
            high, low = halves(v)
            high_ref[pl.ds(64 * at + other, 32), lanes] = high
            low_ref[pl.ds(64 * at + other, 32), lanes] = low
        if i % CHUNK == CHUNK - 1:
            span = slice((i + 1 - CHUNK) * BLK, (i + 1) * BLK)
            dims = (((1,), (1,)), ((), ()))
            left = left_ref[...]
            part = lax.dot_general(left, high_ref[:, span], dims, preferred_element_type=F32)
            part = part + lax.dot_general(left, low_ref[:, span], dims, preferred_element_type=F32)
            acc[...] = part if i < CHUNK else acc[...] + part

    total = acc[0:192] + acc[192:384]
    out_ref[0:192, :] = total[:, 0:BLK]
    out_ref[192:384, :] = jnp.concatenate([total[:, BLK:192], jnp.zeros((192, 64), F32)], axis=1)


def second_image(info, pattern, split, sums, yp, before, after, s, sb, sa, x, xo, ypo):
    n = s.shape[0]
    return pl.pallas_call(
        second_kernel,
        in_specs=memory(pltpu.SMEM, pltpu.SMEM, pl.ANY, *[pltpu.VMEM] * 10),
        out_shape=[jax.ShapeDtypeStruct((192, x.shape[1]), BF16)] * 2 + [jax.ShapeDtypeStruct((384, BLK), F32)],
        scratch_shapes=[
            pltpu.VMEM(split.shape, BF16),
            pltpu.VMEM((3 * n, BLK, BLK), BF16),
            pltpu.VMEM((64, BLK), F32),
            pltpu.VMEM((384, CHUNK * BLK), BF16),
            pltpu.VMEM((384, 192), F32),
            pltpu.SemaphoreType.DMA((n,)),
        ],
        compiler_params=pltpu.CompilerParams(vmem_limit_bytes=VMEM_LIMIT),
        cost_estimate=pl.CostEstimate(flops=8 * 10**9, bytes_accessed=18 * 10**6, transcendentals=0),
        name="second_image",
    )(info, pattern, split, sums, yp, before, after, s, sb, sa, x, xo, ypo)


def picked_row(groups, at):
    return jnp.broadcast_to(groups[at // 8][at % 8 : at % 8 + 1, :], (8, BLK))


def inverse_factor(block):
    lane = lax.broadcasted_iota(jnp.int32, (8, BLK), 1)
    sub = lax.broadcasted_iota(jnp.int32, (8, BLK), 0)
    a = []
    for g in range(4):
        unit = jnp.where(lane - 32 == sub + 8 * g, 1.0, 0.0)
        a.append(jnp.where(lane < 32, block[8 * g : 8 * g + 8, :], unit))
    for start in range(0, 32, PIVOTS):
        columns = [
            [jnp.broadcast_to(a[g][:, start + k : start + k + 1], (8, BLK)) if g >= start // 8 else None for g in range(4)]
            for k in range(PIVOTS)
        ]
        for k in range(PIVOTS):
            at = start + k
            own = at // 8
            pivot = 1.0 / picked_row(columns[k], at)
            factor = [columns[k][g] * pivot if g >= own else None for g in range(4)]
            factor[own] = jnp.where(sub > at % 8, factor[own], 0.0)
            for other in columns[k + 1 :]:
                e = picked_row(other, at)
                for g in range(own, 4):
                    other[g] = other[g] - factor[g] * e
            row = picked_row(a, at)
            for g in range(own, 4):
                a[g] = a[g] - factor[g] * row
    scaled = []
    for g in range(4):
        diagonal = jnp.sum(jnp.where(lane == sub + 8 * g, a[g], 0.0), axis=1, keepdims=True)
        scaled.append(a[g] * lax.rsqrt(diagonal))
    return jnp.concatenate(scaled, axis=0)[:, 32:64]


def exact(left, right, dims):
    return lax.dot_general(left, right, (dims, ((), ())), precision=EXACT, preferred_element_type=F32)


def inverse_cholesky(work, inverse):
    lane = lax.broadcasted_iota(jnp.int32, (32, 192), 1)
    sub = lax.broadcasted_iota(jnp.int32, (32, 192), 0)
    for at in range(0, 192, 32):
        rows = work[at : at + 32, :]
        if at < BLK:
            piece = rows[:, 0:BLK]
        else:
            piece = jnp.concatenate([rows[:, BLK:192], jnp.zeros((32, 64), F32)], axis=1)
        if at % BLK:
            piece = pltpu.roll(piece, BLK - at % BLK, 1)
        small = inverse_factor(piece)
        unit = jnp.where(lane - at == sub, 1.0, 0.0)
        rows = jnp.where((lane >= at) & (lane < at + 32), unit, rows)
        new = exact(small, rows, ((1,), (0,)))
        inverse[at : at + 32, :] = jnp.where(lane < at + 32, new, 0.0)
        if at < 160:
            update = exact(new, new, ((0,), (0,)))
            wide = lax.broadcasted_iota(jnp.int32, (160 - at, 192), 1)
            old = jnp.where((wide >= at) & (wide < at + 32), 0.0, work[at + 32 : 192, :])
            work[at + 32 : 192, :] = old - update[at + 32 : 192, :]


def final_kernel(
    both_ref, chosen_ref, high_ref, low_ref, vectors_ref, directions_ref, ritz_ref, work, raw, inverse, *, factor
):
    for at in range(6):
        for base, target in ((0, work), (96, raw)):
            row = 384 * (at % 2) + base + 32 * (at // 2)
            target[32 * at : 32 * at + 32, 0:BLK] = both_ref[row : row + 32, :]
            target[32 * at : 32 * at + 32, BLK:192] = both_ref[row + 192 : row + 224, 0:64]
    inverse_cholesky(work, inverse)
    whole_inverse = inverse[...]
    half = exact(whole_inverse, raw[...], ((1,), (1,)))
    ritz_ref[...] = exact(half, whole_inverse, ((1,), (1,)))
    mix = factor * exact(chosen_ref[...], whole_inverse, ((1,), (0,)))
    left = jnp.concatenate(halves(mix), axis=0)
    for at in range(0, high_ref.shape[1], 512):
        lanes = slice(at, at + 512)
        product = jnp.dot(left, high_ref[:, lanes], preferred_element_type=F32)
        product = product + jnp.dot(left, low_ref[:, lanes], preferred_element_type=F32)
        product = product[0:64] + product[64:128]
        vectors_ref[:, lanes] = product[0:32]
        directions_ref[:, lanes] = product[32:64]


def final(both, chosen, high, low, factor):
    return pl.pallas_call(
        functools.partial(final_kernel, factor=factor),
        in_specs=memory(*[pltpu.VMEM] * 4),
        out_shape=[jax.ShapeDtypeStruct((32, high.shape[1]), F32)] * 2 + [jax.ShapeDtypeStruct((192, 192), F32)],
        scratch_shapes=[pltpu.VMEM((192, 192), F32)] * 3,
        compiler_params=pltpu.CompilerParams(vmem_limit_bytes=VMEM_LIMIT),
        cost_estimate=pl.CostEstimate(flops=4 * 10**8, bytes_accessed=4 * 10**6, transcendentals=0),
        name="final",
    )(both, chosen, high, low)


def other_core(x):
    return lax.ppermute(x, "cols", [(0, 1), (1, 0)])


def local(vectors, directions, affinity, pattern, rotation):
    width, rows_dev = vectors.shape
    devices = lax.axis_size("rows")
    core = lax.axis_index("cols")
    total = 2 * width
    nodes = rows_dev * devices
    local_blocks = affinity.shape[0]
    all_blocks = local_blocks * devices
    first_block = (lax.axis_index("rows") - 1) * local_blocks
    info = jnp.stack([core, first_block, jnp.int32(all_blocks)]).astype(jnp.int32)
    up, down = ring(devices, 1), ring(devices, -1)

    x_before = lax.ppermute(vectors, "rows", up)
    x_after = lax.ppermute(vectors, "rows", down)
    split, scale = prepare(affinity)
    s_before = lax.ppermute(scale, "rows", up)
    s_after = lax.ppermute(scale, "rows", down)
    x_other = other_core(vectors)
    yp, sums = first_image(info, pattern, split, vectors, x_before, x_after, directions, scale, s_before, s_after)
    yp_before = lax.ppermute(yp, "rows", up)
    yp_after = lax.ppermute(yp, "rows", down)
    yp_other = other_core(yp)
    sums = jnp.sum(exchange(repeated(sums, 32), sheet_groups()), axis=0)
    half = sums[:, 0:64]
    blank = jnp.zeros_like(half)
    row = jnp.where(core == 0, jnp.concatenate([half, blank], axis=1), jnp.concatenate([blank, half], axis=1))
    sums = exchange_cores(repeated(row, 8), line_groups()).reshape(8, BLK)
    high, low, part = second_image(
        info, pattern, split, sums, yp, yp_before, yp_after, scale, s_before, s_after, vectors, x_other, yp_other
    )
    both = sum_large(part.reshape(16, 24, BLK)).reshape(768, BLK)
    mine = lambda m: lax.dynamic_slice_in_dim(m, core * width, width, 1)
    kept = jnp.concatenate([rotation[:total], jnp.zeros((total, total), F32), rotation[2 * total :]], axis=0)
    chosen = jnp.concatenate([mine(rotation), mine(kept)], axis=1).T
    new_vectors, new_directions, ritz_matrix = final(both, chosen, high, low, math.sqrt(nodes))
    return new_vectors, new_directions, ritz_matrix


def solution(mesh):
    in_specs = (P("cols", "rows"), P("cols", "rows"), P("rows", None, None, None), P("rows", None), P())
    out_specs = (P("cols", "rows"), P("cols", "rows"), P())
    return jax.shard_map(local, mesh=mesh, in_specs=in_specs, out_specs=out_specs, check_vma=False)
```

time: 156 us -> 139 us (0.89)
  Pallas kernels: 57.1 us -> 38.4 us
  blocking collectives: 10.4 us -> 24 us
  waiting for transfers between devices: 29 us -> 22.2 us
  starting transfers between devices: 51 us -> 45.8 us
    pallas_call x4, Pallas kernels: 57.1 us -> 38.4 us  [the longest x1 11.9 us: final(): pl.pallas_call(functools.partial(final_kernel, factor=factor), in_specs=m...]
    all_to_all x1 -> x2, blocking collectives: 10.4 us -> 24 us  [exchange(): return lax.all_to_all(x, 'rows', 0, 0, axis_index_groups=groups)]
    all_to_all x1 -> x2, starting transfers between devices: 6.04 us -> 12.3 us  [exchange_cores(): lax.all_to_all(x, ('rows', 'cols'), 0, 0, axis_index_groups=with_cores(gr...]
    all_to_all x2 -> x1, waiting for transfers between devices: 14.4 us -> 8.5 us  [exchange(): return lax.all_to_all(x, 'rows', 0, 0, axis_index_groups=groups)]
    ppermute x4 -> x2, starting transfers between devices: 12.5 us -> 7.04 us  [the longest x1 6.96 us: local(): yp_after = lax.ppermute(yp, 'rows', down)]
    ppermute x4 -> x2, starting transfers between devices: 7.21 us -> 2.67 us  [other_core(): return lax.ppermute(x, 'cols', [(0, 1), (1, 0)])]
    all_to_all x2 -> x1, starting transfers between devices: 7.1 us -> 5.62 us  [exchange(): return lax.all_to_all(x, 'rows', 0, 0, axis_index_groups=groups)]
    all_to_all x1 -> x2, waiting for transfers between devices: 12.9 us -> 13.7 us  [exchange_cores(): lax.all_to_all(x, ('rows', 'cols'), 0, 0, axis_index_groups=with_cores(gr...]
  transfers between devices with their start and end apart: 15 -> 11, of which waited for: 5 -> 3; matrix products, arithmetic and copies ran while one was open for 2% -> 3% of each run, Pallas kernels for 17% -> 6%
where the time goes in v3:
time: 139 us
  starting transfers between devices  45.8 us (33%)
  Pallas kernels  38.4 us (28%)
  blocking collectives  24 us (17%)
  waiting for transfers between devices  22.2 us (16%)
  local copies, waits for them, and re-layouts  6.4 us (5%)
    all_to_all x2, blocking collectives, exchange(): return lax.all_to_all(x, 'rows', 0, 0, axis_index_groups=groups)  24 us
    all_to_all x2, waiting for transfers between devices, exchange_cores(): lax.all_to_all(x, ('rows', 'cols'), 0, 0, axis_index_groups=with_cores(gr...  13.7 us
    all_to_all x2, starting transfers between devices, exchange_cores(): lax.all_to_all(x, ('rows', 'cols'), 0, 0, axis_index_groups=with_cores(gr...  12.3 us
    pallas_call x1, Pallas kernels, final(): pl.pallas_call(functools.partial(final_kernel, factor=factor), in_specs=m...  11.9 us
    pallas_call x1, Pallas kernels, second_image(): pl.pallas_call(second_kernel, in_specs=memory(pltpu.SMEM, pltpu.SMEM, pl....  10.7 us
    ppermute x1, starting transfers between devices, local(): x_after = lax.ppermute(vectors, 'rows', down)  9.02 us
    all_to_all x1, waiting for transfers between devices, exchange(): return lax.all_to_all(x, 'rows', 0, 0, axis_index_groups=groups)  8.5 us
    pallas_call x1, Pallas kernels, prepare(): pl.pallas_call(prepare_kernel, in_specs=[pl.BlockSpec(memory_space=pl.ANY...  8.38 us
  transfers between devices with their start and end apart: 11, of which 3 were waited for; matrix products, arithmetic and copies ran while one was open for 3% of the time, Pallas kernels for 6%

profile of v3, /device:TPU:1, one launch (start us, length us, event | category | flops | bytes accessed | tf_op | source)
XLA Modules:
  0.0 139.0 jit_solution(5372947823213002350)
XLA Ops:
  0.6 2.2 %collective-permute-start = (f32[32,3072]{1,0:T(8,128)}, f32[32,3072]{1,0:T(8,128)S(1)}, u32[]{:S(2)}, u32[]{:S(2)}) collective-permute-start(f32[32,3072]{1,0:T(8,128)} %x_ref.3), channel_id=1, source_target_pairs={{0,2},{2,4},{4,6},{6,8},{8,10},{10,12},{12,14},{14,16},{16,18},{18... | collective-permute-start | bytes 1179656 | tf_op jit(solution)/shard_map/ppermute | solution.py:393
  2.8 9.0 %collective-permute-start.1 = (f32[32,3072]{1,0:T(8,128)}, f32[32,3072]{1,0:T(8,128)S(1)}, u32[]{:S(2)}, u32[]{:S(2)}) collective-permute-start(f32[32,3072]{1,0:T(8,128)} %x_ref.3), channel_id=1, source_target_pairs={{0,254},{2,0},{4,2},{6,4},{8,6},{10,8},{12,10},{14,12},{16,14},{18... | collective-permute-start | bytes 1179656 | tf_op jit(solution)/shard_map/ppermute | solution.py:394
  11.9 8.4 %prepare.1 = (bf16[24,256,768]{2,1,0:T(8,128)(2,1)}, f32[24,128]{1,0:T(8,128)}) custom-call(f32[24,6,128,128]{3,2,1,0:T(8,128)} %a_hbm.1), custom_call_target="tpu_custom_call" | custom-call | flops 10000000 | bytes 19000000 | tf_op jit(solution)/shard_map/prepare/pallas_call | solution.py:102
  20.3 0.1 collective-permute-start.2
  20.4 6.9 %collective-permute-start.3 = (f32[24,128]{1,0:T(8,128)}, f32[24,128]{1,0:T(8,128)S(1)}, u32[]{:S(2)}, u32[]{:S(2)}) collective-permute-start(f32[24,128]{1,0:T(8,128)} %get-tuple-element.11.s_ref), channel_id=1, source_target_pairs={{0,254},{2,0},{4,2},{6,4},{8,6},{10,8},{12,10},{14,12},{16,14},{18... | collective-permute-start | bytes 36872 | tf_op jit(solution)/shard_map/ppermute | solution.py:397
  27.2 0.6 pad_add_fusion.info
  27.8 0.7 copy.16.pat
  28.6 0.5 copy-done.12
  29.1 0.2 copy-done.10
  29.3 0.1 copy-done.11
  29.4 7.4 %first_image.1 = (f32[64,3072]{1,0:T(8,128)}, f32[1,128]{1,0:T(1,128)}) custom-call(s32[3]{0:T(128)} %pad_add_fusion.info, s32[24,6]{1,0:T(8,128)} %copy.16.pat, bf16[24,256,768]{2,1,0:T(8,128)(2,1)} %get-tuple-element.10.a_hbm, f32[32,3072]{1,0:T(8,128)} %x_ref.3, f32[32,3072]{1,0:T(8,128)} %copy-done.10, f32[32,3072]{1,0:T(8,128)} %copy-done.11, ...), custom_call_target="tpu_custom_call" | custom-call | flops 4000000000 | bytes 11000000 | tf_op jit(solution)/shard_map/first_image/pallas_call | solution.py:184
  36.9 7.0 %collective-permute-start.5 = (f32[64,3072]{1,0:T(8,128)}, f32[64,3072]{1,0:T(8,128)S(1)}, u32[]{:S(2)}, u32[]{:S(2)}) collective-permute-start(f32[64,3072]{1,0:T(8,128)} %get-tuple-element.13.yp_ref), channel_id=1, source_target_pairs={{0,254},{2,0},{4,2},{6,4},{8,6},{10,8},{12,10},{14,12},{16,14},{18... | collective-permute-start | bytes 2359304 | tf_op jit(solution)/shard_map/ppermute | solution.py:401
  43.9 2.7 %collective-permute-start.7 = (f32[64,3072]{1,0:T(8,128)}, f32[64,3072]{1,0:T(8,128)S(1)}, u32[]{:S(2)}, u32[]{:S(2)}) collective-permute-start(f32[64,3072]{1,0:T(8,128)} %get-tuple-element.13.yp_ref), channel_id=1, source_target_pairs={{0,1},{1,0},{2,3},{3,2},{4,5},{5,4},{6,7},{7,6},{8,9},{9,8},{10,11... | collective-permute-start | bytes 2359304 | tf_op jit(solution)/shard_map/ppermute | solution.py:378
  46.6 1.2 broadcast_in_dim.15
  47.8 5.6 %all-to-all-start = ((f32[32,1,128]{2,1,0:T(1,128)}), f32[32,1,128]{2,1,0:T(1,128)S(1)}, u32[]{:S(2)}, u32[]{:S(2)}) async-start(f32[32,1,128]{2,1,0:T(1,128)} %broadcast_in_dim.15), calls=%async_computation | async-start | bytes 32768 | tf_op jit(solution)/shard_map/all_to_all | solution.py:56
  53.5 8.5 %all-to-all-done = f32[32,1,128]{2,1,0:T(1,128)S(1)} async-done(((f32[32,1,128]{2,1,0:T(1,128)}), f32[32,1,128]{2,1,0:T(1,128)S(1)}, u32[]{:S(2)}, u32[]{:S(2)}) %all-to-all-start) | async-done | bytes 16416 | tf_op jit(solution)/shard_map/all_to_all | solution.py:56
  62.1 0.6 broadcast_in_dim.17
  62.7 5.2 %all-to-all-start.1 = ((f32[8,1,128]{2,1,0:T(1,128)}), f32[8,1,128]{2,1,0:T(1,128)S(1)}, u32[]{:S(2)}, u32[]{:S(2)}) async-start(f32[8,1,128]{2,1,0:T(1,128)} %broadcast_in_dim.17), calls=%async_computation.1 | async-start | bytes 8192 | tf_op jit(solution)/shard_map/all_to_all | solution.py:60
  67.8 4.5 %all-to-all-done.1 = f32[8,1,128]{2,1,0:T(1,128)S(1)} async-done(((f32[8,1,128]{2,1,0:T(1,128)}), f32[8,1,128]{2,1,0:T(1,128)S(1)}, u32[]{:S(2)}, u32[]{:S(2)}) %all-to-all-start.1) | async-done | bytes 4128 | tf_op jit(solution)/shard_map/all_to_all | solution.py:60
  72.4 0.5 copy-done.2
  72.9 0.3 copy-done.5
  73.2 0.2 copy-done.6
  73.5 0.3 copy-done.7
  73.7 10.7 %second_image.1 = (bf16[192,3072]{1,0:T(8,128)(2,1)}, bf16[192,3072]{1,0:T(8,128)(2,1)}, f32[384,128]{1,0:T(8,128)}) custom-call(s32[3]{0:T(128)} %pad_add_fusion.info, s32[24,6]{1,0:T(8,128)} %copy.16.pat, bf16[24,256,768]{2,1,0:T(8,128)(2,1)} %get-tuple-element.10.a_hbm, f32[8,128]{1,0:T(8,128)} %bitcast.18, f32[64,3072]{1,0:T(8,128)} %get-tuple-element.13.yp_ref, ...), custom_call_target="tpu_custom_call" | custom-call | flops 8000000000 | bytes 18000000 | tf_op jit(solution)/shard_map/second_image/pallas_call | solution.py:261
  84.4 10.5 %all_to_all.25 = f32[16,24,128]{2,1,0:T(8,128)S(1)} all-to-all(f32[16,24,128]{2,1,0:T(8,128)} %bitcast.15), channel_id=1, replica_groups={{0,2,4,6,8,10,12,14,16,18,20,22,24,26,28,30},{32,34,36,38,40,42,44,46,4..., dimensions={0} | all-to-all | bytes 393216 | tf_op jit(solution)/shard_map/all_to_all | solution.py:56
  95.0 13.4 %all_to_all.26 = f32[8,24,128]{2,1,0:T(8,128)S(1)} all-to-all(f32[8,24,128]{2,1,0:T(8,128)S(1)} %broadcast_in_dim.36), channel_id=1, replica_groups={{0,32,64,96,128,160,192,224},{2,34,66,98,130,162,194,226},{4,36,68,100,..., dimensions={0} | all-to-all | bytes 196608 | tf_op jit(solution)/shard_map/all_to_all | solution.py:56
  108.5 0.8 broadcast_in_dim.37
  109.2 7.1 %all-to-all-start.4 = ((f32[32,24,128]{2,1,0:T(8,128)}), f32[32,24,128]{2,1,0:T(8,128)S(1)}, u32[]{:S(2)}, u32[]{:S(2)}) async-start(f32[32,24,128]{2,1,0:T(8,128)} %broadcast_in_dim.37), calls=%async_computation.4 | async-start | bytes 786432 | tf_op jit(solution)/shard_map/all_to_all | solution.py:60
  116.5 0.6 maximum_bitcast_fusion.chosen_ref
  117.1 9.2 %all-to-all-done.4 = f32[32,24,128]{2,1,0:T(8,128)S(1)} async-done(((f32[32,24,128]{2,1,0:T(8,128)}), f32[32,24,128]{2,1,0:T(8,128)S(1)}, u32[]{:S(2)}, u32[]{:S(2)}) %all-to-all-start.4) | async-done | bytes 393248 | tf_op jit(solution)/shard_map/all_to_all | solution.py:60
  126.3 0.7 copy-done
  127.0 11.9 %final.1 = (f32[32,3072]{1,0:T(8,128)}, f32[32,3072]{1,0:T(8,128)}, f32[192,192]{1,0:T(8,128)}) custom-call(f32[768,128]{1,0:T(8,128)} %bitcast.14, f32[64,192]{1,0:T(8,128)} %maximum_bitcast_fusion.chosen_ref, bf16[192,3072]{1,0:T(8,128)(2,1)} %get-tuple-element.15.high_ref, bf16[192,3072]{1,0:T(8,128)(2,1)} %get-tuple-element.16.low_ref), custom_call_target="tpu_custom_call" | custom-call | flops 400000000 | bytes 4000000 | tf_op jit(solution)/shard_map/final/pallas_call | solution.py:366
  (39 shorter events, 0.4 us)
Async XLA Ops:
  0.6 27.2 %copy-start.3 = (s32[24,6]{0,1:T(8,128)S(1)}, s32[24,6]{0,1:T(8,128)}, u32[]{:S(2)}) copy-start(s32[24,6]{0,1:T(8,128)} %param.8) | copy-start | bytes 1732
  0.6 27.9 %collective-permute-start = (f32[32,3072]{1,0:T(8,128)}, f32[32,3072]{1,0:T(8,128)S(1)}, u32[]{:S(2)}, u32[]{:S(2)}) collective-permute-start(f32[32,3072]{1,0:T(8,128)} %x_ref.3), channel_id=1, source_target_pairs={{0,2},{2,4},{4,6},{6,8},{8,10},{10,12},{12,14},{14,16},{16,18},{18... | collective-permute-start | bytes 1179656 | tf_op jit(solution)/shard_map/ppermute | solution.py:393
  2.8 25.7 %collective-permute-start.1 = (f32[32,3072]{1,0:T(8,128)}, f32[32,3072]{1,0:T(8,128)S(1)}, u32[]{:S(2)}, u32[]{:S(2)}) collective-permute-start(f32[32,3072]{1,0:T(8,128)} %x_ref.3), channel_id=1, source_target_pairs={{0,254},{2,0},{4,2},{6,4},{8,6},{10,8},{12,10},{14,12},{16,14},{18... | collective-permute-start | bytes 1179656 | tf_op jit(solution)/shard_map/ppermute | solution.py:394
  20.2 26.3 %copy-start.8 = (f32[32,3072]{1,0:T(8,128)S(1)}, f32[32,3072]{1,0:T(8,128)}, u32[]{:S(2)}) copy-start(f32[32,3072]{1,0:T(8,128)} %x_ref.3) | copy-start | bytes 1179652
  20.3 41.7 %copy-start.4 = (pred[1,128]{1,0:T(4,128)(4,1)S(1)}, pred[1,128]{1,0:T(4,128)(4,1)}, u32[]{:S(2)}) copy-start(pred[1,128]{1,0:T(4,128)(4,1)} %constant.30.clone.1) | copy-start | bytes 388
  20.3 8.3 %collective-permute-start.2 = (f32[24,128]{1,0:T(8,128)}, f32[24,128]{1,0:T(8,128)S(1)}, u32[]{:S(2)}, u32[]{:S(2)}) collective-permute-start(f32[24,128]{1,0:T(8,128)} %get-tuple-element.11.s_ref), channel_id=1, source_target_pairs={{0,2},{2,4},{4,6},{6,8},{8,10},{10,12},{12,14},{14,16},{16,18},{18... | collective-permute-start | bytes 36872 | tf_op jit(solution)/shard_map/ppermute | solution.py:396
  20.4 8.2 %collective-permute-start.3 = (f32[24,128]{1,0:T(8,128)}, f32[24,128]{1,0:T(8,128)S(1)}, u32[]{:S(2)}, u32[]{:S(2)}) collective-permute-start(f32[24,128]{1,0:T(8,128)} %get-tuple-element.11.s_ref), channel_id=1, source_target_pairs={{0,254},{2,0},{4,2},{6,4},{8,6},{10,8},{12,10},{14,12},{16,14},{18... | collective-permute-start | bytes 36872 | tf_op jit(solution)/shard_map/ppermute | solution.py:397
  28.5 0.6 copy-start.12
  28.5 0.6 copy-start.13
  28.6 0.7 copy-start.10
  28.6 0.9 copy-start.11
  36.9 35.5 %collective-permute-start.4 = (f32[64,3072]{1,0:T(8,128)}, f32[64,3072]{1,0:T(8,128)S(1)}, u32[]{:S(2)}, u32[]{:S(2)}) collective-permute-start(f32[64,3072]{1,0:T(8,128)} %get-tuple-element.13.yp_ref), channel_id=1, source_target_pairs={{0,2},{2,4},{4,6},{6,8},{8,10},{10,12},{12,14},{14,16},{16,18},{18... | collective-permute-start | bytes 2359304 | tf_op jit(solution)/shard_map/ppermute | solution.py:400
  36.9 35.4 %collective-permute-start.5 = (f32[64,3072]{1,0:T(8,128)}, f32[64,3072]{1,0:T(8,128)S(1)}, u32[]{:S(2)}, u32[]{:S(2)}) collective-permute-start(f32[64,3072]{1,0:T(8,128)} %get-tuple-element.13.yp_ref), channel_id=1, source_target_pairs={{0,254},{2,0},{4,2},{6,4},{8,6},{10,8},{12,10},{14,12},{16,14},{18... | collective-permute-start | bytes 2359304 | tf_op jit(solution)/shard_map/ppermute | solution.py:401
  43.9 28.4 %collective-permute-start.7 = (f32[64,3072]{1,0:T(8,128)}, f32[64,3072]{1,0:T(8,128)S(1)}, u32[]{:S(2)}, u32[]{:S(2)}) collective-permute-start(f32[64,3072]{1,0:T(8,128)} %get-tuple-element.13.yp_ref), channel_id=1, source_target_pairs={{0,1},{1,0},{2,3},{3,2},{4,5},{5,4},{6,7},{7,6},{8,9},{9,8},{10,11... | collective-permute-start | bytes 2359304 | tf_op jit(solution)/shard_map/ppermute | solution.py:378
  46.6 21.3 %collective-permute-start.6 = (f32[32,3072]{1,0:T(8,128)S(1)}, f32[32,3072]{1,0:T(8,128)S(1)}, u32[]{:S(2)}, u32[]{:S(2)}) collective-permute-start(f32[32,3072]{1,0:T(8,128)S(1)} %copy-done.8), channel_id=1, source_target_pairs={{0,1},{1,0},{2,3},{3,2},{4,5},{5,4},{6,7},{7,6},{8,9},{9,8},{10,11... | collective-permute-start | bytes 1179656 | tf_op jit(solution)/shard_map/ppermute | solution.py:378
  47.8 14.1 %all-to-all-start = ((f32[32,1,128]{2,1,0:T(1,128)}), f32[32,1,128]{2,1,0:T(1,128)S(1)}, u32[]{:S(2)}, u32[]{:S(2)}) async-start(f32[32,1,128]{2,1,0:T(1,128)} %broadcast_in_dim.15), calls=%async_computation | async-start | bytes 32768 | tf_op jit(solution)/shard_map/all_to_all | solution.py:56
  62.7 9.6 %all-to-all-start.1 = ((f32[8,1,128]{2,1,0:T(1,128)}), f32[8,1,128]{2,1,0:T(1,128)S(1)}, u32[]{:S(2)}, u32[]{:S(2)}) async-start(f32[8,1,128]{2,1,0:T(1,128)} %broadcast_in_dim.17), calls=%async_computation.1 | async-start | bytes 8192 | tf_op jit(solution)/shard_map/all_to_all | solution.py:60
  67.8 4.5 %copy-start.9 = (f32[32,3072]{1,0:T(8,128)}, f32[32,3072]{1,0:T(8,128)S(1)}, u32[]{:S(2)}) copy-start(f32[32,3072]{1,0:T(8,128)S(1)} %collective-permute-done.6.xo_ref) | copy-start | bytes 1179652
  72.3 0.6 copy-start.2
  72.3 0.9 copy-start.5
  72.3 1.1 copy-start.6
  72.3 1.4 copy-start.7
  73.7 42.6 %copy-start.1 = (f32[192,64]{0,1:T(8,128)S(1)}, f32[192,64]{0,1:T(8,128)}, u32[]{:S(2)}) copy-start(f32[192,64]{0,1:T(8,128)} %param.9) | copy-start | bytes 147460
  109.2 17.1 %all-to-all-start.4 = ((f32[32,24,128]{2,1,0:T(8,128)}), f32[32,24,128]{2,1,0:T(8,128)S(1)}, u32[]{:S(2)}, u32[]{:S(2)}) async-start(f32[32,24,128]{2,1,0:T(8,128)} %broadcast_in_dim.37), calls=%async_computation.4 | async-start | bytes 786432 | tf_op jit(solution)/shard_map/all_to_all | solution.py:60
  126.3 0.8 copy-start

commit v4 on v3

--- a/solution.py
+++ b/solution.py
@@ -40,14 +40,6 @@
     return [[row_of(z, x, y) for z in range(8)] for x in range(4) for y in range(4)]
 
 
-def sheet_groups():
-    return [[row_of(z, x, y) for z in range(8) for x in range(4)] for y in range(4)]
-
-
-def line_groups():
-    return [[row_of(z, x, y) for y in range(4)] for z in range(8) for x in range(4)]
-
-
 def with_cores(groups):
     return [[2 * i + core for core in range(2) for i in group] for group in groups]
 
@@ -70,25 +62,59 @@
     return exchange_cores(repeated(part, 32), plane_groups())
 
 
-def prepare_kernel(a_hbm, split_hbm, scale_ref, a_ref, split_ref, arrived, sent):
+def loads(a_hbm, a_ref, arrived):
+    copies = [pltpu.make_async_copy(a_hbm.at[i], a_ref.at[i], arrived.at[i]) for i in range(a_hbm.shape[0])]
+    for copy in copies:
+        copy.start()
+    return copies
+
+
+def wait_group(copies, i):
+    if i % GROUP == 0:
+        for copy in copies[i : i + GROUP]:
+            copy.wait()
+
+
+def memory(*spaces):
+    return [pl.BlockSpec(memory_space=space) for space in spaces]
+
+
+def degree_kernel(a_hbm, x_ref, scale_ref, xs_ref, a_ref, arrived):
+    copies = loads(a_hbm, a_ref, arrived)
+    for i in range(a_ref.shape[0]):
+        wait_group(copies, i)
+        total = a_ref[i, 0]
+        for k in range(1, 6):
+            total = total + a_ref[i, k]
+        scale = lax.rsqrt(jnp.sum(total.T, axis=0, keepdims=True))
+        scale_ref[i : i + 1, :] = scale
+        lanes = slice(i * BLK, (i + 1) * BLK)
+        xs_ref[:, lanes] = x_ref[:, lanes] * scale
+
+
+def degrees(affinity, x):
+    n = affinity.shape[0]
+    return pl.pallas_call(
+        degree_kernel,
+        in_specs=memory(pl.ANY, pltpu.VMEM),
+        out_shape=[jax.ShapeDtypeStruct((n, BLK), F32), jax.ShapeDtypeStruct(x.shape, F32)],
+        scratch_shapes=[pltpu.VMEM(affinity.shape, F32), pltpu.SemaphoreType.DMA((n,))],
+        compiler_params=pltpu.CompilerParams(vmem_limit_bytes=VMEM_LIMIT),
+        cost_estimate=pl.CostEstimate(flops=10**7, bytes_accessed=10**7, transcendentals=3072),
+        name="degrees",
+    )(affinity, x)
+
+
+def split_kernel(a_hbm, scale_hbm, split_hbm, a_ref, split_ref, arrived, sent):
     count = a_ref.shape[0]
-    arrivals = [pltpu.make_async_copy(a_hbm.at[i], a_ref.at[i], arrived.at[i]) for i in range(count)]
+    copies = loads(a_hbm, a_ref, arrived)
     sends = [pltpu.make_async_copy(split_ref.at[i], split_hbm.at[i], sent.at[i]) for i in range(count)]
-    for copy in arrivals:
-        copy.start()
     for i in range(count):
-        if i % GROUP == 0:
-            for copy in arrivals[i : i + GROUP]:
-                copy.wait()
-        total = a_ref[i, 0]
+        wait_group(copies, i)
         for k in range(6):
-            a = a_ref[i, k]
-            if k:
-                total = total + a
-            high, low = halves(a)
+            high, low = halves(a_ref[i, k])
             split_ref[i, 0:BLK, k * BLK : (k + 1) * BLK] = high
             split_ref[i, BLK : 2 * BLK, k * BLK : (k + 1) * BLK] = low
-        scale_ref[i : i + 1, :] = lax.rsqrt(jnp.sum(total.T, axis=0, keepdims=True))
         if i % GROUP == GROUP - 1:
             for copy in sends[i + 1 - GROUP : i + 1]:
                 copy.start()
@@ -96,14 +122,14 @@
         copy.wait()
 
 
-def prepare(affinity):
+def split_affinity(affinity, scale):
     n = affinity.shape[0]
     split = (n, 2 * BLK, 6 * BLK)
     return pl.pallas_call(
-        prepare_kernel,
-        in_specs=[pl.BlockSpec(memory_space=pl.ANY)],
-        out_specs=[pl.BlockSpec(memory_space=pl.ANY), pl.BlockSpec(memory_space=pltpu.VMEM)],
-        out_shape=[jax.ShapeDtypeStruct(split, BF16), jax.ShapeDtypeStruct((n, BLK), F32)],
+        split_kernel,
+        in_specs=memory(pl.ANY, pl.ANY),
+        out_specs=pl.BlockSpec(memory_space=pl.ANY),
+        out_shape=jax.ShapeDtypeStruct(split, BF16),
         scratch_shapes=[
             pltpu.VMEM((n, 6, BLK, BLK), F32),
             pltpu.VMEM(split, BF16),
@@ -111,9 +137,9 @@
             pltpu.SemaphoreType.DMA((n,)),
         ],
         compiler_params=pltpu.CompilerParams(vmem_limit_bytes=VMEM_LIMIT),
-        cost_estimate=pl.CostEstimate(flops=10**7, bytes_accessed=19 * 10**6, transcendentals=3072),
-        name="prepare",
-    )(affinity)
+        cost_estimate=pl.CostEstimate(flops=10**7, bytes_accessed=19 * 10**6, transcendentals=0),
+        name="split",
+    )(affinity, scale)
 
 
 def block_of(ref, i):
@@ -131,60 +157,54 @@
     return jnp.concatenate([turned[place] for place in places], axis=0)
 
 
-def loads(a_hbm, split_ref, arrived):
-    copies = [pltpu.make_async_copy(a_hbm.at[i], split_ref.at[i], arrived.at[i]) for i in range(a_hbm.shape[0])]
-    for copy in copies:
-        copy.start()
-    return copies
-
-
-def turn(turned, place, v):
-    turned[place] = v.T.astype(BF16)
+def turn_all(turned, refs, count):
+    for part, v_ref in enumerate(refs):
+
+        @pl.loop(0, count, unroll=UNROLL)
+        def _(j):
+            v = block_of(v_ref, j)
+            high = v.astype(BF16).astype(F32)
+            stack = [high, v - high]
+            if v.shape[0] == 32:
+                stack.append(jnp.zeros((64, BLK), F32))
+            turned[part * count + j] = jnp.concatenate(stack, axis=0).T.astype(BF16)
 
 
 def first_kernel(
-    info, pat, a_hbm, x_ref, xb_ref, xa_ref, p_ref, s_ref, sb_ref, sa_ref, yp_ref, sums_ref, split_ref, turned, arrived
+    info, pat, a_hbm, x_ref, xs_ref, before_ref, after_ref, p_ref, s_ref, y_ref, scaled_ref, sums_ref, split_ref, turned, arrived
 ):
     count = s_ref.shape[0]
     copies = loads(a_hbm, split_ref, arrived)
-    for part, (v_ref, t_ref) in enumerate(((xb_ref, sb_ref), (x_ref, s_ref), (xa_ref, sa_ref))):
-
-        @pl.loop(0, count, unroll=UNROLL)
-        def _(j):
-            v = block_of(v_ref, j) * t_ref[pl.ds(j, 1), :]
-            high = v.astype(BF16).astype(F32)
-            turn(turned, part * count + j, jnp.concatenate([high, v - high, jnp.zeros((64, BLK), F32)], axis=0))
-
-    yp_ref[32:64, :] = p_ref[...]
+    turn_all(turned, (before_ref, xs_ref, after_ref), count)
     xy = jnp.zeros((32, BLK), F32)
     xx = jnp.zeros((32, BLK), F32)
     for i in range(count):
         lanes = slice(i * BLK, (i + 1) * BLK)
-        if i % GROUP == 0:
-            for copy in copies[i : i + GROUP]:
-                copy.wait()
+        wait_group(copies, i)
         weights = gathered(info, pat, turned, i)
         product = jnp.dot(split_ref[i], weights, preferred_element_type=F32)
         image = (product[:BLK] + product[BLK:]).T
-        x = x_ref[:, lanes]
-        y = x - s_ref[i : i + 1, :] * (image[0:32] + image[32:64])
-        yp_ref[0:32, lanes] = y
+        x, s = x_ref[:, lanes], s_ref[i : i + 1, :]
+        y = x - s * (image[0:32] + image[32:64])
+        y_ref[:, lanes] = y
+        scaled_ref[0:32, lanes] = s * y
+        scaled_ref[32:64, lanes] = s * p_ref[:, lanes]
         xy += x * y
         xx += x * x
     stack = jnp.concatenate([xy, xx, jnp.zeros((64, BLK), F32)], axis=0)
     sums_ref[...] = jnp.sum(stack.T, axis=0, keepdims=True)
 
 
-def memory(*spaces):
-    return [pl.BlockSpec(memory_space=space) for space in spaces]
-
-
-def first_image(info, pattern, split, x, xb, xa, p, s, sb, sa):
+def first_image(info, pattern, split, x, xs, before, after, p, s):
     n = s.shape[0]
     return pl.pallas_call(
         first_kernel,
-        in_specs=memory(pltpu.SMEM, pltpu.SMEM, pl.ANY, *[pltpu.VMEM] * 7),
-        out_shape=[jax.ShapeDtypeStruct((64, x.shape[1]), F32), jax.ShapeDtypeStruct((1, BLK), F32)],
+        in_specs=memory(pltpu.SMEM, pltpu.SMEM, pl.ANY, *[pltpu.VMEM] * 6),
+        out_shape=[
+            jax.ShapeDtypeStruct(x.shape, F32),
+            jax.ShapeDtypeStruct((64, x.shape[1]), F32),
+            jax.ShapeDtypeStruct((1, BLK), F32),
+        ],
         scratch_shapes=[
             pltpu.VMEM(split.shape, BF16),
             pltpu.VMEM((3 * n, BLK, BLK), BF16),
@@ -193,11 +213,11 @@
         compiler_params=pltpu.CompilerParams(vmem_limit_bytes=VMEM_LIMIT),
         cost_estimate=pl.CostEstimate(flops=4 * 10**9, bytes_accessed=11 * 10**6, transcendentals=0),
         name="first_image",
-    )(info, pattern, split, x, xb, xa, p, s, sb, sa)
+    )(info, pattern, split, x, xs, before, after, p, s)
 
 
 def second_kernel(
-    info, pat, a_hbm, sums_ref, yp_ref, before_ref, after_ref, s_ref, sb_ref, sa_ref, x_ref, xo_ref, ypo_ref,
+    info, pat, a_hbm, sums_ref, scaled_ref, before_ref, after_ref, s_ref, x_ref, y_ref, p_ref, xo_ref, yo_ref, po_ref,
     high_ref, low_ref, out_ref, split_ref, turned, quotients, left_ref, acc, arrived,
 ):
     count = s_ref.shape[0]
@@ -212,26 +232,18 @@
     quotients[32:64] = column[64:96] / column[96:128]
     q_own = quotients[pl.ds(own, 32), :]
     q_other = quotients[pl.ds(other, 32), :]
-    for part, (v_ref, t_ref) in enumerate(((before_ref, sb_ref), (yp_ref, s_ref), (after_ref, sa_ref))):
-
-        @pl.loop(0, count, unroll=UNROLL)
-        def _(j):
-            v = block_of(v_ref, j) * t_ref[pl.ds(j, 1), :]
-            high = v.astype(BF16).astype(F32)
-            turn(turned, part * count + j, jnp.concatenate([high, v - high], axis=0))
-
+    turn_all(turned, (before_ref, scaled_ref, after_ref), count)
     for i in range(count):
         lanes = slice(i * BLK, (i + 1) * BLK)
         place = slice(i % CHUNK * BLK, (i % CHUNK + 1) * BLK)
-        if i % GROUP == 0:
-            for copy in copies[i : i + GROUP]:
-                copy.wait()
+        wait_group(copies, i)
         weights = gathered(info, pat, turned, i)
         product = jnp.dot(split_ref[i], weights, preferred_element_type=F32)
         image = (product[:BLK] + product[BLK:]).T
-        image = yp_ref[:, lanes] - s_ref[i : i + 1, :] * (image[0:64] + image[64:128])
-        x, y, p = x_ref[:, lanes], yp_ref[0:32, lanes], yp_ref[32:64, lanes]
-        for at, v in enumerate((y - q_own * x, x, p, image[0:32] - q_own * y, y, image[32:64])):
+        x, y, p, s = x_ref[:, lanes], y_ref[:, lanes], p_ref[:, lanes], s_ref[i : i + 1, :]
+        z = y - s * (image[0:32] + image[64:96])
+        p_image = p - s * (image[32:64] + image[96:128])
+        for at, v in enumerate((y - q_own * x, x, p, z - q_own * y, y, p_image)):
             high, low = halves(v)
             left_ref[32 * at : 32 * at + 32, place] = high
             left_ref[192 + 32 * at : 224 + 32 * at, place] = low
@@ -239,7 +251,7 @@
                 high_ref[pl.ds(64 * at + own, 32), lanes] = high
                 low_ref[pl.ds(64 * at + own, 32), lanes] = low
         xo = xo_ref[:, lanes]
-        for at, v in enumerate((ypo_ref[0:32, lanes] - q_other * xo, xo, ypo_ref[32:64, lanes])):
+        for at, v in enumerate((yo_ref[:, lanes] - q_other * xo, xo, po_ref[:, lanes])):
             high, low = halves(v)
             high_ref[pl.ds(64 * at + other, 32), lanes] = high
             low_ref[pl.ds(64 * at + other, 32), lanes] = low
@@ -256,11 +268,11 @@
     out_ref[192:384, :] = jnp.concatenate([total[:, BLK:192], jnp.zeros((192, 64), F32)], axis=1)
 
 
-def second_image(info, pattern, split, sums, yp, before, after, s, sb, sa, x, xo, ypo):
+def second_image(info, pattern, split, sums, scaled, before, after, s, x, y, p, xo, yo, po):
     n = s.shape[0]
     return pl.pallas_call(
         second_kernel,
-        in_specs=memory(pltpu.SMEM, pltpu.SMEM, pl.ANY, *[pltpu.VMEM] * 10),
+        in_specs=memory(pltpu.SMEM, pltpu.SMEM, pl.ANY, *[pltpu.VMEM] * 11),
         out_shape=[jax.ShapeDtypeStruct((192, x.shape[1]), BF16)] * 2 + [jax.ShapeDtypeStruct((384, BLK), F32)],
         scratch_shapes=[
             pltpu.VMEM(split.shape, BF16),
@@ -273,7 +285,7 @@
         compiler_params=pltpu.CompilerParams(vmem_limit_bytes=VMEM_LIMIT),
         cost_estimate=pl.CostEstimate(flops=8 * 10**9, bytes_accessed=18 * 10**6, transcendentals=0),
         name="second_image",
-    )(info, pattern, split, sums, yp, before, after, s, sb, sa, x, xo, ypo)
+    )(info, pattern, split, sums, scaled, before, after, s, x, y, p, xo, yo, po)
 
 
 def picked_row(groups, at):
@@ -390,23 +402,22 @@
     info = jnp.stack([core, first_block, jnp.int32(all_blocks)]).astype(jnp.int32)
     up, down = ring(devices, 1), ring(devices, -1)
 
-    x_before = lax.ppermute(vectors, "rows", up)
-    x_after = lax.ppermute(vectors, "rows", down)
-    split, scale = prepare(affinity)
-    s_before = lax.ppermute(scale, "rows", up)
-    s_after = lax.ppermute(scale, "rows", down)
+    scale, xs = degrees(affinity, vectors)
+    xs_before = lax.ppermute(xs, "rows", up)
+    xs_after = lax.ppermute(xs, "rows", down)
+    split = split_affinity(affinity, scale)
     x_other = other_core(vectors)
-    yp, sums = first_image(info, pattern, split, vectors, x_before, x_after, directions, scale, s_before, s_after)
-    yp_before = lax.ppermute(yp, "rows", up)
-    yp_after = lax.ppermute(yp, "rows", down)
-    yp_other = other_core(yp)
-    sums = jnp.sum(exchange(repeated(sums, 32), sheet_groups()), axis=0)
+    p_other = other_core(directions)
+    y, scaled, sums = first_image(info, pattern, split, vectors, xs, xs_before, xs_after, directions, scale)
+    scaled_before = lax.ppermute(scaled, "rows", up)
+    scaled_after = lax.ppermute(scaled, "rows", down)
+    y_other = other_core(y)
     half = sums[:, 0:64]
     blank = jnp.zeros_like(half)
     row = jnp.where(core == 0, jnp.concatenate([half, blank], axis=1), jnp.concatenate([blank, half], axis=1))
-    sums = exchange_cores(repeated(row, 8), line_groups()).reshape(8, BLK)
+    sums = lax.all_to_all(repeated(row, 2 * devices), ("rows", "cols"), 0, 0).reshape(2 * devices, BLK)
     high, low, part = second_image(
-        info, pattern, split, sums, yp, yp_before, yp_after, scale, s_before, s_after, vectors, x_other, yp_other
+        info, pattern, split, sums, scaled, scaled_before, scaled_after, scale, vectors, y, directions, x_other, y_other, p_other
     )
     both = sum_large(part.reshape(16, 24, BLK)).reshape(768, BLK)
     mine = lambda m: lax.dynamic_slice_in_dim(m, core * width, width, 1)

time: 139 us -> 134 us (0.964)
  starting transfers between devices: 45.8 us -> 33.3 us
  Pallas kernels: 38.4 us -> 44.1 us
    ppermute x6 -> x4, starting transfers between devices: 25.2 us -> 18.2 us  [the longest x1 9.01 us: local(): xs_after = lax.ppermute(xs, 'rows', down)]
    pallas_call x1 -> x2, Pallas kernels: 8.38 us -> 13.7 us  [the longest x1 7.88 us: split_affinity(): pl.pallas_call(split_kernel, in_specs=memory(pl.ANY, pl.ANY), out_specs=p...]
    all_to_all x2 -> x1, starting transfers between devices: 12.3 us -> 6.99 us  [exchange_cores(): lax.all_to_all(x, ('rows', 'cols'), 0, 0, axis_index_groups=with_cores(gr...]
    all_to_all x2 -> x1, waiting for transfers between devices: 13.7 us -> 9.21 us  [exchange_cores(): lax.all_to_all(x, ('rows', 'cols'), 0, 0, axis_index_groups=with_cores(gr...]
    all_to_all x1, waiting for transfers between devices: 8.5 us -> 12.9 us  [local(): lax.all_to_all(repeated(row, 2 * devices), ('rows', 'cols'), 0, 0)]
    unnamed x29 -> x27, local copies, waits for them, and re-layouts: 3.69 us -> 4.14 us
  transfers between devices with their start and end apart: 11 -> 9, of which waited for: 3 -> 2; matrix products, arithmetic and copies ran while one was open for 3% -> 3% of each run, Pallas kernels for 6% -> 6%
where the time goes in v4:
time: 134 us; the launch traced here: 133 us
  Pallas kernels  44.1 us (33%)
  starting transfers between devices  33.3 us (25%)
  blocking collectives  25 us (19%)
  waiting for transfers between devices  22.1 us (16%)
  local copies, waits for them, and re-layouts  5.73 us (4%)
  other arithmetic  2.13 us (2%)
    all_to_all x2, blocking collectives, exchange(): return lax.all_to_all(x, 'rows', 0, 0, axis_index_groups=groups)  25 us
    all_to_all x1, waiting for transfers between devices, local(): lax.all_to_all(repeated(row, 2 * devices), ('rows', 'cols'), 0, 0)  12.9 us
    pallas_call x1, Pallas kernels, final(): pl.pallas_call(functools.partial(final_kernel, factor=factor), in_specs=m...  11.9 us
    pallas_call x1, Pallas kernels, second_image(): pl.pallas_call(second_kernel, in_specs=memory(pltpu.SMEM, pltpu.SMEM, pl....  10.9 us
    all_to_all x1, waiting for transfers between devices, exchange_cores(): lax.all_to_all(x, ('rows', 'cols'), 0, 0, axis_index_groups=with_cores(gr...  9.21 us
    ppermute x1, starting transfers between devices, local(): xs_after = lax.ppermute(xs, 'rows', down)  9.01 us
    pallas_call x1, Pallas kernels, split_affinity(): pl.pallas_call(split_kernel, in_specs=memory(pl.ANY, pl.ANY), out_specs=p...  7.88 us
    pallas_call x1, Pallas kernels, first_image(): pl.pallas_call(first_kernel, in_specs=memory(pltpu.SMEM, pltpu.SMEM, pl.A...  7.64 us
  transfers between devices with their start and end apart: 9, of which 2 were waited for; matrix products, arithmetic and copies ran while one was open for 3% of the time, Pallas kernels for 6%

profile of v4, /device:TPU:1, one launch (start us, length us, event | category | flops | bytes accessed | tf_op | source)
XLA Modules:
  0.0 133.2 jit_solution(698632284368266643)
XLA Ops:
  0.6 5.8 %degrees.1 = (f32[24,128]{1,0:T(8,128)}, f32[32,3072]{1,0:T(8,128)}) custom-call(f32[24,6,128,128]{3,2,1,0:T(8,128)} %a_hbm.3, f32[32,3072]{1,0:T(8,128)} %x_ref.5), custom_call_target="tpu_custom_call" | custom-call | flops 10000000 | bytes 10000000 | tf_op jit(solution)/shard_map/degrees/pallas_call | solution.py:97
  6.5 2.2 %collective-permute-start = (f32[32,3072]{1,0:T(8,128)}, f32[32,3072]{1,0:T(8,128)S(1)}, u32[]{:S(2)}, u32[]{:S(2)}) collective-permute-start(f32[32,3072]{1,0:T(8,128)} %get-tuple-element.12.xs_ref), channel_id=1, source_target_pairs={{0,2},{2,4},{4,6},{6,8},{8,10},{10,12},{12,14},{14,16},{16,18},{18... | collective-permute-start | bytes 1179656 | tf_op jit(solution)/shard_map/ppermute | solution.py:406
  8.7 9.0 %collective-permute-start.1 = (f32[32,3072]{1,0:T(8,128)}, f32[32,3072]{1,0:T(8,128)S(1)}, u32[]{:S(2)}, u32[]{:S(2)}) collective-permute-start(f32[32,3072]{1,0:T(8,128)} %get-tuple-element.12.xs_ref), channel_id=1, source_target_pairs={{0,254},{2,0},{4,2},{6,4},{8,6},{10,8},{12,10},{14,12},{16,14},{18... | collective-permute-start | bytes 1179656 | tf_op jit(solution)/shard_map/ppermute | solution.py:407
  17.7 0.7 copy.13.pat
  18.4 7.9 %split.1.a_hbm = bf16[24,256,768]{2,1,0:T(8,128)(2,1)} custom-call(f32[24,6,128,128]{3,2,1,0:T(8,128)} %a_hbm.3, f32[24,128]{1,0:T(8,128)} %get-tuple-element.11.scale_hbm.s_ref), custom_call_target="tpu_custom_call" | custom-call | flops 10000000 | bytes 19000000 | tf_op jit(solution)/shard_map/split/pallas_call | solution.py:128
  26.3 0.0 copy-start.5
  26.3 0.7 pad_add_fusion.info
  26.9 0.7 copy-done.11
  27.7 0.8 copy-done.12
  28.5 7.6 %first_image.1 = (f32[32,3072]{1,0:T(8,128)}, f32[64,3072]{1,0:T(8,128)}, f32[1,128]{1,0:T(1,128)}) custom-call(s32[3]{0:T(128)} %pad_add_fusion.info, s32[24,6]{1,0:T(8,128)} %copy.13.pat, bf16[24,256,768]{2,1,0:T(8,128)(2,1)} %split.1.a_hbm, f32[32,3072]{1,0:T(8,128)} %x_ref.5, f32[32,3072]{1,0:T(8,128)} %get-tuple-element.12.xs_ref, ...), custom_call_target="tpu_custom_call" | custom-call | flops 4000000000 | bytes 11000000 | tf_op jit(solution)/shard_map/first_image/pallas_call | solution.py:200
  36.1 0.1 collective-permute-start.2
  36.2 6.9 %collective-permute-start.3 = (f32[64,3072]{1,0:T(8,128)}, f32[64,3072]{1,0:T(8,128)S(1)}, u32[]{:S(2)}, u32[]{:S(2)}) collective-permute-start(f32[64,3072]{1,0:T(8,128)} %get-tuple-element.14.scaled_ref), channel_id=1, source_target_pairs={{0,254},{2,0},{4,2},{6,4},{8,6},{10,8},{12,10},{14,12},{16,14},{18... | collective-permute-start | bytes 2359304 | tf_op jit(solution)/shard_map/ppermute | solution.py:413
  43.1 1.5 %collective-permute-start.4 = (f32[32,3072]{1,0:T(8,128)S(1)}, f32[32,3072]{1,0:T(8,128)S(1)}, u32[]{:S(2)}, u32[]{:S(2)}) collective-permute-start(f32[32,3072]{1,0:T(8,128)S(1)} %copy-done.1), channel_id=1, source_target_pairs={{0,1},{1,0},{2,3},{3,2},{4,5},{5,4},{6,7},{7,6},{8,9},{9,8},{10,11... | collective-permute-start | bytes 1179656 | tf_op jit(solution)/shard_map/ppermute | solution.py:390
  44.6 0.1 collective-permute-start.6
  44.7 0.4 collective-permute-start.5
  45.1 0.8 fusion.2
  45.9 0.7 broadcast_in_dim.11
  46.7 6.1 %all-to-all-start = ((f32[256,1,128]{2,1,0:T(1,128)}), f32[256,1,128]{2,1,0:T(1,128)S(1)}, u32[]{:S(2)}, u32[]{:S(2)}) async-start(f32[256,1,128]{2,1,0:T(1,128)} %broadcast_in_dim.11), calls=%async_computation | async-start | bytes 262144 | tf_op jit(solution)/shard_map/all_to_all | solution.py:418
  52.8 12.9 %all-to-all-done = f32[256,1,128]{2,1,0:T(1,128)S(1)} async-done(((f32[256,1,128]{2,1,0:T(1,128)}), f32[256,1,128]{2,1,0:T(1,128)S(1)}, u32[]{:S(2)}, u32[]{:S(2)}) %all-to-all-start) | async-done | bytes 131104 | tf_op jit(solution)/shard_map/all_to_all | solution.py:418
  65.7 0.6 copy-done.3
  66.3 0.3 copy-done.6
  66.6 0.2 copy-done.7
  66.9 10.9 %second_image.1 = (bf16[192,3072]{1,0:T(8,128)(2,1)}, bf16[192,3072]{1,0:T(8,128)(2,1)}, f32[384,128]{1,0:T(8,128)}) custom-call(s32[3]{0:T(128)} %pad_add_fusion.info, s32[24,6]{1,0:T(8,128)} %copy.13.pat, bf16[24,256,768]{2,1,0:T(8,128)(2,1)} %split.1.a_hbm, f32[256,128]{1,0:T(8,128)} %bitcast.12, f32[64,3072]{1,0:T(8,128)} %get-tuple-element.14.scaled_ref, ...), custom_call_target="tpu_custom_call" | custom-call | flops 8000000000 | bytes 18000000 | tf_op jit(solution)/shard_map/second_image/pallas_call | solution.py:273
  77.8 10.4 %all_to_all.20 = f32[16,24,128]{2,1,0:T(8,128)S(1)} all-to-all(f32[16,24,128]{2,1,0:T(8,128)} %bitcast.11), channel_id=1, replica_groups={{0,2,4,6,8,10,12,14,16,18,20,22,24,26,28,30},{32,34,36,38,40,42,44,46,4..., dimensions={0} | all-to-all | bytes 393216 | tf_op jit(solution)/shard_map/all_to_all | solution.py:48
  88.2 14.6 %all_to_all.21 = f32[8,24,128]{2,1,0:T(8,128)S(1)} all-to-all(f32[8,24,128]{2,1,0:T(8,128)S(1)} %broadcast_in_dim.12), channel_id=1, replica_groups={{0,32,64,96,128,160,192,224},{2,34,66,98,130,162,194,226},{4,36,68,100,..., dimensions={0} | all-to-all | bytes 196608 | tf_op jit(solution)/shard_map/all_to_all | solution.py:48
  102.8 0.8 broadcast_in_dim.13
  103.6 7.0 %all-to-all-start.3 = ((f32[32,24,128]{2,1,0:T(8,128)}), f32[32,24,128]{2,1,0:T(8,128)S(1)}, u32[]{:S(2)}, u32[]{:S(2)}) async-start(f32[32,24,128]{2,1,0:T(8,128)} %broadcast_in_dim.13), calls=%async_computation.3 | async-start | bytes 786432 | tf_op jit(solution)/shard_map/all_to_all | solution.py:52
  110.6 0.1 pad.5.clone
  110.7 0.6 maximum_bitcast_fusion.chosen_ref
  111.3 9.2 %all-to-all-done.3 = f32[32,24,128]{2,1,0:T(8,128)S(1)} async-done(((f32[32,24,128]{2,1,0:T(8,128)}), f32[32,24,128]{2,1,0:T(8,128)S(1)}, u32[]{:S(2)}, u32[]{:S(2)}) %all-to-all-start.3) | async-done | bytes 393248 | tf_op jit(solution)/shard_map/all_to_all | solution.py:52
  120.5 0.7 copy-done
  121.3 11.9 %final.1 = (f32[32,3072]{1,0:T(8,128)}, f32[32,3072]{1,0:T(8,128)}, f32[192,192]{1,0:T(8,128)}) custom-call(f32[768,128]{1,0:T(8,128)} %bitcast.10, f32[64,192]{1,0:T(8,128)} %maximum_bitcast_fusion.chosen_ref, bf16[192,3072]{1,0:T(8,128)(2,1)} %get-tuple-element.17.high_ref, bf16[192,3072]{1,0:T(8,128)(2,1)} %get-tuple-element.18.low_ref), custom_call_target="tpu_custom_call" | custom-call | flops 400000000 | bytes 4000000 | tf_op jit(solution)/shard_map/final/pallas_call | solution.py:378
  (32 shorter events, 0.1 us)
Async XLA Ops:
  0.6 17.0 %copy-start.4 = (s32[24,6]{0,1:T(8,128)S(1)}, s32[24,6]{0,1:T(8,128)}, u32[]{:S(2)}) copy-start(s32[24,6]{0,1:T(8,128)} %param.8) | copy-start | bytes 1732
  6.5 20.5 %collective-permute-start = (f32[32,3072]{1,0:T(8,128)}, f32[32,3072]{1,0:T(8,128)S(1)}, u32[]{:S(2)}, u32[]{:S(2)}) collective-permute-start(f32[32,3072]{1,0:T(8,128)} %get-tuple-element.12.xs_ref), channel_id=1, source_target_pairs={{0,2},{2,4},{4,6},{6,8},{8,10},{10,12},{12,14},{14,16},{16,18},{18... | collective-permute-start | bytes 1179656 | tf_op jit(solution)/shard_map/ppermute | solution.py:406
  8.7 18.3 %collective-permute-start.1 = (f32[32,3072]{1,0:T(8,128)}, f32[32,3072]{1,0:T(8,128)S(1)}, u32[]{:S(2)}, u32[]{:S(2)}) collective-permute-start(f32[32,3072]{1,0:T(8,128)} %get-tuple-element.12.xs_ref), channel_id=1, source_target_pairs={{0,254},{2,0},{4,2},{6,4},{8,6},{10,8},{12,10},{14,12},{16,14},{18... | collective-permute-start | bytes 1179656 | tf_op jit(solution)/shard_map/ppermute | solution.py:407
  26.2 16.8 %copy-start.1 = (f32[32,3072]{1,0:T(8,128)S(1)}, f32[32,3072]{1,0:T(8,128)}, u32[]{:S(2)}) copy-start(f32[32,3072]{1,0:T(8,128)} %x_ref.5) | copy-start | bytes 1179652
  26.3 18.4 %copy-start.8 = (f32[32,3072]{1,0:T(8,128)S(1)}, f32[32,3072]{1,0:T(8,128)}, u32[]{:S(2)}) copy-start(f32[32,3072]{1,0:T(8,128)} %p_ref.3) | copy-start | bytes 1179652
  26.3 18.9 %copy-start.5 = (pred[1,128]{1,0:T(4,128)(4,1)S(1)}, pred[1,128]{1,0:T(4,128)(4,1)}, u32[]{:S(2)}) copy-start(pred[1,128]{1,0:T(4,128)(4,1)} %constant.24.clone.1) | copy-start | bytes 388
  26.9 0.7 copy-start.11
  27.7 0.8 copy-start.12
  36.1 29.5 %collective-permute-start.2 = (f32[64,3072]{1,0:T(8,128)}, f32[64,3072]{1,0:T(8,128)S(1)}, u32[]{:S(2)}, u32[]{:S(2)}) collective-permute-start(f32[64,3072]{1,0:T(8,128)} %get-tuple-element.14.scaled_ref), channel_id=1, source_target_pairs={{0,2},{2,4},{4,6},{6,8},{8,10},{10,12},{12,14},{14,16},{16,18},{18... | collective-permute-start | bytes 2359304 | tf_op jit(solution)/shard_map/ppermute | solution.py:412
  36.2 29.5 %collective-permute-start.3 = (f32[64,3072]{1,0:T(8,128)}, f32[64,3072]{1,0:T(8,128)S(1)}, u32[]{:S(2)}, u32[]{:S(2)}) collective-permute-start(f32[64,3072]{1,0:T(8,128)} %get-tuple-element.14.scaled_ref), channel_id=1, source_target_pairs={{0,254},{2,0},{4,2},{6,4},{8,6},{10,8},{12,10},{14,12},{16,14},{18... | collective-permute-start | bytes 2359304 | tf_op jit(solution)/shard_map/ppermute | solution.py:413
  43.1 9.6 %collective-permute-start.4 = (f32[32,3072]{1,0:T(8,128)S(1)}, f32[32,3072]{1,0:T(8,128)S(1)}, u32[]{:S(2)}, u32[]{:S(2)}) collective-permute-start(f32[32,3072]{1,0:T(8,128)S(1)} %copy-done.1), channel_id=1, source_target_pairs={{0,1},{1,0},{2,3},{3,2},{4,5},{5,4},{6,7},{7,6},{8,9},{9,8},{10,11... | collective-permute-start | bytes 1179656 | tf_op jit(solution)/shard_map/ppermute | solution.py:390
  44.6 8.1 %collective-permute-start.6 = (f32[32,3072]{1,0:T(8,128)S(1)}, f32[32,3072]{1,0:T(8,128)S(1)}, u32[]{:S(2)}, u32[]{:S(2)}) collective-permute-start(f32[32,3072]{1,0:T(8,128)S(1)} %copy-done.8), channel_id=1, source_target_pairs={{0,1},{1,0},{2,3},{3,2},{4,5},{5,4},{6,7},{7,6},{8,9},{9,8},{10,11... | collective-permute-start | bytes 1179656 | tf_op jit(solution)/shard_map/ppermute | solution.py:390
  44.7 20.9 %collective-permute-start.5 = (f32[32,3072]{1,0:T(8,128)}, f32[32,3072]{1,0:T(8,128)}, u32[]{:S(2)}, u32[]{:S(2)}) collective-permute-start(f32[32,3072]{1,0:T(8,128)} %get-tuple-element.15.y_ref), channel_id=1, source_target_pairs={{0,1},{1,0},{2,3},{3,2},{4,5},{5,4},{6,7},{7,6},{8,9},{9,8},{10,11... | collective-permute-start | bytes 1179656 | tf_op jit(solution)/shard_map/ppermute | solution.py:390
  46.7 19.0 %all-to-all-start = ((f32[256,1,128]{2,1,0:T(1,128)}), f32[256,1,128]{2,1,0:T(1,128)S(1)}, u32[]{:S(2)}, u32[]{:S(2)}) async-start(f32[256,1,128]{2,1,0:T(1,128)} %broadcast_in_dim.11), calls=%async_computation | async-start | bytes 262144 | tf_op jit(solution)/shard_map/all_to_all | solution.py:418
  52.7 13.0 %copy-start.9 = (f32[32,3072]{1,0:T(8,128)}, f32[32,3072]{1,0:T(8,128)S(1)}, u32[]{:S(2)}) copy-start(f32[32,3072]{1,0:T(8,128)S(1)} %collective-permute-done.4.xo_ref) | copy-start | bytes 1179652
  52.8 12.9 %copy-start.10 = (f32[32,3072]{1,0:T(8,128)}, f32[32,3072]{1,0:T(8,128)S(1)}, u32[]{:S(2)}) copy-start(f32[32,3072]{1,0:T(8,128)S(1)} %collective-permute-done.6.po_ref) | copy-start | bytes 1179652
  65.6 0.7 copy-start.3
  65.6 1.0 copy-start.6
  65.7 1.2 copy-start.7
  66.9 43.7 %copy-start.2 = (f32[192,64]{0,1:T(8,128)S(1)}, f32[192,64]{0,1:T(8,128)}, u32[]{:S(2)}) copy-start(f32[192,64]{0,1:T(8,128)} %param.9) | copy-start | bytes 147460
  103.6 17.0 %all-to-all-start.3 = ((f32[32,24,128]{2,1,0:T(8,128)}), f32[32,24,128]{2,1,0:T(8,128)S(1)}, u32[]{:S(2)}, u32[]{:S(2)}) async-start(f32[32,24,128]{2,1,0:T(8,128)} %broadcast_in_dim.13), calls=%async_computation.3 | async-start | bytes 786432 | tf_op jit(solution)/shard_map/all_to_all | solution.py:52
  120.5 0.7 copy-start

commit v5 on v4

--- a/solution.py
+++ b/solution.py
@@ -24,8 +24,13 @@
     return high, (v - high.astype(F32)).astype(BF16)
 
 
-def ring(devices, step):
-    return [(i, (i + step) % devices) for i in range(devices)]
+def swaps(devices, first):
+    return [pair for i in range(first, devices, 2) for pair in ((i, (i + 1) % devices), ((i + 1) % devices, i))]
+
+
+def from_neighbours(x):
+    devices = lax.axis_size("rows")
+    return [lax.ppermute(x, "rows", swaps(devices, first)) for first in (1, 0)]
 
 
 def row_of(z, x, y):
@@ -157,8 +162,8 @@
     return jnp.concatenate([turned[place] for place in places], axis=0)
 
 
-def turn_all(turned, refs, count):
-    for part, v_ref in enumerate(refs):
+def turn_all(turned, odd, refs, count):
+    for part, v_ref in zip((2 * odd, 1, 2 - 2 * odd), refs):
 
         @pl.loop(0, count, unroll=UNROLL)
         def _(j):
@@ -171,11 +176,11 @@
 
 
 def first_kernel(
-    info, pat, a_hbm, x_ref, xs_ref, before_ref, after_ref, p_ref, s_ref, y_ref, scaled_ref, sums_ref, split_ref, turned, arrived
+    info, pat, a_hbm, x_ref, xs_ref, across_odd_ref, across_even_ref, p_ref, s_ref, y_ref, scaled_ref, sums_ref, split_ref, turned, arrived
 ):
     count = s_ref.shape[0]
     copies = loads(a_hbm, split_ref, arrived)
-    turn_all(turned, (before_ref, xs_ref, after_ref), count)
+    turn_all(turned, info[3], (across_odd_ref, xs_ref, across_even_ref), count)
     xy = jnp.zeros((32, BLK), F32)
     xx = jnp.zeros((32, BLK), F32)
     for i in range(count):
@@ -195,7 +200,7 @@
     sums_ref[...] = jnp.sum(stack.T, axis=0, keepdims=True)
 
 
-def first_image(info, pattern, split, x, xs, before, after, p, s):
+def first_image(info, pattern, split, x, xs, across_odd, across_even, p, s):
     n = s.shape[0]
     return pl.pallas_call(
         first_kernel,
@@ -213,11 +218,11 @@
         compiler_params=pltpu.CompilerParams(vmem_limit_bytes=VMEM_LIMIT),
         cost_estimate=pl.CostEstimate(flops=4 * 10**9, bytes_accessed=11 * 10**6, transcendentals=0),
         name="first_image",
-    )(info, pattern, split, x, xs, before, after, p, s)
+    )(info, pattern, split, x, xs, across_odd, across_even, p, s)
 
 
 def second_kernel(
-    info, pat, a_hbm, sums_ref, scaled_ref, before_ref, after_ref, s_ref, x_ref, y_ref, p_ref, xo_ref, yo_ref, po_ref,
+    info, pat, a_hbm, sums_ref, scaled_ref, across_odd_ref, across_even_ref, s_ref, x_ref, y_ref, p_ref, xo_ref, yo_ref, po_ref,
     high_ref, low_ref, out_ref, split_ref, turned, quotients, left_ref, acc, arrived,
 ):
     count = s_ref.shape[0]
@@ -232,7 +237,7 @@
     quotients[32:64] = column[64:96] / column[96:128]
     q_own = quotients[pl.ds(own, 32), :]
     q_other = quotients[pl.ds(other, 32), :]
-    turn_all(turned, (before_ref, scaled_ref, after_ref), count)
+    turn_all(turned, info[3], (across_odd_ref, scaled_ref, across_even_ref), count)
     for i in range(count):
         lanes = slice(i * BLK, (i + 1) * BLK)
         place = slice(i % CHUNK * BLK, (i % CHUNK + 1) * BLK)
@@ -268,7 +273,7 @@
     out_ref[192:384, :] = jnp.concatenate([total[:, BLK:192], jnp.zeros((192, 64), F32)], axis=1)
 
 
-def second_image(info, pattern, split, sums, scaled, before, after, s, x, y, p, xo, yo, po):
+def second_image(info, pattern, split, sums, scaled, across_odd, across_even, s, x, y, p, xo, yo, po):
     n = s.shape[0]
     return pl.pallas_call(
         second_kernel,
@@ -285,7 +290,7 @@
         compiler_params=pltpu.CompilerParams(vmem_limit_bytes=VMEM_LIMIT),
         cost_estimate=pl.CostEstimate(flops=8 * 10**9, bytes_accessed=18 * 10**6, transcendentals=0),
         name="second_image",
-    )(info, pattern, split, sums, scaled, before, after, s, x, y, p, xo, yo, po)
+    )(info, pattern, split, sums, scaled, across_odd, across_even, s, x, y, p, xo, yo, po)
 
 
 def picked_row(groups, at):
@@ -398,26 +403,23 @@
     nodes = rows_dev * devices
     local_blocks = affinity.shape[0]
     all_blocks = local_blocks * devices
-    first_block = (lax.axis_index("rows") - 1) * local_blocks
-    info = jnp.stack([core, first_block, jnp.int32(all_blocks)]).astype(jnp.int32)
-    up, down = ring(devices, 1), ring(devices, -1)
-
+    place = lax.axis_index("rows")
+    first_block = (place - 1) * local_blocks
+    info = jnp.stack([core, first_block, jnp.int32(all_blocks), place % 2]).astype(jnp.int32)
     scale, xs = degrees(affinity, vectors)
-    xs_before = lax.ppermute(xs, "rows", up)
-    xs_after = lax.ppermute(xs, "rows", down)
+    xs_odd, xs_even = from_neighbours(xs)
     split = split_affinity(affinity, scale)
     x_other = other_core(vectors)
     p_other = other_core(directions)
-    y, scaled, sums = first_image(info, pattern, split, vectors, xs, xs_before, xs_after, directions, scale)
-    scaled_before = lax.ppermute(scaled, "rows", up)
-    scaled_after = lax.ppermute(scaled, "rows", down)
+    y, scaled, sums = first_image(info, pattern, split, vectors, xs, xs_odd, xs_even, directions, scale)
+    scaled_odd, scaled_even = from_neighbours(scaled)
     y_other = other_core(y)
     half = sums[:, 0:64]
     blank = jnp.zeros_like(half)
     row = jnp.where(core == 0, jnp.concatenate([half, blank], axis=1), jnp.concatenate([blank, half], axis=1))
     sums = lax.all_to_all(repeated(row, 2 * devices), ("rows", "cols"), 0, 0).reshape(2 * devices, BLK)
     high, low, part = second_image(
-        info, pattern, split, sums, scaled, scaled_before, scaled_after, scale, vectors, y, directions, x_other, y_other, p_other
+        info, pattern, split, sums, scaled, scaled_odd, scaled_even, scale, vectors, y, directions, x_other, y_other, p_other
     )
     both = sum_large(part.reshape(16, 24, BLK)).reshape(768, BLK)
     mine = lambda m: lax.dynamic_slice_in_dim(m, core * width, width, 1)

time: 134 us -> 133 us (level)
  transfers between devices with their start and end apart: 9 -> 9, of which waited for: 2 -> 3; matrix products, arithmetic and copies ran while one was open for 3% -> 3% of each run, Pallas kernels for 6% -> 6%
where the time goes in v5:
time: 133 us
  Pallas kernels  44.2 us (33%)
  starting transfers between devices  32.8 us (25%)
  blocking collectives  24.9 us (19%)
  waiting for transfers between devices  22.6 us (17%)
  local copies, waits for them, and re-layouts  5.13 us (4%)
  other arithmetic  2.13 us (2%)
    all_to_all x2, blocking collectives, exchange(): return lax.all_to_all(x, 'rows', 0, 0, axis_index_groups=groups)  24.9 us
    ppermute x4, starting transfers between devices, from_neighbours(): return [lax.ppermute(x, 'rows', swaps(devices, first)) for first in (1, 0)]  17.6 us
    all_to_all x1, waiting for transfers between devices, local(): lax.all_to_all(repeated(row, 2 * devices), ('rows', 'cols'), 0, 0)  12.8 us
    pallas_call x1, Pallas kernels, final(): pl.pallas_call(functools.partial(final_kernel, factor=factor), in_specs=m...  11.9 us
    pallas_call x1, Pallas kernels, second_image(): pl.pallas_call(second_kernel, in_specs=memory(pltpu.SMEM, pltpu.SMEM, pl....  10.9 us
    all_to_all x1, waiting for transfers between devices, exchange_cores(): lax.all_to_all(x, ('rows', 'cols'), 0, 0, axis_index_groups=with_cores(gr...  9.21 us
    pallas_call x1, Pallas kernels, split_affinity(): pl.pallas_call(split_kernel, in_specs=memory(pl.ANY, pl.ANY), out_specs=p...  7.88 us
    pallas_call x1, Pallas kernels, first_image(): pl.pallas_call(first_kernel, in_specs=memory(pltpu.SMEM, pltpu.SMEM, pl.A...  7.64 us
  transfers between devices with their start and end apart: 9, of which 3 were waited for; matrix products, arithmetic and copies ran while one was open for 3% of the time, Pallas kernels for 6%

profile of v5, /device:TPU:1, one launch (start us, length us, event | category | flops | bytes accessed | tf_op | source)
XLA Modules:
  0.0 132.7 jit_solution(15426285671747186178)
XLA Ops:
  0.6 5.8 %degrees.1 = (f32[24,128]{1,0:T(8,128)}, f32[32,3072]{1,0:T(8,128)}) custom-call(f32[24,6,128,128]{3,2,1,0:T(8,128)} %a_hbm.3, f32[32,3072]{1,0:T(8,128)} %x_ref.5), custom_call_target="tpu_custom_call" | custom-call | flops 10000000 | bytes 10000000 | tf_op jit(solution)/shard_map/degrees/pallas_call | solution.py:102
  6.5 11.1 %collective-permute-start = (f32[32,3072]{1,0:T(8,128)}, f32[32,3072]{1,0:T(8,128)S(1)}, u32[]{:S(2)}, u32[]{:S(2)}) collective-permute-start(f32[32,3072]{1,0:T(8,128)} %get-tuple-element.12.xs_ref), channel_id=1, source_target_pairs={{2,4},{4,2},{6,8},{8,6},{10,12},{12,10},{14,16},{16,14},{18,20},{2... | collective-permute-start | bytes 1179656 | tf_op jit(solution)/shard_map/ppermute | solution.py:33
  17.6 0.7 copy.13.pat
  18.3 7.9 %split.1.a_hbm = bf16[24,256,768]{2,1,0:T(8,128)(2,1)} custom-call(f32[24,6,128,128]{3,2,1,0:T(8,128)} %a_hbm.3, f32[24,128]{1,0:T(8,128)} %get-tuple-element.11.scale_hbm.s_ref), custom_call_target="tpu_custom_call" | custom-call | flops 10000000 | bytes 19000000 | tf_op jit(solution)/shard_map/split/pallas_call | solution.py:133
  26.2 0.0 copy-start.1
  26.2 0.0 copy-start.5
  26.2 0.7 pad_add_fusion.info
  26.9 0.6 collective-permute-done.1.across_even_ref
  27.5 0.1 copy-done.9
  27.6 0.8 copy-done.10
  28.4 7.6 %first_image.1 = (f32[32,3072]{1,0:T(8,128)}, f32[64,3072]{1,0:T(8,128)}, f32[1,128]{1,0:T(1,128)}) custom-call(s32[4]{0:T(128)} %pad_add_fusion.info, s32[24,6]{1,0:T(8,128)} %copy.13.pat, bf16[24,256,768]{2,1,0:T(8,128)(2,1)} %split.1.a_hbm, f32[32,3072]{1,0:T(8,128)} %x_ref.5, f32[32,3072]{1,0:T(8,128)} %get-tuple-element.12.xs_ref, ...), custom_call_target="tpu_custom_call" | custom-call | flops 4000000000 | bytes 11000000 | tf_op jit(solution)/shard_map/first_image/pallas_call | solution.py:205
  36.0 6.4 %collective-permute-start.2 = (f32[64,3072]{1,0:T(8,128)}, f32[64,3072]{1,0:T(8,128)S(1)}, u32[]{:S(2)}, u32[]{:S(2)}) collective-permute-start(f32[64,3072]{1,0:T(8,128)} %get-tuple-element.14.scaled_ref), channel_id=1, source_target_pairs={{2,4},{4,2},{6,8},{8,6},{10,12},{12,10},{14,16},{16,14},{18,20},{2... | collective-permute-start | bytes 2359304 | tf_op jit(solution)/shard_map/ppermute | solution.py:33
  42.5 1.8 %collective-permute-start.4 = (f32[32,3072]{1,0:T(8,128)S(1)}, f32[32,3072]{1,0:T(8,128)S(1)}, u32[]{:S(2)}, u32[]{:S(2)}) collective-permute-start(f32[32,3072]{1,0:T(8,128)S(1)} %copy-done.1), channel_id=1, source_target_pairs={{0,1},{1,0},{2,3},{3,2},{4,5},{5,4},{6,7},{7,6},{8,9},{9,8},{10,11... | collective-permute-start | bytes 1179656 | tf_op jit(solution)/shard_map/ppermute | solution.py:395
  44.3 0.1 collective-permute-start.6
  44.4 0.4 collective-permute-start.5
  44.8 0.8 fusion.2
  45.6 0.7 broadcast_in_dim.11
  46.4 5.3 %all-to-all-start = ((f32[256,1,128]{2,1,0:T(1,128)}), f32[256,1,128]{2,1,0:T(1,128)S(1)}, u32[]{:S(2)}, u32[]{:S(2)}) async-start(f32[256,1,128]{2,1,0:T(1,128)} %broadcast_in_dim.11), calls=%async_computation | async-start | bytes 262144 | tf_op jit(solution)/shard_map/all_to_all | solution.py:420
  51.7 12.8 %all-to-all-done = f32[256,1,128]{2,1,0:T(1,128)S(1)} async-done(((f32[256,1,128]{2,1,0:T(1,128)}), f32[256,1,128]{2,1,0:T(1,128)S(1)}, u32[]{:S(2)}, u32[]{:S(2)}) %all-to-all-start) | async-done | bytes 131104 | tf_op jit(solution)/shard_map/all_to_all | solution.py:420
  64.6 0.6 copy-done.3
  65.2 0.3 copy-done.6
  65.5 0.2 copy-done.7
  65.7 10.9 %second_image.1 = (bf16[192,3072]{1,0:T(8,128)(2,1)}, bf16[192,3072]{1,0:T(8,128)(2,1)}, f32[384,128]{1,0:T(8,128)}) custom-call(s32[4]{0:T(128)} %pad_add_fusion.info, s32[24,6]{1,0:T(8,128)} %copy.13.pat, bf16[24,256,768]{2,1,0:T(8,128)(2,1)} %split.1.a_hbm, f32[256,128]{1,0:T(8,128)} %bitcast.13, f32[64,3072]{1,0:T(8,128)} %get-tuple-element.14.scaled_ref, ...), custom_call_target="tpu_custom_call" | custom-call | flops 8000000000 | bytes 18000000 | tf_op jit(solution)/shard_map/second_image/pallas_call | solution.py:278
  76.7 10.4 %all_to_all.20 = f32[16,24,128]{2,1,0:T(8,128)S(1)} all-to-all(f32[16,24,128]{2,1,0:T(8,128)} %bitcast.12), channel_id=1, replica_groups={{0,2,4,6,8,10,12,14,16,18,20,22,24,26,28,30},{32,34,36,38,40,42,44,46,4..., dimensions={0} | all-to-all | bytes 393216 | tf_op jit(solution)/shard_map/all_to_all | solution.py:53
  87.2 14.5 %all_to_all.21 = f32[8,24,128]{2,1,0:T(8,128)S(1)} all-to-all(f32[8,24,128]{2,1,0:T(8,128)S(1)} %broadcast_in_dim.12), channel_id=1, replica_groups={{0,32,64,96,128,160,192,224},{2,34,66,98,130,162,194,226},{4,36,68,100,..., dimensions={0} | all-to-all | bytes 196608 | tf_op jit(solution)/shard_map/all_to_all | solution.py:53
  101.6 0.8 broadcast_in_dim.13
  102.4 7.6 %all-to-all-start.3 = ((f32[32,24,128]{2,1,0:T(8,128)}), f32[32,24,128]{2,1,0:T(8,128)S(1)}, u32[]{:S(2)}, u32[]{:S(2)}) async-start(f32[32,24,128]{2,1,0:T(8,128)} %broadcast_in_dim.13), calls=%async_computation.3 | async-start | bytes 786432 | tf_op jit(solution)/shard_map/all_to_all | solution.py:57
  110.1 0.1 pad.5.clone
  110.1 0.6 maximum_bitcast_fusion.chosen_ref
  110.8 9.2 %all-to-all-done.3 = f32[32,24,128]{2,1,0:T(8,128)S(1)} async-done(((f32[32,24,128]{2,1,0:T(8,128)}), f32[32,24,128]{2,1,0:T(8,128)S(1)}, u32[]{:S(2)}, u32[]{:S(2)}) %all-to-all-start.3) | async-done | bytes 393248 | tf_op jit(solution)/shard_map/all_to_all | solution.py:57
  120.0 0.7 copy-done
  120.7 11.9 %final.1 = (f32[32,3072]{1,0:T(8,128)}, f32[32,3072]{1,0:T(8,128)}, f32[192,192]{1,0:T(8,128)}) custom-call(f32[768,128]{1,0:T(8,128)} %bitcast.11, f32[64,192]{1,0:T(8,128)} %maximum_bitcast_fusion.chosen_ref, bf16[192,3072]{1,0:T(8,128)(2,1)} %get-tuple-element.17.high_ref, bf16[192,3072]{1,0:T(8,128)(2,1)} %get-tuple-element.18.low_ref), custom_call_target="tpu_custom_call" | custom-call | flops 400000000 | bytes 4000000 | tf_op jit(solution)/shard_map/final/pallas_call | solution.py:383
  (32 shorter events, 0.1 us)
Async XLA Ops:
  0.6 17.0 %copy-start.4 = (s32[24,6]{0,1:T(8,128)S(1)}, s32[24,6]{0,1:T(8,128)}, u32[]{:S(2)}) copy-start(s32[24,6]{0,1:T(8,128)} %param.8) | copy-start | bytes 1732
  6.5 20.4 %collective-permute-start = (f32[32,3072]{1,0:T(8,128)}, f32[32,3072]{1,0:T(8,128)S(1)}, u32[]{:S(2)}, u32[]{:S(2)}) collective-permute-start(f32[32,3072]{1,0:T(8,128)} %get-tuple-element.12.xs_ref), channel_id=1, source_target_pairs={{2,4},{4,2},{6,8},{8,6},{10,12},{12,10},{14,16},{16,14},{18,20},{2... | collective-permute-start | bytes 1179656 | tf_op jit(solution)/shard_map/ppermute | solution.py:33
  17.6 9.9 %collective-permute-start.1 = (f32[32,3072]{1,0:T(8,128)}, f32[32,3072]{1,0:T(8,128)S(1)}, u32[]{:S(2)}, u32[]{:S(2)}) collective-permute-start(f32[32,3072]{1,0:T(8,128)} %get-tuple-element.12.xs_ref), channel_id=1, source_target_pairs={{0,2},{2,0},{4,6},{6,4},{8,10},{10,8},{12,14},{14,12},{16,18},{18,... | collective-permute-start | bytes 1179656 | tf_op jit(solution)/shard_map/ppermute | solution.py:33
  26.2 16.3 %copy-start.1 = (f32[32,3072]{1,0:T(8,128)S(1)}, f32[32,3072]{1,0:T(8,128)}, u32[]{:S(2)}) copy-start(f32[32,3072]{1,0:T(8,128)} %x_ref.5) | copy-start | bytes 1179652
  26.2 18.1 %copy-start.8 = (f32[32,3072]{1,0:T(8,128)S(1)}, f32[32,3072]{1,0:T(8,128)}, u32[]{:S(2)}) copy-start(f32[32,3072]{1,0:T(8,128)} %p_ref.3) | copy-start | bytes 1179652
  26.2 18.6 %copy-start.5 = (pred[1,128]{1,0:T(4,128)(4,1)S(1)}, pred[1,128]{1,0:T(4,128)(4,1)}, u32[]{:S(2)}) copy-start(pred[1,128]{1,0:T(4,128)(4,1)} %constant.36.clone.1) | copy-start | bytes 388
  26.9 0.7 copy-start.9
  27.6 0.8 copy-start.10
  36.0 28.5 %collective-permute-start.2 = (f32[64,3072]{1,0:T(8,128)}, f32[64,3072]{1,0:T(8,128)S(1)}, u32[]{:S(2)}, u32[]{:S(2)}) collective-permute-start(f32[64,3072]{1,0:T(8,128)} %get-tuple-element.14.scaled_ref), channel_id=1, source_target_pairs={{2,4},{4,2},{6,8},{8,6},{10,12},{12,10},{14,16},{16,14},{18,20},{2... | collective-permute-start | bytes 2359304 | tf_op jit(solution)/shard_map/ppermute | solution.py:33
  42.5 22.1 %collective-permute-start.3 = (f32[64,3072]{1,0:T(8,128)}, f32[64,3072]{1,0:T(8,128)S(1)}, u32[]{:S(2)}, u32[]{:S(2)}) collective-permute-start(f32[64,3072]{1,0:T(8,128)} %get-tuple-element.14.scaled_ref), channel_id=1, source_target_pairs={{0,2},{2,0},{4,6},{6,4},{8,10},{10,8},{12,14},{14,12},{16,18},{18,... | collective-permute-start | bytes 2359304 | tf_op jit(solution)/shard_map/ppermute | solution.py:33
  42.5 9.2 %collective-permute-start.4 = (f32[32,3072]{1,0:T(8,128)S(1)}, f32[32,3072]{1,0:T(8,128)S(1)}, u32[]{:S(2)}, u32[]{:S(2)}) collective-permute-start(f32[32,3072]{1,0:T(8,128)S(1)} %copy-done.1), channel_id=1, source_target_pairs={{0,1},{1,0},{2,3},{3,2},{4,5},{5,4},{6,7},{7,6},{8,9},{9,8},{10,11... | collective-permute-start | bytes 1179656 | tf_op jit(solution)/shard_map/ppermute | solution.py:395
  44.3 7.4 %collective-permute-start.6 = (f32[32,3072]{1,0:T(8,128)S(1)}, f32[32,3072]{1,0:T(8,128)S(1)}, u32[]{:S(2)}, u32[]{:S(2)}) collective-permute-start(f32[32,3072]{1,0:T(8,128)S(1)} %copy-done.8), channel_id=1, source_target_pairs={{0,1},{1,0},{2,3},{3,2},{4,5},{5,4},{6,7},{7,6},{8,9},{9,8},{10,11... | collective-permute-start | bytes 1179656 | tf_op jit(solution)/shard_map/ppermute | solution.py:395
  44.4 20.1 %collective-permute-start.5 = (f32[32,3072]{1,0:T(8,128)}, f32[32,3072]{1,0:T(8,128)}, u32[]{:S(2)}, u32[]{:S(2)}) collective-permute-start(f32[32,3072]{1,0:T(8,128)} %get-tuple-element.15.y_ref), channel_id=1, source_target_pairs={{0,1},{1,0},{2,3},{3,2},{4,5},{5,4},{6,7},{7,6},{8,9},{9,8},{10,11... | collective-permute-start | bytes 1179656 | tf_op jit(solution)/shard_map/ppermute | solution.py:395
  46.4 18.2 %all-to-all-start = ((f32[256,1,128]{2,1,0:T(1,128)}), f32[256,1,128]{2,1,0:T(1,128)S(1)}, u32[]{:S(2)}, u32[]{:S(2)}) async-start(f32[256,1,128]{2,1,0:T(1,128)} %broadcast_in_dim.11), calls=%async_computation | async-start | bytes 262144 | tf_op jit(solution)/shard_map/all_to_all | solution.py:420
  51.7 12.9 %copy-start.11 = (f32[32,3072]{1,0:T(8,128)}, f32[32,3072]{1,0:T(8,128)S(1)}, u32[]{:S(2)}) copy-start(f32[32,3072]{1,0:T(8,128)S(1)} %collective-permute-done.4.xo_ref) | copy-start | bytes 1179652
  51.7 12.9 %copy-start.12 = (f32[32,3072]{1,0:T(8,128)}, f32[32,3072]{1,0:T(8,128)S(1)}, u32[]{:S(2)}) copy-start(f32[32,3072]{1,0:T(8,128)S(1)} %collective-permute-done.6.po_ref) | copy-start | bytes 1179652
  64.5 0.7 copy-start.3
  64.5 1.0 copy-start.6
  64.6 1.2 copy-start.7
  65.7 44.3 %copy-start.2 = (f32[192,64]{0,1:T(8,128)S(1)}, f32[192,64]{0,1:T(8,128)}, u32[]{:S(2)}) copy-start(f32[192,64]{0,1:T(8,128)} %param.9) | copy-start | bytes 147460
  102.4 17.6 %all-to-all-start.3 = ((f32[32,24,128]{2,1,0:T(8,128)}), f32[32,24,128]{2,1,0:T(8,128)S(1)}, u32[]{:S(2)}, u32[]{:S(2)}) async-start(f32[32,24,128]{2,1,0:T(8,128)} %broadcast_in_dim.13), calls=%async_computation.3 | async-start | bytes 786432 | tf_op jit(solution)/shard_map/all_to_all | solution.py:57
  120.0 0.7 copy-start

commit v6 on v5

--- a/solution.py
+++ b/solution.py
@@ -13,7 +13,7 @@
 BF16 = jnp.bfloat16
 UNROLL = 24
 GROUP = 6
-CHUNK = 8
+CHUNK = 4
 VMEM_LIMIT = 60 * 2**20
 PIVOTS = 16
 EXACT = lax.Precision.HIGHEST
@@ -110,10 +110,13 @@
     )(affinity, x)
 
 
-def split_kernel(a_hbm, scale_hbm, split_hbm, a_ref, split_ref, arrived, sent):
+def split_kernel(a_hbm, scale_ref, p_ref, split_hbm, ps_ref, a_ref, split_ref, arrived, sent):
     count = a_ref.shape[0]
     copies = loads(a_hbm, a_ref, arrived)
     sends = [pltpu.make_async_copy(split_ref.at[i], split_hbm.at[i], sent.at[i]) for i in range(count)]
+    for i in range(count):
+        lanes = slice(i * BLK, (i + 1) * BLK)
+        ps_ref[:, lanes] = p_ref[:, lanes] * scale_ref[i : i + 1, :]
     for i in range(count):
         wait_group(copies, i)
         for k in range(6):
@@ -127,14 +130,14 @@
         copy.wait()
 
 
-def split_affinity(affinity, scale):
+def split_affinity(affinity, scale, p):
     n = affinity.shape[0]
     split = (n, 2 * BLK, 6 * BLK)
     return pl.pallas_call(
         split_kernel,
-        in_specs=memory(pl.ANY, pl.ANY),
-        out_specs=pl.BlockSpec(memory_space=pl.ANY),
-        out_shape=jax.ShapeDtypeStruct(split, BF16),
+        in_specs=memory(pl.ANY, pltpu.VMEM, pltpu.VMEM),
+        out_specs=memory(pl.ANY, pltpu.VMEM),
+        out_shape=[jax.ShapeDtypeStruct(split, BF16), jax.ShapeDtypeStruct(p.shape, F32)],
         scratch_shapes=[
             pltpu.VMEM((n, 6, BLK, BLK), F32),
             pltpu.VMEM(split, BF16),
@@ -144,7 +147,7 @@
         compiler_params=pltpu.CompilerParams(vmem_limit_bytes=VMEM_LIMIT),
         cost_estimate=pl.CostEstimate(flops=10**7, bytes_accessed=19 * 10**6, transcendentals=0),
         name="split",
-    )(affinity, scale)
+    )(affinity, scale, p)
 
 
 def block_of(ref, i):
@@ -162,25 +165,27 @@
     return jnp.concatenate([turned[place] for place in places], axis=0)
 
 
-def turn_all(turned, odd, refs, count):
-    for part, v_ref in zip((2 * odd, 1, 2 - 2 * odd), refs):
+def turn_all(turned, odd, triples, count):
+    for part, refs in zip((2 * odd, 1, 2 - 2 * odd), triples):
 
         @pl.loop(0, count, unroll=UNROLL)
         def _(j):
-            v = block_of(v_ref, j)
-            high = v.astype(BF16).astype(F32)
-            stack = [high, v - high]
-            if v.shape[0] == 32:
+            stack = []
+            for v_ref in refs:
+                v = block_of(v_ref, j)
+                high = v.astype(BF16).astype(F32)
+                stack += [high, v - high]
+            if len(refs) == 1:
                 stack.append(jnp.zeros((64, BLK), F32))
             turned[part * count + j] = jnp.concatenate(stack, axis=0).T.astype(BF16)
 
 
 def first_kernel(
-    info, pat, a_hbm, x_ref, xs_ref, across_odd_ref, across_even_ref, p_ref, s_ref, y_ref, scaled_ref, sums_ref, split_ref, turned, arrived
+    info, pat, a_hbm, x_ref, xs_ref, across_odd_ref, across_even_ref, s_ref, y_ref, ys_ref, sums_ref, split_ref, turned, arrived
 ):
     count = s_ref.shape[0]
     copies = loads(a_hbm, split_ref, arrived)
-    turn_all(turned, info[3], (across_odd_ref, xs_ref, across_even_ref), count)
+    turn_all(turned, info[3], ((across_odd_ref,), (xs_ref,), (across_even_ref,)), count)
     xy = jnp.zeros((32, BLK), F32)
     xx = jnp.zeros((32, BLK), F32)
     for i in range(count):
@@ -192,22 +197,21 @@
         x, s = x_ref[:, lanes], s_ref[i : i + 1, :]
         y = x - s * (image[0:32] + image[32:64])
         y_ref[:, lanes] = y
-        scaled_ref[0:32, lanes] = s * y
-        scaled_ref[32:64, lanes] = s * p_ref[:, lanes]
+        ys_ref[:, lanes] = s * y
         xy += x * y
         xx += x * x
     stack = jnp.concatenate([xy, xx, jnp.zeros((64, BLK), F32)], axis=0)
     sums_ref[...] = jnp.sum(stack.T, axis=0, keepdims=True)
 
 
-def first_image(info, pattern, split, x, xs, across_odd, across_even, p, s):
+def first_image(info, pattern, split, x, xs, across_odd, across_even, s):
     n = s.shape[0]
     return pl.pallas_call(
         first_kernel,
-        in_specs=memory(pltpu.SMEM, pltpu.SMEM, pl.ANY, *[pltpu.VMEM] * 6),
+        in_specs=memory(pltpu.SMEM, pltpu.SMEM, pl.ANY, *[pltpu.VMEM] * 5),
         out_shape=[
             jax.ShapeDtypeStruct(x.shape, F32),
-            jax.ShapeDtypeStruct((64, x.shape[1]), F32),
+            jax.ShapeDtypeStruct(x.shape, F32),
             jax.ShapeDtypeStruct((1, BLK), F32),
         ],
         scratch_shapes=[
@@ -218,37 +222,62 @@
         compiler_params=pltpu.CompilerParams(vmem_limit_bytes=VMEM_LIMIT),
         cost_estimate=pl.CostEstimate(flops=4 * 10**9, bytes_accessed=11 * 10**6, transcendentals=0),
         name="first_image",
-    )(info, pattern, split, x, xs, across_odd, across_even, p, s)
+    )(info, pattern, split, x, xs, across_odd, across_even, s)
 
 
 def second_kernel(
-    info, pat, a_hbm, sums_ref, scaled_ref, across_odd_ref, across_even_ref, s_ref, x_ref, y_ref, p_ref, xo_ref, yo_ref, po_ref,
-    high_ref, low_ref, out_ref, split_ref, turned, quotients, left_ref, acc, arrived,
+    info, pat, a_hbm, ys_ref, ys_odd_ref, ys_even_ref, ps_ref, ps_odd_ref, ps_even_ref, s_ref, y_ref, p_ref,
+    z_ref, image_ref, split_ref, turned, arrived,
 ):
     count = s_ref.shape[0]
+    copies = loads(a_hbm, split_ref, arrived)
+    turn_all(turned, info[3], ((ys_odd_ref, ps_odd_ref), (ys_ref, ps_ref), (ys_even_ref, ps_even_ref)), count)
+    for i in range(count):
+        lanes = slice(i * BLK, (i + 1) * BLK)
+        wait_group(copies, i)
+        weights = gathered(info, pat, turned, i)
+        product = jnp.dot(split_ref[i], weights, preferred_element_type=F32)
+        image = (product[:BLK] + product[BLK:]).T
+        s = s_ref[i : i + 1, :]
+        z_ref[:, lanes] = y_ref[:, lanes] - s * (image[0:32] + image[32:64])
+        image_ref[:, lanes] = p_ref[:, lanes] - s * (image[64:96] + image[96:128])
+
+
+def second_image(info, pattern, split, ys, ys_odd, ys_even, ps, ps_odd, ps_even, s, y, p):
+    n = s.shape[0]
+    return pl.pallas_call(
+        second_kernel,
+        in_specs=memory(pltpu.SMEM, pltpu.SMEM, pl.ANY, *[pltpu.VMEM] * 9),
+        out_shape=[jax.ShapeDtypeStruct(y.shape, F32)] * 2,
+        scratch_shapes=[
+            pltpu.VMEM(split.shape, BF16),
+            pltpu.VMEM((3 * n, BLK, BLK), BF16),
+            pltpu.SemaphoreType.DMA((n,)),
+        ],
+        compiler_params=pltpu.CompilerParams(vmem_limit_bytes=VMEM_LIMIT),
+        cost_estimate=pl.CostEstimate(flops=4 * 10**9, bytes_accessed=14 * 10**6, transcendentals=0),
+        name="second_image",
+    )(info, pattern, split, ys, ys_odd, ys_even, ps, ps_odd, ps_even, s, y, p)
+
+
+def products_kernel(
+    info, sums_ref, x_ref, y_ref, p_ref, xo_ref, yo_ref, po_ref, z_ref, image_ref, high_ref, low_ref, out_ref, quotients, left_ref, acc
+):
     core = info[0]
     own = pl.multiple_of(core * 32, 32)
     other = pl.multiple_of((1 - core) * 32, 32)
-    copies = loads(a_hbm, split_ref, arrived)
-
     sums = jnp.sum(sums_ref[...], axis=0, keepdims=True)
     column = jnp.broadcast_to(sums, (BLK, BLK)).T
     quotients[0:32] = column[0:32] / column[32:64]
     quotients[32:64] = column[64:96] / column[96:128]
     q_own = quotients[pl.ds(own, 32), :]
     q_other = quotients[pl.ds(other, 32), :]
-    turn_all(turned, info[3], (across_odd_ref, scaled_ref, across_even_ref), count)
-    for i in range(count):
+    for i in range(x_ref.shape[1] // BLK):
         lanes = slice(i * BLK, (i + 1) * BLK)
         place = slice(i % CHUNK * BLK, (i % CHUNK + 1) * BLK)
-        wait_group(copies, i)
-        weights = gathered(info, pat, turned, i)
-        product = jnp.dot(split_ref[i], weights, preferred_element_type=F32)
-        image = (product[:BLK] + product[BLK:]).T
-        x, y, p, s = x_ref[:, lanes], y_ref[:, lanes], p_ref[:, lanes], s_ref[i : i + 1, :]
-        z = y - s * (image[0:32] + image[64:96])
-        p_image = p - s * (image[32:64] + image[96:128])
-        for at, v in enumerate((y - q_own * x, x, p, z - q_own * y, y, p_image)):
+        x, y = x_ref[:, lanes], y_ref[:, lanes]
+        rows = (y - q_own * x, x, p_ref[:, lanes], z_ref[:, lanes] - q_own * y, y, image_ref[:, lanes])
+        for at, v in enumerate(rows):
             high, low = halves(v)
             left_ref[32 * at : 32 * at + 32, place] = high
             left_ref[192 + 32 * at : 224 + 32 * at, place] = low
@@ -273,24 +302,20 @@
     out_ref[192:384, :] = jnp.concatenate([total[:, BLK:192], jnp.zeros((192, 64), F32)], axis=1)
 
 
-def second_image(info, pattern, split, sums, scaled, across_odd, across_even, s, x, y, p, xo, yo, po):
-    n = s.shape[0]
-    return pl.pallas_call(
-        second_kernel,
-        in_specs=memory(pltpu.SMEM, pltpu.SMEM, pl.ANY, *[pltpu.VMEM] * 11),
+def products(info, sums, x, y, p, xo, yo, po, z, image):
+    return pl.pallas_call(
+        products_kernel,
+        in_specs=memory(pltpu.SMEM, *[pltpu.VMEM] * 9),
         out_shape=[jax.ShapeDtypeStruct((192, x.shape[1]), BF16)] * 2 + [jax.ShapeDtypeStruct((384, BLK), F32)],
         scratch_shapes=[
-            pltpu.VMEM(split.shape, BF16),
-            pltpu.VMEM((3 * n, BLK, BLK), BF16),
             pltpu.VMEM((64, BLK), F32),
             pltpu.VMEM((384, CHUNK * BLK), BF16),
             pltpu.VMEM((384, 192), F32),
-            pltpu.SemaphoreType.DMA((n,)),
         ],
         compiler_params=pltpu.CompilerParams(vmem_limit_bytes=VMEM_LIMIT),
-        cost_estimate=pl.CostEstimate(flops=8 * 10**9, bytes_accessed=18 * 10**6, transcendentals=0),
-        name="second_image",
-    )(info, pattern, split, sums, scaled, across_odd, across_even, s, x, y, p, xo, yo, po)
+        cost_estimate=pl.CostEstimate(flops=2 * 10**9, bytes_accessed=6 * 10**6, transcendentals=0),
+        name="products",
+    )(info, sums, x, y, p, xo, yo, po, z, image)
 
 
 def picked_row(groups, at):
@@ -408,19 +433,19 @@
     info = jnp.stack([core, first_block, jnp.int32(all_blocks), place % 2]).astype(jnp.int32)
     scale, xs = degrees(affinity, vectors)
     xs_odd, xs_even = from_neighbours(xs)
-    split = split_affinity(affinity, scale)
+    split, ps = split_affinity(affinity, scale, directions)
+    ps_odd, ps_even = from_neighbours(ps)
     x_other = other_core(vectors)
     p_other = other_core(directions)
-    y, scaled, sums = first_image(info, pattern, split, vectors, xs, xs_odd, xs_even, directions, scale)
-    scaled_odd, scaled_even = from_neighbours(scaled)
+    y, ys, sums = first_image(info, pattern, split, vectors, xs, xs_odd, xs_even, scale)
+    ys_odd, ys_even = from_neighbours(ys)
     y_other = other_core(y)
     half = sums[:, 0:64]
     blank = jnp.zeros_like(half)
     row = jnp.where(core == 0, jnp.concatenate([half, blank], axis=1), jnp.concatenate([blank, half], axis=1))
     sums = lax.all_to_all(repeated(row, 2 * devices), ("rows", "cols"), 0, 0).reshape(2 * devices, BLK)
-    high, low, part = second_image(
-        info, pattern, split, sums, scaled, scaled_odd, scaled_even, scale, vectors, y, directions, x_other, y_other, p_other
-    )
+    z, image = second_image(info, pattern, split, ys, ys_odd, ys_even, ps, ps_odd, ps_even, scale, y, directions)
+    high, low, part = products(info, sums, vectors, y, directions, x_other, y_other, p_other, z, image)
     both = sum_large(part.reshape(16, 24, BLK)).reshape(768, BLK)
     mine = lambda m: lax.dynamic_slice_in_dim(m, core * width, width, 1)
     kept = jnp.concatenate([rotation[:total], jnp.zeros((total, total), F32), rotation[2 * total :]], axis=0)

time: 133 us -> 127 us (0.955)
  waiting for transfers between devices: 22.6 us -> 13.1 us
  Pallas kernels: 44.2 us -> 47.8 us
    all_to_all x1, waiting for transfers between devices: 12.8 us -> 4.15 us  [local(): lax.all_to_all(repeated(row, 2 * devices), ('rows', 'cols'), 0, 0)]
    pallas_call x1 -> x2, Pallas kernels: 7.88 us -> 14.7 us  [the longest x1 9.65 us: split_affinity(): pl.pallas_call(split_kernel, in_specs=memory(pl.ANY, pltpu.VMEM, pltpu.VM...]
    pallas_call x1, Pallas kernels: 10.9 us -> 7.95 us  [second_image(): pl.pallas_call(second_kernel, in_specs=memory(pltpu.SMEM, pltpu.SMEM, pl....]
    ppermute x4 -> x6, starting transfers between devices: 17.6 us -> 18.2 us  [from_neighbours(): return [lax.ppermute(x, 'rows', swaps(devices, first)) for first in (1, 0)]]
    unnamed x27 -> x31, local copies, waits for them, and re-layouts: 3.55 us -> 3.86 us
  transfers between devices with their start and end apart: 9 -> 11, of which waited for: 3 -> 2; matrix products, arithmetic and copies ran while one was open for 3% -> 3% of each run, Pallas kernels for 6% -> 20%
where the time goes in v6:
time: 127 us
  Pallas kernels  47.8 us (38%)
  starting transfers between devices  32.8 us (26%)
  blocking collectives  24.7 us (19%)
  waiting for transfers between devices  13.1 us (10%)
  local copies, waits for them, and re-layouts  5.45 us (4%)
  other arithmetic  2.03 us (2%)
    all_to_all x2, blocking collectives, exchange(): return lax.all_to_all(x, 'rows', 0, 0, axis_index_groups=groups)  24.7 us
    ppermute x6, starting transfers between devices, from_neighbours(): return [lax.ppermute(x, 'rows', swaps(devices, first)) for first in (1, 0)]  18.2 us
    pallas_call x1, Pallas kernels, final(): pl.pallas_call(functools.partial(final_kernel, factor=factor), in_specs=m...  11.9 us
    pallas_call x1, Pallas kernels, split_affinity(): pl.pallas_call(split_kernel, in_specs=memory(pl.ANY, pltpu.VMEM, pltpu.VM...  9.65 us
    all_to_all x1, waiting for transfers between devices, exchange_cores(): lax.all_to_all(x, ('rows', 'cols'), 0, 0, axis_index_groups=with_cores(gr...  8.92 us
    pallas_call x1, Pallas kernels, second_image(): pl.pallas_call(second_kernel, in_specs=memory(pltpu.SMEM, pltpu.SMEM, pl....  7.95 us
    pallas_call x1, Pallas kernels, first_image(): pl.pallas_call(first_kernel, in_specs=memory(pltpu.SMEM, pltpu.SMEM, pl.A...  7.4 us
    all_to_all x1, starting transfers between devices, exchange_cores(): lax.all_to_all(x, ('rows', 'cols'), 0, 0, axis_index_groups=with_cores(gr...  6.77 us
  transfers between devices with their start and end apart: 11, of which 2 were waited for; matrix products, arithmetic and copies ran while one was open for 3% of the time, Pallas kernels for 20%

profile of v6, /device:TPU:1, one launch (start us, length us, event | category | flops | bytes accessed | tf_op | source)
XLA Modules:
  0.0 126.8 jit_solution(7806972549993709062)
XLA Ops:
  0.6 5.8 %degrees.1 = (f32[24,128]{1,0:T(8,128)}, f32[32,3072]{1,0:T(8,128)}) custom-call(f32[24,6,128,128]{3,2,1,0:T(8,128)} %a_hbm.3, f32[32,3072]{1,0:T(8,128)} %x_ref.5), custom_call_target="tpu_custom_call" | custom-call | flops 10000000 | bytes 10000000 | tf_op jit(solution)/shard_map/degrees/pallas_call | solution.py:102
  6.5 11.1 %collective-permute-start = (f32[32,3072]{1,0:T(8,128)}, f32[32,3072]{1,0:T(8,128)S(1)}, u32[]{:S(2)}, u32[]{:S(2)}) collective-permute-start(f32[32,3072]{1,0:T(8,128)} %get-tuple-element.17.xs_ref), channel_id=1, source_target_pairs={{2,4},{4,2},{6,8},{8,6},{10,12},{12,10},{14,16},{16,14},{18,20},{2... | collective-permute-start | bytes 1179656 | tf_op jit(solution)/shard_map/ppermute | solution.py:33
  17.6 9.6 %split.1 = (bf16[24,256,768]{2,1,0:T(8,128)(2,1)}, f32[32,3072]{1,0:T(8,128)}) custom-call(f32[24,6,128,128]{3,2,1,0:T(8,128)} %a_hbm.3, f32[24,128]{1,0:T(8,128)} %get-tuple-element.15.scale_ref.s_ref, f32[32,3072]{1,0:T(8,128)} %p_ref.5), custom_call_target="tpu_custom_call" | custom-call | flops 10000000 | bytes 19000000 | tf_op jit(solution)/shard_map/split/pallas_call | solution.py:136
  27.3 0.7 collective-permute-start.7
  28.0 0.9 collective-permute-start.8
  28.9 0.7 copy.12.pat
  29.6 0.6 pad_add_fusion.info
  30.2 0.7 copy-done.9
  30.9 0.1 copy-done.10
  31.1 7.4 %first_image.1 = (f32[32,3072]{1,0:T(8,128)}, f32[32,3072]{1,0:T(8,128)}, f32[1,128]{1,0:T(1,128)}) custom-call(s32[4]{0:T(128)} %pad_add_fusion.info, s32[24,6]{1,0:T(8,128)} %copy.12.pat, bf16[24,256,768]{2,1,0:T(8,128)(2,1)} %get-tuple-element.16.a_hbm, f32[32,3072]{1,0:T(8,128)} %x_ref.5, f32[32,3072]{1,0:T(8,128)} %get-tuple-element.17.xs_ref, ...), custom_call_target="tpu_custom_call" | custom-call | flops 4000000000 | bytes 11000000 | tf_op jit(solution)/shard_map/first_image/pallas_call | solution.py:209
  38.5 5.4 %collective-permute-start.5 = (f32[32,3072]{1,0:T(8,128)}, f32[32,3072]{1,0:T(8,128)S(1)}, u32[]{:S(2)}, u32[]{:S(2)}) collective-permute-start(f32[32,3072]{1,0:T(8,128)} %get-tuple-element.20.ys_ref), channel_id=1, source_target_pairs={{2,4},{4,2},{6,8},{8,6},{10,12},{12,10},{14,16},{16,14},{18,20},{2... | collective-permute-start | bytes 1179656 | tf_op jit(solution)/shard_map/ppermute | solution.py:33
  43.9 1.5 %collective-permute-start.2 = (f32[32,3072]{1,0:T(8,128)S(1)}, f32[32,3072]{1,0:T(8,128)S(1)}, u32[]{:S(2)}, u32[]{:S(2)}) collective-permute-start(f32[32,3072]{1,0:T(8,128)S(1)} %copy-done.1), channel_id=1, source_target_pairs={{0,1},{1,0},{2,3},{3,2},{4,5},{5,4},{6,7},{7,6},{8,9},{9,8},{10,11... | collective-permute-start | bytes 1179656 | tf_op jit(solution)/shard_map/ppermute | solution.py:420
  45.5 0.1 collective-permute-start.4
  45.6 0.5 collective-permute-start.3
  46.1 0.8 fusion.2
  46.9 0.7 broadcast_in_dim.11
  47.6 5.7 %all-to-all-start = ((f32[256,1,128]{2,1,0:T(1,128)}), f32[256,1,128]{2,1,0:T(1,128)S(1)}, u32[]{:S(2)}, u32[]{:S(2)}) async-start(f32[256,1,128]{2,1,0:T(1,128)} %broadcast_in_dim.11), calls=%async_computation | async-start | bytes 262144 | tf_op jit(solution)/shard_map/all_to_all | solution.py:446
  53.4 0.7 copy-done.14
  54.1 7.9 %second_image.1 = (f32[32,3072]{1,0:T(8,128)}, f32[32,3072]{1,0:T(8,128)}) custom-call(s32[4]{0:T(128)} %pad_add_fusion.info, s32[24,6]{1,0:T(8,128)} %copy.12.pat, bf16[24,256,768]{2,1,0:T(8,128)(2,1)} %get-tuple-element.16.a_hbm, f32[32,3072]{1,0:T(8,128)} %get-tuple-element.20.ys_ref, f32[32,3072]{1,0:T(8,128)} %copy-done.14, ...), custom_call_target="tpu_custom_call" | custom-call | flops 4000000000 | bytes 14000000 | tf_op jit(solution)/shard_map/second_image/pallas_call | solution.py:248
  62.1 4.1 %all-to-all-done = f32[256,1,128]{2,1,0:T(1,128)S(1)} async-done(((f32[256,1,128]{2,1,0:T(1,128)}), f32[256,1,128]{2,1,0:T(1,128)S(1)}, u32[]{:S(2)}, u32[]{:S(2)}) %all-to-all-start) | async-done | bytes 131104 | tf_op jit(solution)/shard_map/all_to_all | solution.py:446
  66.3 0.6 copy-done.4
  66.9 0.1 copy-done.13
  67.0 5.0 %products.1 = (bf16[192,3072]{1,0:T(8,128)(2,1)}, bf16[192,3072]{1,0:T(8,128)(2,1)}, f32[384,128]{1,0:T(8,128)}) custom-call(s32[4]{0:T(128)} %pad_add_fusion.info, f32[256,128]{1,0:T(8,128)} %bitcast.13, f32[32,3072]{1,0:T(8,128)} %x_ref.5, f32[32,3072]{1,0:T(8,128)} %get-tuple-element.19.y_ref, f32[32,3072]{1,0:T(8,128)} %p_ref.5, f32[32,3072]{1,0:T(8,128)} %copy-done.11, ...), custom_call_target="tpu_custom_call" | custom-call | flops 2000000000 | bytes 6000000 | tf_op jit(solution)/shard_map/products/pallas_call | solution.py:306
  72.1 10.4 %all_to_all.20 = f32[16,24,128]{2,1,0:T(8,128)S(1)} all-to-all(f32[16,24,128]{2,1,0:T(8,128)} %bitcast.12), channel_id=1, replica_groups={{0,2,4,6,8,10,12,14,16,18,20,22,24,26,28,30},{32,34,36,38,40,42,44,46,4..., dimensions={0} | all-to-all | bytes 393216 | tf_op jit(solution)/shard_map/all_to_all | solution.py:53
  82.5 14.3 %all_to_all.21 = f32[8,24,128]{2,1,0:T(8,128)S(1)} all-to-all(f32[8,24,128]{2,1,0:T(8,128)S(1)} %broadcast_in_dim.12), channel_id=1, replica_groups={{0,32,64,96,128,160,192,224},{2,34,66,98,130,162,194,226},{4,36,68,100,..., dimensions={0} | all-to-all | bytes 196608 | tf_op jit(solution)/shard_map/all_to_all | solution.py:53
  96.9 0.8 broadcast_in_dim.13
  97.6 6.8 %all-to-all-start.3 = ((f32[32,24,128]{2,1,0:T(8,128)}), f32[32,24,128]{2,1,0:T(8,128)S(1)}, u32[]{:S(2)}, u32[]{:S(2)}) async-start(f32[32,24,128]{2,1,0:T(8,128)} %broadcast_in_dim.13), calls=%async_computation.3 | async-start | bytes 786432 | tf_op jit(solution)/shard_map/all_to_all | solution.py:57
  104.4 0.1 pad.5.clone
  104.5 0.6 maximum_bitcast_fusion.chosen_ref
  105.2 8.9 %all-to-all-done.3 = f32[32,24,128]{2,1,0:T(8,128)S(1)} async-done(((f32[32,24,128]{2,1,0:T(8,128)}), f32[32,24,128]{2,1,0:T(8,128)S(1)}, u32[]{:S(2)}, u32[]{:S(2)}) %all-to-all-start.3) | async-done | bytes 393248 | tf_op jit(solution)/shard_map/all_to_all | solution.py:57
  114.1 0.8 copy-done
  114.8 11.9 %final.1 = (f32[32,3072]{1,0:T(8,128)}, f32[32,3072]{1,0:T(8,128)}, f32[192,192]{1,0:T(8,128)}) custom-call(f32[768,128]{1,0:T(8,128)} %bitcast.11, f32[64,192]{1,0:T(8,128)} %maximum_bitcast_fusion.chosen_ref, bf16[192,3072]{1,0:T(8,128)(2,1)} %get-tuple-element.25.high_ref, bf16[192,3072]{1,0:T(8,128)(2,1)} %get-tuple-element.26.low_ref), custom_call_target="tpu_custom_call" | custom-call | flops 400000000 | bytes 4000000 | tf_op jit(solution)/shard_map/final/pallas_call | solution.py:408
  (41 shorter events, 0.2 us)
Async XLA Ops:
  0.6 28.3 %copy-start.5 = (s32[24,6]{0,1:T(8,128)S(1)}, s32[24,6]{0,1:T(8,128)}, u32[]{:S(2)}) copy-start(s32[24,6]{0,1:T(8,128)} %param.8) | copy-start | bytes 1732
  6.5 23.7 %collective-permute-start = (f32[32,3072]{1,0:T(8,128)}, f32[32,3072]{1,0:T(8,128)S(1)}, u32[]{:S(2)}, u32[]{:S(2)}) collective-permute-start(f32[32,3072]{1,0:T(8,128)} %get-tuple-element.17.xs_ref), channel_id=1, source_target_pairs={{2,4},{4,2},{6,8},{8,6},{10,12},{12,10},{14,16},{16,14},{18,20},{2... | collective-permute-start | bytes 1179656 | tf_op jit(solution)/shard_map/ppermute | solution.py:33
  17.6 12.6 %collective-permute-start.1 = (f32[32,3072]{1,0:T(8,128)}, f32[32,3072]{1,0:T(8,128)S(1)}, u32[]{:S(2)}, u32[]{:S(2)}) collective-permute-start(f32[32,3072]{1,0:T(8,128)} %get-tuple-element.17.xs_ref), channel_id=1, source_target_pairs={{0,2},{2,0},{4,6},{6,4},{8,10},{10,8},{12,14},{14,12},{16,18},{18,... | collective-permute-start | bytes 1179656 | tf_op jit(solution)/shard_map/ppermute | solution.py:33
  27.3 16.7 %copy-start.1 = (f32[32,3072]{1,0:T(8,128)S(1)}, f32[32,3072]{1,0:T(8,128)}, u32[]{:S(2)}) copy-start(f32[32,3072]{1,0:T(8,128)} %x_ref.5) | copy-start | bytes 1179652
  27.3 18.2 %copy-start.2 = (f32[32,3072]{1,0:T(8,128)S(1)}, f32[32,3072]{1,0:T(8,128)}, u32[]{:S(2)}) copy-start(f32[32,3072]{1,0:T(8,128)} %p_ref.5) | copy-start | bytes 1179652
  27.3 18.8 %copy-start.6 = (pred[1,128]{1,0:T(4,128)(4,1)S(1)}, pred[1,128]{1,0:T(4,128)(4,1)}, u32[]{:S(2)}) copy-start(pred[1,128]{1,0:T(4,128)(4,1)} %constant.36.clone.1) | copy-start | bytes 388
  27.3 18.2 %collective-permute-start.7 = (f32[32,3072]{1,0:T(8,128)}, f32[32,3072]{1,0:T(8,128)S(1)}, u32[]{:S(2)}, u32[]{:S(2)}) collective-permute-start(f32[32,3072]{1,0:T(8,128)} %get-tuple-element.21.ps_ref), channel_id=1, source_target_pairs={{2,4},{4,2},{6,8},{8,6},{10,12},{12,10},{14,16},{16,14},{18,20},{2... | collective-permute-start | bytes 1179656 | tf_op jit(solution)/shard_map/ppermute | solution.py:33
  28.0 17.6 %collective-permute-start.8 = (f32[32,3072]{1,0:T(8,128)}, f32[32,3072]{1,0:T(8,128)S(1)}, u32[]{:S(2)}, u32[]{:S(2)}) collective-permute-start(f32[32,3072]{1,0:T(8,128)} %get-tuple-element.21.ps_ref), channel_id=1, source_target_pairs={{0,2},{2,0},{4,6},{6,4},{8,10},{10,8},{12,14},{14,12},{16,18},{18,... | collective-permute-start | bytes 1179656 | tf_op jit(solution)/shard_map/ppermute | solution.py:33
  30.2 0.8 copy-start.9
  30.2 0.9 copy-start.10
  38.5 14.8 %collective-permute-start.5 = (f32[32,3072]{1,0:T(8,128)}, f32[32,3072]{1,0:T(8,128)S(1)}, u32[]{:S(2)}, u32[]{:S(2)}) collective-permute-start(f32[32,3072]{1,0:T(8,128)} %get-tuple-element.20.ys_ref), channel_id=1, source_target_pairs={{2,4},{4,2},{6,8},{8,6},{10,12},{12,10},{14,16},{16,14},{18,20},{2... | collective-permute-start | bytes 1179656 | tf_op jit(solution)/shard_map/ppermute | solution.py:33
  43.9 9.4 %collective-permute-start.6 = (f32[32,3072]{1,0:T(8,128)}, f32[32,3072]{1,0:T(8,128)}, u32[]{:S(2)}, u32[]{:S(2)}) collective-permute-start(f32[32,3072]{1,0:T(8,128)} %get-tuple-element.20.ys_ref), channel_id=1, source_target_pairs={{0,2},{2,0},{4,6},{6,4},{8,10},{10,8},{12,14},{14,12},{16,18},{18,... | collective-permute-start | bytes 1179656 | tf_op jit(solution)/shard_map/ppermute | solution.py:33
  43.9 18.1 %collective-permute-start.2 = (f32[32,3072]{1,0:T(8,128)S(1)}, f32[32,3072]{1,0:T(8,128)S(1)}, u32[]{:S(2)}, u32[]{:S(2)}) collective-permute-start(f32[32,3072]{1,0:T(8,128)S(1)} %copy-done.1), channel_id=1, source_target_pairs={{0,1},{1,0},{2,3},{3,2},{4,5},{5,4},{6,7},{7,6},{8,9},{9,8},{10,11... | collective-permute-start | bytes 1179656 | tf_op jit(solution)/shard_map/ppermute | solution.py:420
  45.4 7.9 %copy-start.7 = (f32[32,3072]{1,0:T(8,128)}, f32[32,3072]{1,0:T(8,128)S(1)}, u32[]{:S(2)}) copy-start(f32[32,3072]{1,0:T(8,128)S(1)} %collective-permute-done.7.ps_odd_ref) | copy-start | bytes 1179652
  45.5 16.6 %collective-permute-start.4 = (f32[32,3072]{1,0:T(8,128)S(1)}, f32[32,3072]{1,0:T(8,128)S(1)}, u32[]{:S(2)}, u32[]{:S(2)}) collective-permute-start(f32[32,3072]{1,0:T(8,128)S(1)} %copy-done.2), channel_id=1, source_target_pairs={{0,1},{1,0},{2,3},{3,2},{4,5},{5,4},{6,7},{7,6},{8,9},{9,8},{10,11... | collective-permute-start | bytes 1179656 | tf_op jit(solution)/shard_map/ppermute | solution.py:420
  45.6 7.8 %copy-start.8 = (f32[32,3072]{1,0:T(8,128)}, f32[32,3072]{1,0:T(8,128)S(1)}, u32[]{:S(2)}) copy-start(f32[32,3072]{1,0:T(8,128)S(1)} %collective-permute-done.8.ps_even_ref) | copy-start | bytes 1179652
  45.6 20.7 %collective-permute-start.3 = (f32[32,3072]{1,0:T(8,128)}, f32[32,3072]{1,0:T(8,128)S(1)}, u32[]{:S(2)}, u32[]{:S(2)}) collective-permute-start(f32[32,3072]{1,0:T(8,128)} %get-tuple-element.19.y_ref), channel_id=1, source_target_pairs={{0,1},{1,0},{2,3},{3,2},{4,5},{5,4},{6,7},{7,6},{8,9},{9,8},{10,11... | collective-permute-start | bytes 1179656 | tf_op jit(solution)/shard_map/ppermute | solution.py:420
  47.6 18.7 %all-to-all-start = ((f32[256,1,128]{2,1,0:T(1,128)}), f32[256,1,128]{2,1,0:T(1,128)S(1)}, u32[]{:S(2)}, u32[]{:S(2)}) async-start(f32[256,1,128]{2,1,0:T(1,128)} %broadcast_in_dim.11), calls=%async_computation | async-start | bytes 262144 | tf_op jit(solution)/shard_map/all_to_all | solution.py:446
  53.3 51.1 %copy-start.3 = (f32[192,64]{0,1:T(8,128)S(1)}, f32[192,64]{0,1:T(8,128)}, u32[]{:S(2)}) copy-start(f32[192,64]{0,1:T(8,128)} %param.9) | copy-start | bytes 147460
  53.3 0.7 copy-start.14
  62.1 4.2 %copy-start.11 = (f32[32,3072]{1,0:T(8,128)}, f32[32,3072]{1,0:T(8,128)S(1)}, u32[]{:S(2)}) copy-start(f32[32,3072]{1,0:T(8,128)S(1)} %collective-permute-done.2.xo_ref) | copy-start | bytes 1179652
  62.1 4.2 %copy-start.12 = (f32[32,3072]{1,0:T(8,128)}, f32[32,3072]{1,0:T(8,128)S(1)}, u32[]{:S(2)}) copy-start(f32[32,3072]{1,0:T(8,128)S(1)} %collective-permute-done.4.po_ref) | copy-start | bytes 1179652
  66.2 0.7 copy-start.4
  66.2 0.8 copy-start.13
  97.6 16.4 %all-to-all-start.3 = ((f32[32,24,128]{2,1,0:T(8,128)}), f32[32,24,128]{2,1,0:T(8,128)S(1)}, u32[]{:S(2)}, u32[]{:S(2)}) async-start(f32[32,24,128]{2,1,0:T(8,128)} %broadcast_in_dim.13), calls=%async_computation.3 | async-start | bytes 786432 | tf_op jit(solution)/shard_map/all_to_all | solution.py:57
  114.1 0.8 copy-start

commit v7 on v6

--- a/solution.py
+++ b/solution.py
@@ -13,6 +13,8 @@
 BF16 = jnp.bfloat16
 UNROLL = 24
 GROUP = 6
+WIDE_GROUP = 12
+PIECE = 64
 CHUNK = 4
 VMEM_LIMIT = 60 * 2**20
 PIVOTS = 16
@@ -74,9 +76,9 @@
     return copies
 
 
-def wait_group(copies, i):
-    if i % GROUP == 0:
-        for copy in copies[i : i + GROUP]:
+def wait_group(copies, i, group):
+    if i % group == 0:
+        for copy in copies[i : i + group]:
             copy.wait()
 
 
@@ -84,10 +86,16 @@
     return [pl.BlockSpec(memory_space=space) for space in spaces]
 
 
-def degree_kernel(a_hbm, x_ref, scale_ref, xs_ref, a_ref, arrived):
+def degree_kernel(a_hbm, x_hbm, scale_ref, xs_hbm, a_ref, x_ref, xs_ref, arrived, x_arrived, sent):
+    count = a_ref.shape[0]
     copies = loads(a_hbm, a_ref, arrived)
-    for i in range(a_ref.shape[0]):
-        wait_group(copies, i)
+    x_copy = pltpu.make_async_copy(x_hbm, x_ref, x_arrived)
+    x_copy.start()
+    sends = []
+    for i in range(count):
+        wait_group(copies, i, GROUP)
+        if i == 0:
+            x_copy.wait()
         total = a_ref[i, 0]
         for k in range(1, 6):
             total = total + a_ref[i, k]
@@ -95,15 +103,29 @@
         scale_ref[i : i + 1, :] = scale
         lanes = slice(i * BLK, (i + 1) * BLK)
         xs_ref[:, lanes] = x_ref[:, lanes] * scale
+        if i % GROUP == GROUP - 1:
+            span = pl.ds((i + 1 - GROUP) * BLK, GROUP * BLK)
+            sends.append(pltpu.make_async_copy(xs_ref.at[:, span], xs_hbm.at[:, span], sent.at[i // GROUP]))
+            sends[-1].start()
+    for copy in sends:
+        copy.wait()
 
 
 def degrees(affinity, x):
     n = affinity.shape[0]
     return pl.pallas_call(
         degree_kernel,
-        in_specs=memory(pl.ANY, pltpu.VMEM),
+        in_specs=memory(pl.ANY, pl.ANY),
+        out_specs=memory(pltpu.VMEM, pl.ANY),
         out_shape=[jax.ShapeDtypeStruct((n, BLK), F32), jax.ShapeDtypeStruct(x.shape, F32)],
-        scratch_shapes=[pltpu.VMEM(affinity.shape, F32), pltpu.SemaphoreType.DMA((n,))],
+        scratch_shapes=[
+            pltpu.VMEM(affinity.shape, F32),
+            pltpu.VMEM(x.shape, F32),
+            pltpu.VMEM(x.shape, F32),
+            pltpu.SemaphoreType.DMA((n,)),
+            pltpu.SemaphoreType.DMA,
+            pltpu.SemaphoreType.DMA((n // GROUP,)),
+        ],
         compiler_params=pltpu.CompilerParams(vmem_limit_bytes=VMEM_LIMIT),
         cost_estimate=pl.CostEstimate(flops=10**7, bytes_accessed=10**7, transcendentals=3072),
         name="degrees",
@@ -118,13 +140,13 @@
         lanes = slice(i * BLK, (i + 1) * BLK)
         ps_ref[:, lanes] = p_ref[:, lanes] * scale_ref[i : i + 1, :]
     for i in range(count):
-        wait_group(copies, i)
+        wait_group(copies, i, WIDE_GROUP)
         for k in range(6):
             high, low = halves(a_ref[i, k])
             split_ref[i, 0:BLK, k * BLK : (k + 1) * BLK] = high
             split_ref[i, BLK : 2 * BLK, k * BLK : (k + 1) * BLK] = low
-        if i % GROUP == GROUP - 1:
-            for copy in sends[i + 1 - GROUP : i + 1]:
+        if i % WIDE_GROUP == WIDE_GROUP - 1:
+            for copy in sends[i + 1 - WIDE_GROUP : i + 1]:
                 copy.start()
     for copy in sends:
         copy.wait()
@@ -161,7 +183,7 @@
 
 
 def gathered(info, pat, turned, i):
-    places = [local_place(pat[i, k], info[1], info[2]) for k in range(6)]
+    places = [local_place(pat[k, i], info[1], info[2]) for k in range(6)]
     return jnp.concatenate([turned[place] for place in places], axis=0)
 
 
@@ -190,7 +212,7 @@
     xx = jnp.zeros((32, BLK), F32)
     for i in range(count):
         lanes = slice(i * BLK, (i + 1) * BLK)
-        wait_group(copies, i)
+        wait_group(copies, i, GROUP)
         weights = gathered(info, pat, turned, i)
         product = jnp.dot(split_ref[i], weights, preferred_element_type=F32)
         image = (product[:BLK] + product[BLK:]).T
@@ -234,7 +256,7 @@
     turn_all(turned, info[3], ((ys_odd_ref, ps_odd_ref), (ys_ref, ps_ref), (ys_even_ref, ps_even_ref)), count)
     for i in range(count):
         lanes = slice(i * BLK, (i + 1) * BLK)
-        wait_group(copies, i)
+        wait_group(copies, i, GROUP)
         weights = gathered(info, pat, turned, i)
         product = jnp.dot(split_ref[i], weights, preferred_element_type=F32)
         image = (product[:BLK] + product[BLK:]).T
@@ -325,33 +347,34 @@
 def inverse_factor(block):
     lane = lax.broadcasted_iota(jnp.int32, (8, BLK), 1)
     sub = lax.broadcasted_iota(jnp.int32, (8, BLK), 0)
+    tall = PIECE // 8
     a = []
-    for g in range(4):
-        unit = jnp.where(lane - 32 == sub + 8 * g, 1.0, 0.0)
-        a.append(jnp.where(lane < 32, block[8 * g : 8 * g + 8, :], unit))
-    for start in range(0, 32, PIVOTS):
+    for g in range(tall):
+        unit = jnp.where(lane - PIECE == sub + 8 * g, 1.0, 0.0)
+        a.append(jnp.where(lane < PIECE, block[8 * g : 8 * g + 8, :], unit))
+    for start in range(0, PIECE, PIVOTS):
         columns = [
-            [jnp.broadcast_to(a[g][:, start + k : start + k + 1], (8, BLK)) if g >= start // 8 else None for g in range(4)]
+            [jnp.broadcast_to(a[g][:, start + k : start + k + 1], (8, BLK)) if g >= start // 8 else None for g in range(tall)]
             for k in range(PIVOTS)
         ]
         for k in range(PIVOTS):
             at = start + k
             own = at // 8
             pivot = 1.0 / picked_row(columns[k], at)
-            factor = [columns[k][g] * pivot if g >= own else None for g in range(4)]
+            factor = [columns[k][g] * pivot if g >= own else None for g in range(tall)]
             factor[own] = jnp.where(sub > at % 8, factor[own], 0.0)
             for other in columns[k + 1 :]:
                 e = picked_row(other, at)
-                for g in range(own, 4):
+                for g in range(own, tall):
                     other[g] = other[g] - factor[g] * e
             row = picked_row(a, at)
-            for g in range(own, 4):
+            for g in range(own, tall):
                 a[g] = a[g] - factor[g] * row
     scaled = []
-    for g in range(4):
+    for g in range(tall):
         diagonal = jnp.sum(jnp.where(lane == sub + 8 * g, a[g], 0.0), axis=1, keepdims=True)
         scaled.append(a[g] * lax.rsqrt(diagonal))
-    return jnp.concatenate(scaled, axis=0)[:, 32:64]
+    return jnp.concatenate(scaled, axis=0)[:, PIECE : 2 * PIECE]
 
 
 def exact(left, right, dims):
@@ -359,31 +382,37 @@
 
 
 def inverse_cholesky(work, inverse):
-    lane = lax.broadcasted_iota(jnp.int32, (32, 192), 1)
-    sub = lax.broadcasted_iota(jnp.int32, (32, 192), 0)
-    for at in range(0, 192, 32):
-        rows = work[at : at + 32, :]
+    lane = lax.broadcasted_iota(jnp.int32, (PIECE, 192), 1)
+    sub = lax.broadcasted_iota(jnp.int32, (PIECE, 192), 0)
+    for at in range(0, 192, PIECE):
+        rows = work[at : at + PIECE, :]
         if at < BLK:
             piece = rows[:, 0:BLK]
         else:
-            piece = jnp.concatenate([rows[:, BLK:192], jnp.zeros((32, 64), F32)], axis=1)
+            piece = jnp.concatenate([rows[:, BLK:192], jnp.zeros((PIECE, 64), F32)], axis=1)
         if at % BLK:
             piece = pltpu.roll(piece, BLK - at % BLK, 1)
         small = inverse_factor(piece)
         unit = jnp.where(lane - at == sub, 1.0, 0.0)
-        rows = jnp.where((lane >= at) & (lane < at + 32), unit, rows)
+        rows = jnp.where((lane >= at) & (lane < at + PIECE), unit, rows)
         new = exact(small, rows, ((1,), (0,)))
-        inverse[at : at + 32, :] = jnp.where(lane < at + 32, new, 0.0)
-        if at < 160:
+        inverse[at : at + PIECE, :] = jnp.where(lane < at + PIECE, new, 0.0)
+        if at + PIECE < 192:
             update = exact(new, new, ((0,), (0,)))
-            wide = lax.broadcasted_iota(jnp.int32, (160 - at, 192), 1)
-            old = jnp.where((wide >= at) & (wide < at + 32), 0.0, work[at + 32 : 192, :])
-            work[at + 32 : 192, :] = old - update[at + 32 : 192, :]
+            wide = lax.broadcasted_iota(jnp.int32, (192 - PIECE - at, 192), 1)
+            old = jnp.where((wide >= at) & (wide < at + PIECE), 0.0, work[at + PIECE : 192, :])
+            work[at + PIECE : 192, :] = old - update[at + PIECE : 192, :]
 
 
 def final_kernel(
-    both_ref, chosen_ref, high_ref, low_ref, vectors_ref, directions_ref, ritz_ref, work, raw, inverse, *, factor
+    both_ref, chosen_ref, high_hbm, low_hbm, vectors_ref, directions_ref, ritz_ref, high_ref, low_ref, work, raw, inverse, arrived, *, factor
 ):
+    copies = [
+        pltpu.make_async_copy(high_hbm, high_ref, arrived.at[0]),
+        pltpu.make_async_copy(low_hbm, low_ref, arrived.at[1]),
+    ]
+    for copy in copies:
+        copy.start()
     for at in range(6):
         for base, target in ((0, work), (96, raw)):
             row = 384 * (at % 2) + base + 32 * (at // 2)
@@ -395,6 +424,8 @@
     ritz_ref[...] = exact(half, whole_inverse, ((1,), (1,)))
     mix = factor * exact(chosen_ref[...], whole_inverse, ((1,), (0,)))
     left = jnp.concatenate(halves(mix), axis=0)
+    for copy in copies:
+        copy.wait()
     for at in range(0, high_ref.shape[1], 512):
         lanes = slice(at, at + 512)
         product = jnp.dot(left, high_ref[:, lanes], preferred_element_type=F32)
@@ -407,9 +438,9 @@
 def final(both, chosen, high, low, factor):
     return pl.pallas_call(
         functools.partial(final_kernel, factor=factor),
-        in_specs=memory(*[pltpu.VMEM] * 4),
+        in_specs=memory(pltpu.VMEM, pltpu.VMEM, pl.ANY, pl.ANY),
         out_shape=[jax.ShapeDtypeStruct((32, high.shape[1]), F32)] * 2 + [jax.ShapeDtypeStruct((192, 192), F32)],
-        scratch_shapes=[pltpu.VMEM((192, 192), F32)] * 3,
+        scratch_shapes=[pltpu.VMEM(high.shape, BF16)] * 2 + [pltpu.VMEM((192, 192), F32)] * 3 + [pltpu.SemaphoreType.DMA((2,))],
         compiler_params=pltpu.CompilerParams(vmem_limit_bytes=VMEM_LIMIT),
         cost_estimate=pl.CostEstimate(flops=4 * 10**8, bytes_accessed=4 * 10**6, transcendentals=0),
         name="final",
@@ -431,20 +462,21 @@
     place = lax.axis_index("rows")
     first_block = (place - 1) * local_blocks
     info = jnp.stack([core, first_block, jnp.int32(all_blocks), place % 2]).astype(jnp.int32)
+    columns = pattern.T
     scale, xs = degrees(affinity, vectors)
     xs_odd, xs_even = from_neighbours(xs)
     split, ps = split_affinity(affinity, scale, directions)
     ps_odd, ps_even = from_neighbours(ps)
     x_other = other_core(vectors)
     p_other = other_core(directions)
-    y, ys, sums = first_image(info, pattern, split, vectors, xs, xs_odd, xs_even, scale)
+    y, ys, sums = first_image(info, columns, split, vectors, xs, xs_odd, xs_even, scale)
     ys_odd, ys_even = from_neighbours(ys)
     y_other = other_core(y)
     half = sums[:, 0:64]
     blank = jnp.zeros_like(half)
     row = jnp.where(core == 0, jnp.concatenate([half, blank], axis=1), jnp.concatenate([blank, half], axis=1))
     sums = lax.all_to_all(repeated(row, 2 * devices), ("rows", "cols"), 0, 0).reshape(2 * devices, BLK)
-    z, image = second_image(info, pattern, split, ys, ys_odd, ys_even, ps, ps_odd, ps_even, scale, y, directions)
+    z, image = second_image(info, columns, split, ys, ys_odd, ys_even, ps, ps_odd, ps_even, scale, y, directions)
     high, low, part = products(info, sums, vectors, y, directions, x_other, y_other, p_other, z, image)
     both = sum_large(part.reshape(16, 24, BLK)).reshape(768, BLK)
     mine = lambda m: lax.dynamic_slice_in_dim(m, core * width, width, 1)

time: 127 us -> 125 us (0.984)
  Pallas kernels: 47.8 us -> 45.7 us
    pallas_call x1, Pallas kernels: 11.9 us -> 10.3 us  [final(): pl.pallas_call(functools.partial(final_kernel, factor=factor), in_specs=m...]
    unnamed x31 -> x28, local copies, waits for them, and re-layouts: 3.86 us -> 3.17 us
  transfers between devices with their start and end apart: 11 -> 11, of which waited for: 2 -> 2; matrix products, arithmetic and copies ran while one was open for 3% -> 2% of each run, Pallas kernels for 20% -> 20%
where the time goes in v7:
time: 125 us; the launch traced here: 124 us
  Pallas kernels  45.7 us (37%)
  starting transfers between devices  32.8 us (26%)
  blocking collectives  24.7 us (20%)
  waiting for transfers between devices  13.1 us (10%)
  local copies, waits for them, and re-layouts  4.76 us (4%)
  other arithmetic  2.14 us (2%)
    all_to_all x2, blocking collectives, exchange(): return lax.all_to_all(x, 'rows', 0, 0, axis_index_groups=groups)  24.7 us
    ppermute x6, starting transfers between devices, from_neighbours(): return [lax.ppermute(x, 'rows', swaps(devices, first)) for first in (1, 0)]  18.2 us
    pallas_call x1, Pallas kernels, final(): pl.pallas_call(functools.partial(final_kernel, factor=factor), in_specs=m...  10.3 us
    pallas_call x1, Pallas kernels, split_affinity(): pl.pallas_call(split_kernel, in_specs=memory(pl.ANY, pltpu.VMEM, pltpu.VM...  8.91 us
    all_to_all x1, waiting for transfers between devices, exchange_cores(): lax.all_to_all(x, ('rows', 'cols'), 0, 0, axis_index_groups=with_cores(gr...  8.9 us
    pallas_call x1, Pallas kernels, second_image(): pl.pallas_call(second_kernel, in_specs=memory(pltpu.SMEM, pltpu.SMEM, pl....  7.93 us
    pallas_call x1, Pallas kernels, first_image(): pl.pallas_call(first_kernel, in_specs=memory(pltpu.SMEM, pltpu.SMEM, pl.A...  7.4 us
    all_to_all x1, starting transfers between devices, exchange_cores(): lax.all_to_all(x, ('rows', 'cols'), 0, 0, axis_index_groups=with_cores(gr...  6.77 us
  transfers between devices with their start and end apart: 11, of which 2 were waited for; matrix products, arithmetic and copies ran while one was open for 2% of the time, Pallas kernels for 20%

profile of v7, /device:TPU:1, one launch (start us, length us, event | category | flops | bytes accessed | tf_op | source)
XLA Modules:
  0.0 124.3 jit_solution(3422553710622289401)
XLA Ops:
  0.6 6.1 %degrees.1 = (f32[24,128]{1,0:T(8,128)}, f32[32,3072]{1,0:T(8,128)}) custom-call(f32[24,6,128,128]{3,2,1,0:T(8,128)} %a_hbm.3, f32[32,3072]{1,0:T(8,128)} %x_ref.3), custom_call_target="tpu_custom_call" | custom-call | flops 10000000 | bytes 10000000 | tf_op jit(solution)/shard_map/degrees/pallas_call | solution.py:116
  6.7 11.1 %collective-permute-start = (f32[32,3072]{1,0:T(8,128)}, f32[32,3072]{1,0:T(8,128)S(1)}, u32[]{:S(2)}, u32[]{:S(2)}) collective-permute-start(f32[32,3072]{1,0:T(8,128)} %get-tuple-element.17.xs_ref), channel_id=1, source_target_pairs={{2,4},{4,2},{6,8},{8,6},{10,12},{12,10},{14,16},{16,14},{18,20},{2... | collective-permute-start | bytes 1179656 | tf_op jit(solution)/shard_map/ppermute | solution.py:35
  17.8 8.9 %split.1 = (bf16[24,256,768]{2,1,0:T(8,128)(2,1)}, f32[32,3072]{1,0:T(8,128)}) custom-call(f32[24,6,128,128]{3,2,1,0:T(8,128)} %a_hbm.3, f32[24,128]{1,0:T(8,128)} %get-tuple-element.15.scale_ref.s_ref, f32[32,3072]{1,0:T(8,128)} %p_ref.5), custom_call_target="tpu_custom_call" | custom-call | flops 10000000 | bytes 19000000 | tf_op jit(solution)/shard_map/split/pallas_call | solution.py:158
  26.8 0.0 copy-start.5
  26.8 0.7 collective-permute-start.7
  27.5 0.9 collective-permute-start.8
  28.4 0.7 pad_add_fusion.info
  29.1 0.8 copy-done.8
  29.9 0.1 copy-done.9
  30.0 7.4 %first_image.1 = (f32[32,3072]{1,0:T(8,128)}, f32[32,3072]{1,0:T(8,128)}, f32[1,128]{1,0:T(1,128)}) custom-call(s32[4]{0:T(128)} %pad_add_fusion.info, s32[6,24]{1,0:T(8,128)} %bitcast.16, bf16[24,256,768]{2,1,0:T(8,128)(2,1)} %get-tuple-element.16.a_hbm, f32[32,3072]{1,0:T(8,128)} %x_ref.3, f32[32,3072]{1,0:T(8,128)} %get-tuple-element.17.xs_ref, ...), custom_call_target="tpu_custom_call" | custom-call | flops 4000000000 | bytes 11000000 | tf_op jit(solution)/shard_map/first_image/pallas_call | solution.py:231
  37.4 5.4 %collective-permute-start.5 = (f32[32,3072]{1,0:T(8,128)}, f32[32,3072]{1,0:T(8,128)S(1)}, u32[]{:S(2)}, u32[]{:S(2)}) collective-permute-start(f32[32,3072]{1,0:T(8,128)} %get-tuple-element.20.ys_ref), channel_id=1, source_target_pairs={{2,4},{4,2},{6,8},{8,6},{10,12},{12,10},{14,16},{16,14},{18,20},{2... | collective-permute-start | bytes 1179656 | tf_op jit(solution)/shard_map/ppermute | solution.py:35
  42.8 1.5 %collective-permute-start.2 = (f32[32,3072]{1,0:T(8,128)S(1)}, f32[32,3072]{1,0:T(8,128)S(1)}, u32[]{:S(2)}, u32[]{:S(2)}) collective-permute-start(f32[32,3072]{1,0:T(8,128)S(1)} %copy-done.1), channel_id=1, source_target_pairs={{0,1},{1,0},{2,3},{3,2},{4,5},{5,4},{6,7},{7,6},{8,9},{9,8},{10,11... | collective-permute-start | bytes 1179656 | tf_op jit(solution)/shard_map/ppermute | solution.py:451
  44.4 0.1 collective-permute-start.4
  44.5 0.5 collective-permute-start.3
  45.0 0.8 fusion.2
  45.8 0.7 broadcast_in_dim.11
  46.5 5.7 %all-to-all-start = ((f32[256,1,128]{2,1,0:T(1,128)}), f32[256,1,128]{2,1,0:T(1,128)S(1)}, u32[]{:S(2)}, u32[]{:S(2)}) async-start(f32[256,1,128]{2,1,0:T(1,128)} %broadcast_in_dim.11), calls=%async_computation | async-start | bytes 262144 | tf_op jit(solution)/shard_map/all_to_all | solution.py:478
  52.3 0.7 copy-done.13
  53.0 7.9 %second_image.1 = (f32[32,3072]{1,0:T(8,128)}, f32[32,3072]{1,0:T(8,128)}) custom-call(s32[4]{0:T(128)} %pad_add_fusion.info, s32[6,24]{1,0:T(8,128)} %bitcast.17, bf16[24,256,768]{2,1,0:T(8,128)(2,1)} %get-tuple-element.16.a_hbm, f32[32,3072]{1,0:T(8,128)} %get-tuple-element.20.ys_ref, f32[32,3072]{1,0:T(8,128)} %copy-done.13, ...), custom_call_target="tpu_custom_call" | custom-call | flops 4000000000 | bytes 14000000 | tf_op jit(solution)/shard_map/second_image/pallas_call | solution.py:270
  61.0 4.2 %all-to-all-done = f32[256,1,128]{2,1,0:T(1,128)S(1)} async-done(((f32[256,1,128]{2,1,0:T(1,128)}), f32[256,1,128]{2,1,0:T(1,128)S(1)}, u32[]{:S(2)}, u32[]{:S(2)}) %all-to-all-start) | async-done | bytes 131104 | tf_op jit(solution)/shard_map/all_to_all | solution.py:478
  65.2 0.6 copy-done.4
  65.8 0.1 copy-done.12
  65.9 5.0 %products.1 = (bf16[192,3072]{1,0:T(8,128)(2,1)}, bf16[192,3072]{1,0:T(8,128)(2,1)}, f32[384,128]{1,0:T(8,128)}) custom-call(s32[4]{0:T(128)} %pad_add_fusion.info, f32[256,128]{1,0:T(8,128)} %bitcast.14, f32[32,3072]{1,0:T(8,128)} %x_ref.3, f32[32,3072]{1,0:T(8,128)} %get-tuple-element.19.y_ref, f32[32,3072]{1,0:T(8,128)} %p_ref.5, f32[32,3072]{1,0:T(8,128)} %copy-done.10, ...), custom_call_target="tpu_custom_call" | custom-call | flops 2000000000 | bytes 6000000 | tf_op jit(solution)/shard_map/products/pallas_call | solution.py:328
  71.0 10.4 %all_to_all.20 = f32[16,24,128]{2,1,0:T(8,128)S(1)} all-to-all(f32[16,24,128]{2,1,0:T(8,128)} %bitcast.13), channel_id=1, replica_groups={{0,2,4,6,8,10,12,14,16,18,20,22,24,26,28,30},{32,34,36,38,40,42,44,46,4..., dimensions={0} | all-to-all | bytes 393216 | tf_op jit(solution)/shard_map/all_to_all | solution.py:55
  81.4 14.3 %all_to_all.21 = f32[8,24,128]{2,1,0:T(8,128)S(1)} all-to-all(f32[8,24,128]{2,1,0:T(8,128)S(1)} %broadcast_in_dim.12), channel_id=1, replica_groups={{0,32,64,96,128,160,192,224},{2,34,66,98,130,162,194,226},{4,36,68,100,..., dimensions={0} | all-to-all | bytes 196608 | tf_op jit(solution)/shard_map/all_to_all | solution.py:55
  95.8 0.8 broadcast_in_dim.13
  96.5 6.8 %all-to-all-start.3 = ((f32[32,24,128]{2,1,0:T(8,128)}), f32[32,24,128]{2,1,0:T(8,128)S(1)}, u32[]{:S(2)}, u32[]{:S(2)}) async-start(f32[32,24,128]{2,1,0:T(8,128)} %broadcast_in_dim.13), calls=%async_computation.3 | async-start | bytes 786432 | tf_op jit(solution)/shard_map/all_to_all | solution.py:59
  103.4 0.1 pad.5.clone
  103.4 0.6 maximum_bitcast_fusion.chosen_ref
  104.1 8.9 %all-to-all-done.3 = f32[32,24,128]{2,1,0:T(8,128)S(1)} async-done(((f32[32,24,128]{2,1,0:T(8,128)}), f32[32,24,128]{2,1,0:T(8,128)S(1)}, u32[]{:S(2)}, u32[]{:S(2)}) %all-to-all-start.3) | async-done | bytes 393248 | tf_op jit(solution)/shard_map/all_to_all | solution.py:59
  113.0 0.8 copy-done
  113.7 10.3 %final.1 = (f32[32,3072]{1,0:T(8,128)}, f32[32,3072]{1,0:T(8,128)}, f32[192,192]{1,0:T(8,128)}) custom-call(f32[768,128]{1,0:T(8,128)} %bitcast.12, f32[64,192]{1,0:T(8,128)} %maximum_bitcast_fusion.chosen_ref, bf16[192,3072]{1,0:T(8,128)(2,1)} %get-tuple-element.25.high_hbm, bf16[192,3072]{1,0:T(8,128)(2,1)} %get-tuple-element.26.low_hbm), custom_call_target="tpu_custom_call" | custom-call | flops 400000000 | bytes 4000000 | tf_op jit(solution)/shard_map/final/pallas_call | solution.py:439
  (38 shorter events, 0.1 us)
Async XLA Ops:
  6.7 22.4 %collective-permute-start = (f32[32,3072]{1,0:T(8,128)}, f32[32,3072]{1,0:T(8,128)S(1)}, u32[]{:S(2)}, u32[]{:S(2)}) collective-permute-start(f32[32,3072]{1,0:T(8,128)} %get-tuple-element.17.xs_ref), channel_id=1, source_target_pairs={{2,4},{4,2},{6,8},{8,6},{10,12},{12,10},{14,16},{16,14},{18,20},{2... | collective-permute-start | bytes 1179656 | tf_op jit(solution)/shard_map/ppermute | solution.py:35
  17.8 11.3 %collective-permute-start.1 = (f32[32,3072]{1,0:T(8,128)}, f32[32,3072]{1,0:T(8,128)S(1)}, u32[]{:S(2)}, u32[]{:S(2)}) collective-permute-start(f32[32,3072]{1,0:T(8,128)} %get-tuple-element.17.xs_ref), channel_id=1, source_target_pairs={{0,2},{2,0},{4,6},{6,4},{8,10},{10,8},{12,14},{14,12},{16,18},{18,... | collective-permute-start | bytes 1179656 | tf_op jit(solution)/shard_map/ppermute | solution.py:35
  26.8 16.1 %copy-start.1 = (f32[32,3072]{1,0:T(8,128)S(1)}, f32[32,3072]{1,0:T(8,128)}, u32[]{:S(2)}) copy-start(f32[32,3072]{1,0:T(8,128)} %x_ref.3) | copy-start | bytes 1179652
  26.8 17.6 %copy-start.2 = (f32[32,3072]{1,0:T(8,128)S(1)}, f32[32,3072]{1,0:T(8,128)}, u32[]{:S(2)}) copy-start(f32[32,3072]{1,0:T(8,128)} %p_ref.5) | copy-start | bytes 1179652
  26.8 18.2 %copy-start.5 = (pred[1,128]{1,0:T(4,128)(4,1)S(1)}, pred[1,128]{1,0:T(4,128)(4,1)}, u32[]{:S(2)}) copy-start(pred[1,128]{1,0:T(4,128)(4,1)} %constant.36.clone.1) | copy-start | bytes 388
  26.8 17.6 %collective-permute-start.7 = (f32[32,3072]{1,0:T(8,128)}, f32[32,3072]{1,0:T(8,128)S(1)}, u32[]{:S(2)}, u32[]{:S(2)}) collective-permute-start(f32[32,3072]{1,0:T(8,128)} %get-tuple-element.21.ps_ref), channel_id=1, source_target_pairs={{2,4},{4,2},{6,8},{8,6},{10,12},{12,10},{14,16},{16,14},{18,20},{2... | collective-permute-start | bytes 1179656 | tf_op jit(solution)/shard_map/ppermute | solution.py:35
  27.5 17.0 %collective-permute-start.8 = (f32[32,3072]{1,0:T(8,128)}, f32[32,3072]{1,0:T(8,128)S(1)}, u32[]{:S(2)}, u32[]{:S(2)}) collective-permute-start(f32[32,3072]{1,0:T(8,128)} %get-tuple-element.21.ps_ref), channel_id=1, source_target_pairs={{0,2},{2,0},{4,6},{6,4},{8,10},{10,8},{12,14},{14,12},{16,18},{18,... | collective-permute-start | bytes 1179656 | tf_op jit(solution)/shard_map/ppermute | solution.py:35
  29.1 0.8 copy-start.8
  29.1 0.9 copy-start.9
  37.4 14.8 %collective-permute-start.5 = (f32[32,3072]{1,0:T(8,128)}, f32[32,3072]{1,0:T(8,128)S(1)}, u32[]{:S(2)}, u32[]{:S(2)}) collective-permute-start(f32[32,3072]{1,0:T(8,128)} %get-tuple-element.20.ys_ref), channel_id=1, source_target_pairs={{2,4},{4,2},{6,8},{8,6},{10,12},{12,10},{14,16},{16,14},{18,20},{2... | collective-permute-start | bytes 1179656 | tf_op jit(solution)/shard_map/ppermute | solution.py:35
  42.8 9.4 %collective-permute-start.6 = (f32[32,3072]{1,0:T(8,128)}, f32[32,3072]{1,0:T(8,128)}, u32[]{:S(2)}, u32[]{:S(2)}) collective-permute-start(f32[32,3072]{1,0:T(8,128)} %get-tuple-element.20.ys_ref), channel_id=1, source_target_pairs={{0,2},{2,0},{4,6},{6,4},{8,10},{10,8},{12,14},{14,12},{16,18},{18,... | collective-permute-start | bytes 1179656 | tf_op jit(solution)/shard_map/ppermute | solution.py:35
  42.8 18.1 %collective-permute-start.2 = (f32[32,3072]{1,0:T(8,128)S(1)}, f32[32,3072]{1,0:T(8,128)S(1)}, u32[]{:S(2)}, u32[]{:S(2)}) collective-permute-start(f32[32,3072]{1,0:T(8,128)S(1)} %copy-done.1), channel_id=1, source_target_pairs={{0,1},{1,0},{2,3},{3,2},{4,5},{5,4},{6,7},{7,6},{8,9},{9,8},{10,11... | collective-permute-start | bytes 1179656 | tf_op jit(solution)/shard_map/ppermute | solution.py:451
  44.4 7.9 %copy-start.6 = (f32[32,3072]{1,0:T(8,128)}, f32[32,3072]{1,0:T(8,128)S(1)}, u32[]{:S(2)}) copy-start(f32[32,3072]{1,0:T(8,128)S(1)} %collective-permute-done.7.ps_odd_ref) | copy-start | bytes 1179652
  44.4 16.6 %collective-permute-start.4 = (f32[32,3072]{1,0:T(8,128)S(1)}, f32[32,3072]{1,0:T(8,128)S(1)}, u32[]{:S(2)}, u32[]{:S(2)}) collective-permute-start(f32[32,3072]{1,0:T(8,128)S(1)} %copy-done.2), channel_id=1, source_target_pairs={{0,1},{1,0},{2,3},{3,2},{4,5},{5,4},{6,7},{7,6},{8,9},{9,8},{10,11... | collective-permute-start | bytes 1179656 | tf_op jit(solution)/shard_map/ppermute | solution.py:451
  44.5 7.8 %copy-start.7 = (f32[32,3072]{1,0:T(8,128)}, f32[32,3072]{1,0:T(8,128)S(1)}, u32[]{:S(2)}) copy-start(f32[32,3072]{1,0:T(8,128)S(1)} %collective-permute-done.8.ps_even_ref) | copy-start | bytes 1179652
  44.5 20.7 %collective-permute-start.3 = (f32[32,3072]{1,0:T(8,128)}, f32[32,3072]{1,0:T(8,128)S(1)}, u32[]{:S(2)}, u32[]{:S(2)}) collective-permute-start(f32[32,3072]{1,0:T(8,128)} %get-tuple-element.19.y_ref), channel_id=1, source_target_pairs={{0,1},{1,0},{2,3},{3,2},{4,5},{5,4},{6,7},{7,6},{8,9},{9,8},{10,11... | collective-permute-start | bytes 1179656 | tf_op jit(solution)/shard_map/ppermute | solution.py:451
  46.5 18.7 %all-to-all-start = ((f32[256,1,128]{2,1,0:T(1,128)}), f32[256,1,128]{2,1,0:T(1,128)S(1)}, u32[]{:S(2)}, u32[]{:S(2)}) async-start(f32[256,1,128]{2,1,0:T(1,128)} %broadcast_in_dim.11), calls=%async_computation | async-start | bytes 262144 | tf_op jit(solution)/shard_map/all_to_all | solution.py:478
  52.2 51.1 %copy-start.3 = (f32[192,64]{0,1:T(8,128)S(1)}, f32[192,64]{0,1:T(8,128)}, u32[]{:S(2)}) copy-start(f32[192,64]{0,1:T(8,128)} %param.9) | copy-start | bytes 147460
  52.2 0.7 copy-start.13
  60.9 4.2 %copy-start.10 = (f32[32,3072]{1,0:T(8,128)}, f32[32,3072]{1,0:T(8,128)S(1)}, u32[]{:S(2)}) copy-start(f32[32,3072]{1,0:T(8,128)S(1)} %collective-permute-done.2.xo_ref) | copy-start | bytes 1179652
  61.0 4.2 %copy-start.11 = (f32[32,3072]{1,0:T(8,128)}, f32[32,3072]{1,0:T(8,128)S(1)}, u32[]{:S(2)}) copy-start(f32[32,3072]{1,0:T(8,128)S(1)} %collective-permute-done.4.po_ref) | copy-start | bytes 1179652
  65.1 0.7 copy-start.4
  65.1 0.8 copy-start.12
  96.5 16.4 %all-to-all-start.3 = ((f32[32,24,128]{2,1,0:T(8,128)}), f32[32,24,128]{2,1,0:T(8,128)S(1)}, u32[]{:S(2)}, u32[]{:S(2)}) async-start(f32[32,24,128]{2,1,0:T(8,128)} %broadcast_in_dim.13), calls=%async_computation.3 | async-start | bytes 786432 | tf_op jit(solution)/shard_map/all_to_all | solution.py:59
  113.0 0.8 copy-start

commit v8 on v7

--- a/solution.py
+++ b/solution.py
@@ -47,16 +47,8 @@
     return [[row_of(z, x, y) for z in range(8)] for x in range(4) for y in range(4)]
 
 
-def with_cores(groups):
-    return [[2 * i + core for core in range(2) for i in group] for group in groups]
-
-
 def exchange(x, groups):
     return lax.all_to_all(x, "rows", 0, 0, axis_index_groups=groups)
-
-
-def exchange_cores(x, groups):
-    return lax.all_to_all(x, ("rows", "cols"), 0, 0, axis_index_groups=with_cores(groups))
 
 
 def repeated(x, count):
@@ -66,7 +58,7 @@
 def sum_large(x):
     part = jnp.sum(exchange(x, plane_groups()), axis=0)
     part = jnp.sum(exchange(repeated(part, 8), column_groups()), axis=0)
-    return exchange_cores(repeated(part, 32), plane_groups())
+    return exchange(repeated(part, 16), plane_groups())
 
 
 def loads(a_hbm, a_ref, arrived):
@@ -86,16 +78,10 @@
     return [pl.BlockSpec(memory_space=space) for space in spaces]
 
 
-def degree_kernel(a_hbm, x_hbm, scale_ref, xs_hbm, a_ref, x_ref, xs_ref, arrived, x_arrived, sent):
-    count = a_ref.shape[0]
+def degree_kernel(a_hbm, x_ref, scale_ref, xs_ref, a_ref, arrived):
     copies = loads(a_hbm, a_ref, arrived)
-    x_copy = pltpu.make_async_copy(x_hbm, x_ref, x_arrived)
-    x_copy.start()
-    sends = []
-    for i in range(count):
+    for i in range(a_ref.shape[0]):
         wait_group(copies, i, GROUP)
-        if i == 0:
-            x_copy.wait()
         total = a_ref[i, 0]
         for k in range(1, 6):
             total = total + a_ref[i, k]
@@ -103,29 +89,15 @@
         scale_ref[i : i + 1, :] = scale
         lanes = slice(i * BLK, (i + 1) * BLK)
         xs_ref[:, lanes] = x_ref[:, lanes] * scale
-        if i % GROUP == GROUP - 1:
-            span = pl.ds((i + 1 - GROUP) * BLK, GROUP * BLK)
-            sends.append(pltpu.make_async_copy(xs_ref.at[:, span], xs_hbm.at[:, span], sent.at[i // GROUP]))
-            sends[-1].start()
-    for copy in sends:
-        copy.wait()
 
 
 def degrees(affinity, x):
     n = affinity.shape[0]
     return pl.pallas_call(
         degree_kernel,
-        in_specs=memory(pl.ANY, pl.ANY),
-        out_specs=memory(pltpu.VMEM, pl.ANY),
+        in_specs=memory(pl.ANY, pltpu.VMEM),
         out_shape=[jax.ShapeDtypeStruct((n, BLK), F32), jax.ShapeDtypeStruct(x.shape, F32)],
-        scratch_shapes=[
-            pltpu.VMEM(affinity.shape, F32),
-            pltpu.VMEM(x.shape, F32),
-            pltpu.VMEM(x.shape, F32),
-            pltpu.SemaphoreType.DMA((n,)),
-            pltpu.SemaphoreType.DMA,
-            pltpu.SemaphoreType.DMA((n // GROUP,)),
-        ],
+        scratch_shapes=[pltpu.VMEM(affinity.shape, F32), pltpu.SemaphoreType.DMA((n,))],
         compiler_params=pltpu.CompilerParams(vmem_limit_bytes=VMEM_LIMIT),
         cost_estimate=pl.CostEstimate(flops=10**7, bytes_accessed=10**7, transcendentals=3072),
         name="degrees",
@@ -222,11 +194,13 @@
         ys_ref[:, lanes] = s * y
         xy += x * y
         xx += x * x
-    stack = jnp.concatenate([xy, xx, jnp.zeros((64, BLK), F32)], axis=0)
-    sums_ref[...] = jnp.sum(stack.T, axis=0, keepdims=True)
-
-
-def first_image(info, pattern, split, x, xs, across_odd, across_even, s):
+    core = info[0]
+    pair = jnp.concatenate([xy, xx], axis=0)
+    stack = jnp.concatenate([jnp.where(core == 0, pair, 0.0), jnp.where(core == 1, pair, 0.0)], axis=0)
+    sums_ref[...] = jnp.broadcast_to(jnp.sum(stack.T, axis=0, keepdims=True), sums_ref.shape)
+
+
+def first_image(info, pattern, split, x, xs, across_odd, across_even, s, copies):
     n = s.shape[0]
     return pl.pallas_call(
         first_kernel,
@@ -234,7 +208,7 @@
         out_shape=[
             jax.ShapeDtypeStruct(x.shape, F32),
             jax.ShapeDtypeStruct(x.shape, F32),
-            jax.ShapeDtypeStruct((1, BLK), F32),
+            jax.ShapeDtypeStruct((copies, BLK), F32),
         ],
         scratch_shapes=[
             pltpu.VMEM(split.shape, BF16),
@@ -405,7 +379,8 @@
 
 
 def final_kernel(
-    both_ref, chosen_ref, high_hbm, low_hbm, vectors_ref, directions_ref, ritz_ref, high_ref, low_ref, work, raw, inverse, arrived, *, factor
+    info, summed_ref, theirs_ref, chosen_ref, high_hbm, low_hbm, vectors_ref, directions_ref, ritz_ref,
+    high_ref, low_ref, work, raw, inverse, arrived, *, factor
 ):
     copies = [
         pltpu.make_async_copy(high_hbm, high_ref, arrived.at[0]),
@@ -413,11 +388,14 @@
     ]
     for copy in copies:
         copy.start()
+    first = info[0] == 0
     for at in range(6):
+        mine = first if at % 2 == 0 else jnp.logical_not(first)
         for base, target in ((0, work), (96, raw)):
-            row = 384 * (at % 2) + base + 32 * (at // 2)
-            target[32 * at : 32 * at + 32, 0:BLK] = both_ref[row : row + 32, :]
-            target[32 * at : 32 * at + 32, BLK:192] = both_ref[row + 192 : row + 224, 0:64]
+            row = base + 32 * (at // 2)
+            head, tail = slice(row, row + 32), slice(row + 192, row + 224)
+            target[32 * at : 32 * at + 32, 0:BLK] = jnp.where(mine, summed_ref[head, :], theirs_ref[head, :])
+            target[32 * at : 32 * at + 32, BLK:192] = jnp.where(mine, summed_ref[tail, 0:64], theirs_ref[tail, 0:64])
     inverse_cholesky(work, inverse)
     whole_inverse = inverse[...]
     half = exact(whole_inverse, raw[...], ((1,), (1,)))
@@ -435,16 +413,16 @@
         directions_ref[:, lanes] = product[32:64]
 
 
-def final(both, chosen, high, low, factor):
+def final(info, summed, theirs, chosen, high, low, factor):
     return pl.pallas_call(
         functools.partial(final_kernel, factor=factor),
-        in_specs=memory(pltpu.VMEM, pltpu.VMEM, pl.ANY, pl.ANY),
+        in_specs=memory(pltpu.SMEM, pltpu.VMEM, pltpu.VMEM, pltpu.VMEM, pl.ANY, pl.ANY),
         out_shape=[jax.ShapeDtypeStruct((32, high.shape[1]), F32)] * 2 + [jax.ShapeDtypeStruct((192, 192), F32)],
         scratch_shapes=[pltpu.VMEM(high.shape, BF16)] * 2 + [pltpu.VMEM((192, 192), F32)] * 3 + [pltpu.SemaphoreType.DMA((2,))],
         compiler_params=pltpu.CompilerParams(vmem_limit_bytes=VMEM_LIMIT),
         cost_estimate=pl.CostEstimate(flops=4 * 10**8, bytes_accessed=4 * 10**6, transcendentals=0),
         name="final",
-    )(both, chosen, high, low)
+    )(info, summed, theirs, chosen, high, low)
 
 
 def other_core(x):
@@ -469,20 +447,18 @@
     ps_odd, ps_even = from_neighbours(ps)
     x_other = other_core(vectors)
     p_other = other_core(directions)
-    y, ys, sums = first_image(info, columns, split, vectors, xs, xs_odd, xs_even, scale)
+    y, ys, sums = first_image(info, columns, split, vectors, xs, xs_odd, xs_even, scale, 2 * devices)
     ys_odd, ys_even = from_neighbours(ys)
     y_other = other_core(y)
-    half = sums[:, 0:64]
-    blank = jnp.zeros_like(half)
-    row = jnp.where(core == 0, jnp.concatenate([half, blank], axis=1), jnp.concatenate([blank, half], axis=1))
-    sums = lax.all_to_all(repeated(row, 2 * devices), ("rows", "cols"), 0, 0).reshape(2 * devices, BLK)
+    sums = lax.all_to_all(sums.reshape(2 * devices, 1, BLK), ("rows", "cols"), 0, 0).reshape(2 * devices, BLK)
     z, image = second_image(info, columns, split, ys, ys_odd, ys_even, ps, ps_odd, ps_even, scale, y, directions)
     high, low, part = products(info, sums, vectors, y, directions, x_other, y_other, p_other, z, image)
-    both = sum_large(part.reshape(16, 24, BLK)).reshape(768, BLK)
+    summed = sum_large(part.reshape(16, 24, BLK)).reshape(384, BLK)
+    theirs = other_core(summed)
     mine = lambda m: lax.dynamic_slice_in_dim(m, core * width, width, 1)
     kept = jnp.concatenate([rotation[:total], jnp.zeros((total, total), F32), rotation[2 * total :]], axis=0)
     chosen = jnp.concatenate([mine(rotation), mine(kept)], axis=1).T
-    new_vectors, new_directions, ritz_matrix = final(both, chosen, high, low, math.sqrt(nodes))
+    new_vectors, new_directions, ritz_matrix = final(info, summed, theirs, chosen, high, low, math.sqrt(nodes))
     return new_vectors, new_directions, ritz_matrix
 
 

time: 125 us -> 123 us (0.984)
  blocking collectives: 24.7 us -> 10.4 us
  starting transfers between devices: 32.8 us -> 40.7 us
  waiting for transfers between devices: 13.1 us -> 19.1 us
    all_to_all x2 -> x1, blocking collectives: 24.7 us -> 10.4 us  [exchange(): return lax.all_to_all(x, 'rows', 0, 0, axis_index_groups=groups)]
    ppermute x3 -> x4, starting transfers between devices: 2.11 us -> 6.42 us  [other_core(): return lax.ppermute(x, 'cols', [(0, 1), (1, 0)])]
    all_to_all x2 -> x3, waiting for transfers between devices: 13.1 us -> 17.1 us  [the longest x2 14.5 us: exchange(): return lax.all_to_all(x, 'rows', 0, 0, axis_index_groups=groups)]
    all_to_all x2 -> x3, starting transfers between devices: 12.5 us -> 16.1 us  [the longest x2 10.4 us: exchange(): return lax.all_to_all(x, 'rows', 0, 0, axis_index_groups=groups)]
    ppermute x6, waiting for transfers between devices: 0.02 us -> 1.54 us  [from_neighbours(): return [lax.ppermute(x, 'rows', swaps(devices, first)) for first in (1, 0)]]
  transfers between devices with their start and end apart: 11 -> 13, of which waited for: 2 -> 5; matrix products, arithmetic and copies ran while one was open for 2% -> 1% of each run, Pallas kernels for 20% -> 20%
where the time goes in v8:
time: 123 us
  Pallas kernels  45.5 us (37%)
  starting transfers between devices  40.7 us (33%)
  waiting for transfers between devices  19.1 us (16%)
  blocking collectives  10.4 us (8%)
  local copies, waits for them, and re-layouts  4.54 us (4%)
    ppermute x6, starting transfers between devices, from_neighbours(): return [lax.ppermute(x, 'rows', swaps(devices, first)) for first in (1, 0)]  18.2 us
    all_to_all x2, waiting for transfers between devices, exchange(): return lax.all_to_all(x, 'rows', 0, 0, axis_index_groups=groups)  14.5 us
    all_to_all x1, blocking collectives, exchange(): return lax.all_to_all(x, 'rows', 0, 0, axis_index_groups=groups)  10.4 us
    all_to_all x2, starting transfers between devices, exchange(): return lax.all_to_all(x, 'rows', 0, 0, axis_index_groups=groups)  10.4 us
    pallas_call x1, Pallas kernels, final(): pl.pallas_call(functools.partial(final_kernel, factor=factor), in_specs=m...  10.3 us
    pallas_call x1, Pallas kernels, split_affinity(): pl.pallas_call(split_kernel, in_specs=memory(pl.ANY, pltpu.VMEM, pltpu.VM...  8.89 us
    pallas_call x1, Pallas kernels, second_image(): pl.pallas_call(second_kernel, in_specs=memory(pltpu.SMEM, pltpu.SMEM, pl....  7.96 us
    pallas_call x1, Pallas kernels, first_image(): pl.pallas_call(first_kernel, in_specs=memory(pltpu.SMEM, pltpu.SMEM, pl.A...  7.49 us
  transfers between devices with their start and end apart: 13, of which 5 were waited for; matrix products, arithmetic and copies ran while one was open for 1% of the time, Pallas kernels for 20%

profile of v8, /device:TPU:1, one launch (start us, length us, event | category | flops | bytes accessed | tf_op | source)
XLA Modules:
  0.0 122.6 jit_solution(12360709845372628153)
XLA Ops:
  0.6 5.8 %degrees.1 = (f32[24,128]{1,0:T(8,128)}, f32[32,3072]{1,0:T(8,128)}) custom-call(f32[24,6,128,128]{3,2,1,0:T(8,128)} %a_hbm.3, f32[32,3072]{1,0:T(8,128)} %x_ref.5), custom_call_target="tpu_custom_call" | custom-call | flops 10000000 | bytes 10000000 | tf_op jit(solution)/shard_map/degrees/pallas_call | solution.py:96
  6.4 11.1 %collective-permute-start = (f32[32,3072]{1,0:T(8,128)}, f32[32,3072]{1,0:T(8,128)S(1)}, u32[]{:S(2)}, u32[]{:S(2)}) collective-permute-start(f32[32,3072]{1,0:T(8,128)} %get-tuple-element.17.xs_ref), channel_id=1, source_target_pairs={{2,4},{4,2},{6,8},{8,6},{10,12},{12,10},{14,16},{16,14},{18,20},{2... | collective-permute-start | bytes 1179656 | tf_op jit(solution)/shard_map/ppermute | solution.py:35
  17.6 8.9 %split.1 = (bf16[24,256,768]{2,1,0:T(8,128)(2,1)}, f32[32,3072]{1,0:T(8,128)}) custom-call(f32[24,6,128,128]{3,2,1,0:T(8,128)} %a_hbm.3, f32[24,128]{1,0:T(8,128)} %get-tuple-element.15.scale_ref.s_ref, f32[32,3072]{1,0:T(8,128)} %p_ref.5), custom_call_target="tpu_custom_call" | custom-call | flops 10000000 | bytes 19000000 | tf_op jit(solution)/shard_map/split/pallas_call | solution.py:130
  26.5 0.7 collective-permute-start.7
  27.2 0.9 collective-permute-start.8
  28.2 0.6 pad_add_fusion.info
  28.7 0.8 copy-done.8
  29.5 0.1 copy-done.9
  29.6 7.5 %first_image.1 = (f32[32,3072]{1,0:T(8,128)}, f32[32,3072]{1,0:T(8,128)}, f32[256,128]{1,0:T(8,128)}) custom-call(s32[4]{0:T(128)} %pad_add_fusion.info, s32[6,24]{1,0:T(8,128)} %bitcast.17, bf16[24,256,768]{2,1,0:T(8,128)(2,1)} %get-tuple-element.16.a_hbm, f32[32,3072]{1,0:T(8,128)} %x_ref.5, f32[32,3072]{1,0:T(8,128)} %get-tuple-element.17.xs_ref, ...), custom_call_target="tpu_custom_call" | custom-call | flops 4000000000 | bytes 11000000 | tf_op jit(solution)/shard_map/first_image/pallas_call | solution.py:205
  37.1 5.4 %collective-permute-start.5 = (f32[32,3072]{1,0:T(8,128)}, f32[32,3072]{1,0:T(8,128)S(1)}, u32[]{:S(2)}, u32[]{:S(2)}) collective-permute-start(f32[32,3072]{1,0:T(8,128)} %get-tuple-element.20.ys_ref), channel_id=1, source_target_pairs={{2,4},{4,2},{6,8},{8,6},{10,12},{12,10},{14,16},{16,14},{18,20},{2... | collective-permute-start | bytes 1179656 | tf_op jit(solution)/shard_map/ppermute | solution.py:35
  42.6 1.5 %collective-permute-start.2 = (f32[32,3072]{1,0:T(8,128)S(1)}, f32[32,3072]{1,0:T(8,128)S(1)}, u32[]{:S(2)}, u32[]{:S(2)}) collective-permute-start(f32[32,3072]{1,0:T(8,128)S(1)} %copy-done.1), channel_id=1, source_target_pairs={{0,1},{1,0},{2,3},{3,2},{4,5},{5,4},{6,7},{7,6},{8,9},{9,8},{10,11... | collective-permute-start | bytes 1179656 | tf_op jit(solution)/shard_map/ppermute | solution.py:429
  44.2 0.5 collective-permute-start.3
  44.7 5.7 %all-to-all-start = ((f32[256,1,128]{2,1,0:T(1,128)}), f32[256,1,128]{2,1,0:T(1,128)S(1)}, u32[]{:S(2)}, u32[]{:S(2)}) async-start(f32[256,1,128]{2,1,0:T(1,128)} %bitcast.15), calls=%async_computation | async-start | bytes 262144 | tf_op jit(solution)/shard_map/all_to_all | solution.py:453
  50.4 1.5 %collective-permute-done.5.ys_odd_ref = f32[32,3072]{1,0:T(8,128)S(1)} collective-permute-done((f32[32,3072]{1,0:T(8,128)}, f32[32,3072]{1,0:T(8,128)S(1)}, u32[]{:S(2)}, u32[]{:S(2)}) %collective-permute-start.5) | collective-permute-done | bytes 393248 | tf_op jit(solution)/shard_map/ppermute | solution.py:35
  52.0 0.7 copy-done.13
  52.7 8.0 %second_image.1 = (f32[32,3072]{1,0:T(8,128)}, f32[32,3072]{1,0:T(8,128)}) custom-call(s32[4]{0:T(128)} %pad_add_fusion.info, s32[6,24]{1,0:T(8,128)} %bitcast.18, bf16[24,256,768]{2,1,0:T(8,128)(2,1)} %get-tuple-element.16.a_hbm, f32[32,3072]{1,0:T(8,128)} %get-tuple-element.20.ys_ref, f32[32,3072]{1,0:T(8,128)} %copy-done.13, ...), custom_call_target="tpu_custom_call" | custom-call | flops 4000000000 | bytes 14000000 | tf_op jit(solution)/shard_map/second_image/pallas_call | solution.py:244
  60.7 2.6 %all-to-all-done = f32[256,1,128]{2,1,0:T(1,128)S(1)} async-done(((f32[256,1,128]{2,1,0:T(1,128)}), f32[256,1,128]{2,1,0:T(1,128)S(1)}, u32[]{:S(2)}, u32[]{:S(2)}) %all-to-all-start) | async-done | bytes 131104 | tf_op jit(solution)/shard_map/all_to_all | solution.py:453
  63.4 0.6 copy-done.5
  64.0 0.1 copy-done.12
  64.1 5.0 %products.1 = (bf16[192,3072]{1,0:T(8,128)(2,1)}, bf16[192,3072]{1,0:T(8,128)(2,1)}, f32[384,128]{1,0:T(8,128)}) custom-call(s32[4]{0:T(128)} %pad_add_fusion.info, f32[256,128]{1,0:T(8,128)} %bitcast.16, f32[32,3072]{1,0:T(8,128)} %x_ref.5, f32[32,3072]{1,0:T(8,128)} %get-tuple-element.19.y_ref, f32[32,3072]{1,0:T(8,128)} %p_ref.5, f32[32,3072]{1,0:T(8,128)} %copy-done.10, ...), custom_call_target="tpu_custom_call" | custom-call | flops 2000000000 | bytes 6000000 | tf_op jit(solution)/shard_map/products/pallas_call | solution.py:302
  69.2 10.4 %all_to_all.20 = f32[16,24,128]{2,1,0:T(8,128)S(1)} all-to-all(f32[16,24,128]{2,1,0:T(8,128)} %bitcast.14), channel_id=1, replica_groups={{0,2,4,6,8,10,12,14,16,18,20,22,24,26,28,30},{32,34,36,38,40,42,44,46,4..., dimensions={0} | all-to-all | bytes 393216 | tf_op jit(solution)/shard_map/all_to_all | solution.py:51
  79.6 0.6 broadcast_in_dim.6
  80.3 6.8 %all-to-all-start.2 = ((f32[8,24,128]{2,1,0:T(8,128)}), f32[8,24,128]{2,1,0:T(8,128)S(1)}, u32[]{:S(2)}, u32[]{:S(2)}) async-start(f32[8,24,128]{2,1,0:T(8,128)} %broadcast_in_dim.6), calls=%async_computation.2 | async-start | bytes 196608 | tf_op jit(solution)/shard_map/all_to_all | solution.py:51
  87.2 7.6 %all-to-all-done.2 = f32[8,24,128]{2,1,0:T(8,128)S(1)} async-done(((f32[8,24,128]{2,1,0:T(8,128)}), f32[8,24,128]{2,1,0:T(8,128)S(1)}, u32[]{:S(2)}, u32[]{:S(2)}) %all-to-all-start.2) | async-done | bytes 98336 | tf_op jit(solution)/shard_map/all_to_all | solution.py:51
  94.8 0.7 broadcast_in_dim.7
  95.5 3.5 %all-to-all-start.3 = ((f32[16,24,128]{2,1,0:T(8,128)}), f32[16,24,128]{2,1,0:T(8,128)S(1)}, u32[]{:S(2)}, u32[]{:S(2)}) async-start(f32[16,24,128]{2,1,0:T(8,128)} %broadcast_in_dim.7), calls=%async_computation.3 | async-start | bytes 393216 | tf_op jit(solution)/shard_map/all_to_all | solution.py:51
  99.1 6.9 %all-to-all-done.3 = f32[16,24,128]{2,1,0:T(8,128)S(1)} async-done(((f32[16,24,128]{2,1,0:T(8,128)}), f32[16,24,128]{2,1,0:T(8,128)S(1)}, u32[]{:S(2)}, u32[]{:S(2)}) %all-to-all-start.3) | async-done | bytes 196640 | tf_op jit(solution)/shard_map/all_to_all | solution.py:51
  106.0 4.3 %collective-permute-start.9 = (f32[384,128]{1,0:T(8,128)S(1)}, f32[384,128]{1,0:T(8,128)S(1)}, u32[]{:S(2)}, u32[]{:S(2)}) collective-permute-start(f32[384,128]{1,0:T(8,128)S(1)} %bitcast.12), channel_id=1, source_target_pairs={{0,1},{1,0},{2,3},{3,2},{4,5},{5,4},{6,7},{7,6},{8,9},{9,8},{10,11... | collective-permute-start | bytes 589832 | tf_op jit(solution)/shard_map/ppermute | solution.py:429
  110.3 0.6 maximum_bitcast_fusion.chosen_ref
  110.9 0.4 collective-permute-done.9.theirs_ref
  111.4 0.7 copy-done.3
  112.0 10.3 %final.1 = (f32[32,3072]{1,0:T(8,128)}, f32[32,3072]{1,0:T(8,128)}, f32[192,192]{1,0:T(8,128)}) custom-call(s32[4]{0:T(128)} %pad_add_fusion.info, f32[384,128]{1,0:T(8,128)} %bitcast.13, f32[384,128]{1,0:T(8,128)} %copy-done.3, f32[64,192]{1,0:T(8,128)} %maximum_bitcast_fusion.chosen_ref, bf16[192,3072]{1,0:T(8,128)(2,1)} %get-tuple-element.25.high_hbm, ...), custom_call_target="tpu_custom_call" | custom-call | flops 400000000 | bytes 4000000 | tf_op jit(solution)/shard_map/final/pallas_call | solution.py:417
  (39 shorter events, 0.3 us)
Async XLA Ops:
  6.4 22.3 %collective-permute-start = (f32[32,3072]{1,0:T(8,128)}, f32[32,3072]{1,0:T(8,128)S(1)}, u32[]{:S(2)}, u32[]{:S(2)}) collective-permute-start(f32[32,3072]{1,0:T(8,128)} %get-tuple-element.17.xs_ref), channel_id=1, source_target_pairs={{2,4},{4,2},{6,8},{8,6},{10,12},{12,10},{14,16},{16,14},{18,20},{2... | collective-permute-start | bytes 1179656 | tf_op jit(solution)/shard_map/ppermute | solution.py:35
  17.6 11.1 %collective-permute-start.1 = (f32[32,3072]{1,0:T(8,128)}, f32[32,3072]{1,0:T(8,128)S(1)}, u32[]{:S(2)}, u32[]{:S(2)}) collective-permute-start(f32[32,3072]{1,0:T(8,128)} %get-tuple-element.17.xs_ref), channel_id=1, source_target_pairs={{0,2},{2,0},{4,6},{6,4},{8,10},{10,8},{12,14},{14,12},{16,18},{18,... | collective-permute-start | bytes 1179656 | tf_op jit(solution)/shard_map/ppermute | solution.py:35
  26.5 16.1 %copy-start.1 = (f32[32,3072]{1,0:T(8,128)S(1)}, f32[32,3072]{1,0:T(8,128)}, u32[]{:S(2)}) copy-start(f32[32,3072]{1,0:T(8,128)} %x_ref.5) | copy-start | bytes 1179652
  26.5 17.6 %copy-start.2 = (f32[32,3072]{1,0:T(8,128)S(1)}, f32[32,3072]{1,0:T(8,128)}, u32[]{:S(2)}) copy-start(f32[32,3072]{1,0:T(8,128)} %p_ref.5) | copy-start | bytes 1179652
  26.5 17.6 %collective-permute-start.7 = (f32[32,3072]{1,0:T(8,128)}, f32[32,3072]{1,0:T(8,128)S(1)}, u32[]{:S(2)}, u32[]{:S(2)}) collective-permute-start(f32[32,3072]{1,0:T(8,128)} %get-tuple-element.21.ps_ref), channel_id=1, source_target_pairs={{2,4},{4,2},{6,8},{8,6},{10,12},{12,10},{14,16},{16,14},{18,20},{2... | collective-permute-start | bytes 1179656 | tf_op jit(solution)/shard_map/ppermute | solution.py:35
  27.2 17.0 %collective-permute-start.8 = (f32[32,3072]{1,0:T(8,128)}, f32[32,3072]{1,0:T(8,128)S(1)}, u32[]{:S(2)}, u32[]{:S(2)}) collective-permute-start(f32[32,3072]{1,0:T(8,128)} %get-tuple-element.21.ps_ref), channel_id=1, source_target_pairs={{0,2},{2,0},{4,6},{6,4},{8,10},{10,8},{12,14},{14,12},{16,18},{18,... | collective-permute-start | bytes 1179656 | tf_op jit(solution)/shard_map/ppermute | solution.py:35
  28.7 0.8 copy-start.8
  28.7 0.9 copy-start.9
  37.1 14.8 %collective-permute-start.5 = (f32[32,3072]{1,0:T(8,128)}, f32[32,3072]{1,0:T(8,128)S(1)}, u32[]{:S(2)}, u32[]{:S(2)}) collective-permute-start(f32[32,3072]{1,0:T(8,128)} %get-tuple-element.20.ys_ref), channel_id=1, source_target_pairs={{2,4},{4,2},{6,8},{8,6},{10,12},{12,10},{14,16},{16,14},{18,20},{2... | collective-permute-start | bytes 1179656 | tf_op jit(solution)/shard_map/ppermute | solution.py:35
  42.5 9.4 %collective-permute-start.6 = (f32[32,3072]{1,0:T(8,128)}, f32[32,3072]{1,0:T(8,128)}, u32[]{:S(2)}, u32[]{:S(2)}) collective-permute-start(f32[32,3072]{1,0:T(8,128)} %get-tuple-element.20.ys_ref), channel_id=1, source_target_pairs={{0,2},{2,0},{4,6},{6,4},{8,10},{10,8},{12,14},{14,12},{16,18},{18,... | collective-permute-start | bytes 1179656 | tf_op jit(solution)/shard_map/ppermute | solution.py:35
  42.6 18.1 %collective-permute-start.2 = (f32[32,3072]{1,0:T(8,128)S(1)}, f32[32,3072]{1,0:T(8,128)S(1)}, u32[]{:S(2)}, u32[]{:S(2)}) collective-permute-start(f32[32,3072]{1,0:T(8,128)S(1)} %copy-done.1), channel_id=1, source_target_pairs={{0,1},{1,0},{2,3},{3,2},{4,5},{5,4},{6,7},{7,6},{8,9},{9,8},{10,11... | collective-permute-start | bytes 1179656 | tf_op jit(solution)/shard_map/ppermute | solution.py:429
  44.1 7.9 %copy-start.6 = (f32[32,3072]{1,0:T(8,128)}, f32[32,3072]{1,0:T(8,128)S(1)}, u32[]{:S(2)}) copy-start(f32[32,3072]{1,0:T(8,128)S(1)} %collective-permute-done.7.ps_odd_ref) | copy-start | bytes 1179652
  44.1 16.6 %collective-permute-start.4 = (f32[32,3072]{1,0:T(8,128)S(1)}, f32[32,3072]{1,0:T(8,128)S(1)}, u32[]{:S(2)}, u32[]{:S(2)}) collective-permute-start(f32[32,3072]{1,0:T(8,128)S(1)} %copy-done.2), channel_id=1, source_target_pairs={{0,1},{1,0},{2,3},{3,2},{4,5},{5,4},{6,7},{7,6},{8,9},{9,8},{10,11... | collective-permute-start | bytes 1179656 | tf_op jit(solution)/shard_map/ppermute | solution.py:429
  44.2 7.8 %copy-start.7 = (f32[32,3072]{1,0:T(8,128)}, f32[32,3072]{1,0:T(8,128)S(1)}, u32[]{:S(2)}) copy-start(f32[32,3072]{1,0:T(8,128)S(1)} %collective-permute-done.8.ps_even_ref) | copy-start | bytes 1179652
  44.2 19.1 %collective-permute-start.3 = (f32[32,3072]{1,0:T(8,128)}, f32[32,3072]{1,0:T(8,128)S(1)}, u32[]{:S(2)}, u32[]{:S(2)}) collective-permute-start(f32[32,3072]{1,0:T(8,128)} %get-tuple-element.19.y_ref), channel_id=1, source_target_pairs={{0,1},{1,0},{2,3},{3,2},{4,5},{5,4},{6,7},{7,6},{8,9},{9,8},{10,11... | collective-permute-start | bytes 1179656 | tf_op jit(solution)/shard_map/ppermute | solution.py:429
  44.7 18.6 %all-to-all-start = ((f32[256,1,128]{2,1,0:T(1,128)}), f32[256,1,128]{2,1,0:T(1,128)S(1)}, u32[]{:S(2)}, u32[]{:S(2)}) async-start(f32[256,1,128]{2,1,0:T(1,128)} %bitcast.15), calls=%async_computation | async-start | bytes 262144 | tf_op jit(solution)/shard_map/all_to_all | solution.py:453
  50.4 48.6 %copy-start.4 = (f32[192,64]{0,1:T(8,128)S(1)}, f32[192,64]{0,1:T(8,128)}, u32[]{:S(2)}) copy-start(f32[192,64]{0,1:T(8,128)} %param.9) | copy-start | bytes 147460
  51.9 0.7 copy-start.13
  60.7 2.7 %copy-start.10 = (f32[32,3072]{1,0:T(8,128)}, f32[32,3072]{1,0:T(8,128)S(1)}, u32[]{:S(2)}) copy-start(f32[32,3072]{1,0:T(8,128)S(1)} %collective-permute-done.2.xo_ref) | copy-start | bytes 1179652
  60.7 2.6 %copy-start.11 = (f32[32,3072]{1,0:T(8,128)}, f32[32,3072]{1,0:T(8,128)S(1)}, u32[]{:S(2)}) copy-start(f32[32,3072]{1,0:T(8,128)S(1)} %collective-permute-done.4.po_ref) | copy-start | bytes 1179652
  63.3 0.6 copy-start.5
  63.3 0.8 copy-start.12
  80.3 14.5 %all-to-all-start.2 = ((f32[8,24,128]{2,1,0:T(8,128)}), f32[8,24,128]{2,1,0:T(8,128)S(1)}, u32[]{:S(2)}, u32[]{:S(2)}) async-start(f32[8,24,128]{2,1,0:T(8,128)} %broadcast_in_dim.6), calls=%async_computation.2 | async-start | bytes 196608 | tf_op jit(solution)/shard_map/all_to_all | solution.py:51
  95.5 10.5 %all-to-all-start.3 = ((f32[16,24,128]{2,1,0:T(8,128)}), f32[16,24,128]{2,1,0:T(8,128)S(1)}, u32[]{:S(2)}, u32[]{:S(2)}) async-start(f32[16,24,128]{2,1,0:T(8,128)} %broadcast_in_dim.7), calls=%async_computation.3 | async-start | bytes 393216 | tf_op jit(solution)/shard_map/all_to_all | solution.py:51
  106.0 5.4 %copy-start = (f32[16,24,128]{2,1,0:T(8,128)}, f32[16,24,128]{2,1,0:T(8,128)S(1)}, u32[]{:S(2)}) copy-start(f32[16,24,128]{2,1,0:T(8,128)S(1)} %all-to-all-done.3) | copy-start | bytes 589828
  106.0 5.4 %collective-permute-start.9 = (f32[384,128]{1,0:T(8,128)S(1)}, f32[384,128]{1,0:T(8,128)S(1)}, u32[]{:S(2)}, u32[]{:S(2)}) collective-permute-start(f32[384,128]{1,0:T(8,128)S(1)} %bitcast.12), channel_id=1, source_target_pairs={{0,1},{1,0},{2,3},{3,2},{4,5},{5,4},{6,7},{7,6},{8,9},{9,8},{10,11... | collective-permute-start | bytes 589832 | tf_op jit(solution)/shard_map/ppermute | solution.py:429
  111.4 0.7 copy-start.3

commit v9 on v8

--- a/solution.py
+++ b/solution.py
@@ -98,7 +98,7 @@
         in_specs=memory(pl.ANY, pltpu.VMEM),
         out_shape=[jax.ShapeDtypeStruct((n, BLK), F32), jax.ShapeDtypeStruct(x.shape, F32)],
         scratch_shapes=[pltpu.VMEM(affinity.shape, F32), pltpu.SemaphoreType.DMA((n,))],
-        compiler_params=pltpu.CompilerParams(vmem_limit_bytes=VMEM_LIMIT),
+        compiler_params=pltpu.CompilerParams(vmem_limit_bytes=60 * 2**20),
         cost_estimate=pl.CostEstimate(flops=10**7, bytes_accessed=10**7, transcendentals=3072),
         name="degrees",
     )(affinity, x)
@@ -138,7 +138,7 @@
             pltpu.SemaphoreType.DMA((n,)),
             pltpu.SemaphoreType.DMA((n,)),
         ],
-        compiler_params=pltpu.CompilerParams(vmem_limit_bytes=VMEM_LIMIT),
+        compiler_params=pltpu.CompilerParams(vmem_limit_bytes=60 * 2**20),
         cost_estimate=pl.CostEstimate(flops=10**7, bytes_accessed=19 * 10**6, transcendentals=0),
         name="split",
     )(affinity, scale, p)
@@ -215,7 +215,7 @@
             pltpu.VMEM((3 * n, BLK, BLK), BF16),
             pltpu.SemaphoreType.DMA((n,)),
         ],
-        compiler_params=pltpu.CompilerParams(vmem_limit_bytes=VMEM_LIMIT),
+        compiler_params=pltpu.CompilerParams(vmem_limit_bytes=52 * 2**20),
         cost_estimate=pl.CostEstimate(flops=4 * 10**9, bytes_accessed=11 * 10**6, transcendentals=0),
         name="first_image",
     )(info, pattern, split, x, xs, across_odd, across_even, s)
@@ -250,7 +250,7 @@
             pltpu.VMEM((3 * n, BLK, BLK), BF16),
             pltpu.SemaphoreType.DMA((n,)),
         ],
-        compiler_params=pltpu.CompilerParams(vmem_limit_bytes=VMEM_LIMIT),
+        compiler_params=pltpu.CompilerParams(vmem_limit_bytes=52 * 2**20),
         cost_estimate=pl.CostEstimate(flops=4 * 10**9, bytes_accessed=14 * 10**6, transcendentals=0),
         name="second_image",
     )(info, pattern, split, ys, ys_odd, ys_even, ps, ps_odd, ps_even, s, y, p)
@@ -308,7 +308,7 @@
             pltpu.VMEM((384, CHUNK * BLK), BF16),
             pltpu.VMEM((384, 192), F32),
         ],
-        compiler_params=pltpu.CompilerParams(vmem_limit_bytes=VMEM_LIMIT),
+        compiler_params=pltpu.CompilerParams(vmem_limit_bytes=24 * 2**20),
         cost_estimate=pl.CostEstimate(flops=2 * 10**9, bytes_accessed=6 * 10**6, transcendentals=0),
         name="products",
     )(info, sums, x, y, p, xo, yo, po, z, image)
@@ -419,7 +419,7 @@
         in_specs=memory(pltpu.SMEM, pltpu.VMEM, pltpu.VMEM, pltpu.VMEM, pl.ANY, pl.ANY),
         out_shape=[jax.ShapeDtypeStruct((32, high.shape[1]), F32)] * 2 + [jax.ShapeDtypeStruct((192, 192), F32)],
         scratch_shapes=[pltpu.VMEM(high.shape, BF16)] * 2 + [pltpu.VMEM((192, 192), F32)] * 3 + [pltpu.SemaphoreType.DMA((2,))],
-        compiler_params=pltpu.CompilerParams(vmem_limit_bytes=VMEM_LIMIT),
+        compiler_params=pltpu.CompilerParams(vmem_limit_bytes=24 * 2**20),
         cost_estimate=pl.CostEstimate(flops=4 * 10**8, bytes_accessed=4 * 10**6, transcendentals=0),
         name="final",
     )(info, summed, theirs, chosen, high, low)

time: 123 us -> 129 us (1.049)
  local copies, waits for them, and re-layouts: 4.54 us -> 15.2 us
  Pallas kernels: 45.5 us -> 41.8 us
  waiting for transfers between devices: 19.1 us -> 17 us
    unnamed x28 -> x46, local copies, waits for them, and re-layouts: 3.12 us -> 13 us
    pallas_call x1, Pallas kernels: 5.04 us -> 3.13 us  [products(): pl.pallas_call(products_kernel, in_specs=memory(pltpu.SMEM, *[pltpu.VMEM]...]
  transfers between devices with their start and end apart: 13 -> 13, of which waited for: 5 -> 5; matrix products, arithmetic and copies ran while one was open for 1% -> 1% of each run, Pallas kernels for 20% -> 18%
where the time goes in v9:
time: 129 us; the launch traced here: 128 us
  Pallas kernels  41.8 us (32%)
  starting transfers between devices  41.3 us (32%)
  waiting for transfers between devices  17 us (13%)
  local copies, waits for them, and re-layouts  15.2 us (12%)
  blocking collectives  10.7 us (8%)
    ppermute x6, starting transfers between devices, from_neighbours(): return [lax.ppermute(x, 'rows', swaps(devices, first)) for first in (1, 0)]  18.2 us
    all_to_all x2, waiting for transfers between devices, exchange(): return lax.all_to_all(x, 'rows', 0, 0, axis_index_groups=groups)  13.7 us
    unnamed x46, local copies, waits for them, and re-layouts  13 us
    all_to_all x2, starting transfers between devices, exchange(): return lax.all_to_all(x, 'rows', 0, 0, axis_index_groups=groups)  11 us
    all_to_all x1, blocking collectives, exchange(): return lax.all_to_all(x, 'rows', 0, 0, axis_index_groups=groups)  10.7 us
    pallas_call x1, Pallas kernels, final(): pl.pallas_call(functools.partial(final_kernel, factor=factor), in_specs=m...  9.76 us
    pallas_call x1, Pallas kernels, split_affinity(): pl.pallas_call(split_kernel, in_specs=memory(pl.ANY, pltpu.VMEM, pltpu.VM...  8.88 us
    pallas_call x1, Pallas kernels, first_image(): pl.pallas_call(first_kernel, in_specs=memory(pltpu.SMEM, pltpu.SMEM, pl.A...  7.16 us
  transfers between devices with their start and end apart: 13, of which 5 were waited for; matrix products, arithmetic and copies ran while one was open for 1% of the time, Pallas kernels for 18%

profile of v9, /device:TPU:1, one launch (start us, length us, event | category | flops | bytes accessed | tf_op | source)
XLA Modules:
  0.0 128.0 jit_solution(17570504379569953730)
XLA Ops:
  0.6 5.9 %degrees.1 = (f32[24,128]{1,0:T(8,128)}, f32[32,3072]{1,0:T(8,128)}) custom-call(f32[24,6,128,128]{3,2,1,0:T(8,128)} %a_hbm.3, f32[32,3072]{1,0:T(8,128)} %x_ref.5), custom_call_target="tpu_custom_call" | custom-call | flops 10000000 | bytes 10000000 | tf_op jit(solution)/shard_map/degrees/pallas_call | solution.py:96
  6.5 11.1 %collective-permute-start = (f32[32,3072]{1,0:T(8,128)}, f32[32,3072]{1,0:T(8,128)S(1)}, u32[]{:S(2)}, u32[]{:S(2)}) collective-permute-start(f32[32,3072]{1,0:T(8,128)} %get-tuple-element.17.xs_ref), channel_id=1, source_target_pairs={{2,4},{4,2},{6,8},{8,6},{10,12},{12,10},{14,16},{16,14},{18,20},{2... | collective-permute-start | bytes 1179656 | tf_op jit(solution)/shard_map/ppermute | solution.py:35
  17.7 8.9 %split.1 = (bf16[24,256,768]{2,1,0:T(8,128)(2,1)}, f32[32,3072]{1,0:T(8,128)}) custom-call(f32[24,6,128,128]{3,2,1,0:T(8,128)} %a_hbm.3, f32[24,128]{1,0:T(8,128)} %get-tuple-element.15.scale_ref.s_ref, f32[32,3072]{1,0:T(8,128)} %p_ref.5), custom_call_target="tpu_custom_call" | custom-call | flops 10000000 | bytes 19000000 | tf_op jit(solution)/shard_map/split/pallas_call | solution.py:130
  27.3 0.9 collective-permute-start.8
  28.3 0.8 copy-done.21
  29.2 7.2 %first_image.1 = (f32[32,3072]{1,0:T(8,128)S(1)}, f32[32,3072]{1,0:T(8,128)S(1)}, f32[256,128]{1,0:T(8,128)}) custom-call(s32[4]{0:T(128)S(1)} %pad_add_fusion.info, s32[6,24]{1,0:T(8,128)S(1)} %bitcast.16, bf16[24,256,768]{2,1,0:T(8,128)(2,1)} %get-tuple-element.16.a_hbm, f32[32,3072]{1,0:T(8,128)S(1)} %copy-done, f32[32,3072]{1,0:T(8,128)S(1)} %copy-done.6, ...), custom_call_target="tpu_custom_call" | custom-call | flops 4000000000 | bytes 11000000 | tf_op jit(solution)/shard_map/first_image/pallas_call | solution.py:205
  36.4 5.4 %collective-permute-start.5 = (f32[32,3072]{1,0:T(8,128)S(1)}, f32[32,3072]{1,0:T(8,128)}, u32[]{:S(2)}, u32[]{:S(2)}) collective-permute-start(f32[32,3072]{1,0:T(8,128)S(1)} %get-tuple-element.20.ys_ref), channel_id=1, source_target_pairs={{2,4},{4,2},{6,8},{8,6},{10,12},{12,10},{14,16},{16,14},{18,20},{2... | collective-permute-start | bytes 1179656 | tf_op jit(solution)/shard_map/ppermute | solution.py:35
  41.8 1.5 %collective-permute-start.2 = (f32[32,3072]{1,0:T(8,128)S(1)}, f32[32,3072]{1,0:T(8,128)S(1)}, u32[]{:S(2)}, u32[]{:S(2)}) collective-permute-start(f32[32,3072]{1,0:T(8,128)S(1)} %copy-done), channel_id=1, source_target_pairs={{0,1},{1,0},{2,3},{3,2},{4,5},{5,4},{6,7},{7,6},{8,9},{9,8},{10,11... | collective-permute-start | bytes 1179656 | tf_op jit(solution)/shard_map/ppermute | solution.py:429
  44.0 0.8 copy-done.20
  44.7 5.7 %all-to-all-start = ((f32[256,1,128]{2,1,0:T(1,128)}), f32[256,1,128]{2,1,0:T(1,128)S(1)}, u32[]{:S(2)}, u32[]{:S(2)}) async-start(f32[256,1,128]{2,1,0:T(1,128)} %bitcast.5), calls=%async_computation | async-start | bytes 262144 | tf_op jit(solution)/shard_map/all_to_all | solution.py:453
  51.1 7.1 %second_image.1 = (f32[32,3072]{1,0:T(8,128)S(1)}, f32[32,3072]{1,0:T(8,128)S(1)}) custom-call(s32[4]{0:T(128)S(1)} %pad_add_fusion.info, s32[6,24]{1,0:T(8,128)S(1)} %bitcast.17, bf16[24,256,768]{2,1,0:T(8,128)(2,1)} %get-tuple-element.16.a_hbm, f32[32,3072]{1,0:T(8,128)S(1)} %get-tuple-element.20.ys_ref, f32[32,3072]{1,0:T(8,128)} %collective-permute-done.5.ys_odd_ref, ...), custom_call_target="tpu_custom_call" | custom-call | flops 4000000000 | bytes 14000000 | tf_op jit(solution)/shard_map/second_image/pallas_call | solution.py:244
  59.0 0.8 copy-done.18
  60.5 0.8 copy-done.11
  61.2 2.3 %all-to-all-done = f32[256,1,128]{2,1,0:T(1,128)S(1)} async-done(((f32[256,1,128]{2,1,0:T(1,128)}), f32[256,1,128]{2,1,0:T(1,128)S(1)}, u32[]{:S(2)}, u32[]{:S(2)}) %all-to-all-start) | async-done | bytes 131104 | tf_op jit(solution)/shard_map/all_to_all | solution.py:453
  64.1 0.8 copy-done.13
  64.9 0.9 copy-done.4
  65.8 1.0 copy-done.8
  66.8 1.0 copy-done.10
  67.8 1.0 copy-done.12
  68.8 1.0 copy-done.14
  69.8 1.0 copy-done.17
  70.8 1.0 copy-done.19
  71.8 3.1 %products.1 = (bf16[192,3072]{1,0:T(8,128)(2,1)S(1)}, bf16[192,3072]{1,0:T(8,128)(2,1)S(1)}, f32[384,128]{1,0:T(8,128)S(1)}) custom-call(s32[4]{0:T(128)S(1)} %pad_add_fusion.info, f32[256,128]{1,0:T(8,128)S(1)} %bitcast.15, f32[32,3072]{1,0:T(8,128)S(1)} %copy-done, f32[32,3072]{1,0:T(8,128)S(1)} %copy-done.8, f32[32,3072]{1,0:T(8,128)S(1)} %copy-done.2, ...), custom_call_target="tpu_custom_call" | custom-call | flops 2000000000 | bytes 6000000 | tf_op jit(solution)/shard_map/products/pallas_call | solution.py:302
  74.9 10.7 %all_to_all.20 = f32[16,24,128]{2,1,0:T(8,128)S(1)} all-to-all(f32[16,24,128]{2,1,0:T(8,128)S(1)} %bitcast.14), channel_id=1, replica_groups={{0,2,4,6,8,10,12,14,16,18,20,22,24,26,28,30},{32,34,36,38,40,42,44,46,4..., dimensions={0} | all-to-all | bytes 393216 | tf_op jit(solution)/shard_map/all_to_all | solution.py:51
  86.3 7.4 %all-to-all-start.2 = ((f32[8,24,128]{2,1,0:T(8,128)}), f32[8,24,128]{2,1,0:T(8,128)S(1)}, u32[]{:S(2)}, u32[]{:S(2)}) async-start(f32[8,24,128]{2,1,0:T(8,128)} %broadcast_in_dim.6), calls=%async_computation.2 | async-start | bytes 196608 | tf_op jit(solution)/shard_map/all_to_all | solution.py:51
  93.9 7.6 %all-to-all-done.2 = f32[8,24,128]{2,1,0:T(8,128)S(1)} async-done(((f32[8,24,128]{2,1,0:T(8,128)}), f32[8,24,128]{2,1,0:T(8,128)S(1)}, u32[]{:S(2)}, u32[]{:S(2)}) %all-to-all-start.2) | async-done | bytes 98336 | tf_op jit(solution)/shard_map/all_to_all | solution.py:51
  102.2 3.5 %all-to-all-start.3 = ((f32[16,24,128]{2,1,0:T(8,128)}), f32[16,24,128]{2,1,0:T(8,128)S(1)}, u32[]{:S(2)}, u32[]{:S(2)}) async-start(f32[16,24,128]{2,1,0:T(8,128)} %broadcast_in_dim.7), calls=%async_computation.3 | async-start | bytes 393216 | tf_op jit(solution)/shard_map/all_to_all | solution.py:51
  105.7 0.8 fusion.2
  106.5 6.1 %all-to-all-done.3 = f32[16,24,128]{2,1,0:T(8,128)S(1)} async-done(((f32[16,24,128]{2,1,0:T(8,128)}), f32[16,24,128]{2,1,0:T(8,128)S(1)}, u32[]{:S(2)}, u32[]{:S(2)}) %all-to-all-start.3) | async-done | bytes 196640 | tf_op jit(solution)/shard_map/all_to_all | solution.py:51
  112.6 4.3 %collective-permute-start.9 = (f32[384,128]{1,0:T(8,128)S(1)}, f32[384,128]{1,0:T(8,128)S(1)}, u32[]{:S(2)}, u32[]{:S(2)}) collective-permute-start(f32[384,128]{1,0:T(8,128)S(1)} %bitcast.12), channel_id=1, source_target_pairs={{0,1},{1,0},{2,3},{3,2},{4,5},{5,4},{6,7},{7,6},{8,9},{9,8},{10,11... | collective-permute-start | bytes 589832 | tf_op jit(solution)/shard_map/ppermute | solution.py:429
  117.0 0.8 fusion.1
  118.0 9.8 %final.1 = (f32[32,3072]{1,0:T(8,128)}, f32[32,3072]{1,0:T(8,128)}, f32[192,192]{1,0:T(8,128)}) custom-call(s32[4]{0:T(128)S(1)} %pad_add_fusion.info, f32[384,128]{1,0:T(8,128)S(1)} %bitcast.13, f32[384,128]{1,0:T(8,128)S(1)} %collective-permute-done.9.theirs_ref, f32[64,192]{1,0:T(8,128)S(1)} %maximum_bitcast_fusion.chosen_ref, ...), custom_call_target="tpu_custom_call" | custom-call | flops 400000000 | bytes 4000000 | tf_op jit(solution)/shard_map/final/pallas_call | solution.py:417
  (57 shorter events, 6.2 us)
Async XLA Ops:
  0.6 28.6 %copy-start = (f32[32,3072]{1,0:T(8,128)S(1)}, f32[32,3072]{1,0:T(8,128)}, u32[]{:S(2)}) copy-start(f32[32,3072]{1,0:T(8,128)} %x_ref.5) | copy-start | bytes 1179652
  0.6 28.6 %copy-start.15 = (s32[24,6]{0,1:T(8,128)S(1)}, s32[24,6]{0,1:T(8,128)}, u32[]{:S(2)}) copy-start(s32[24,6]{0,1:T(8,128)} %param.8) | copy-start | bytes 1732
  6.5 22.7 %copy-start.5 = (f32[24,128]{1,0:T(8,128)S(1)}, f32[24,128]{1,0:T(8,128)}, u32[]{:S(2)}) copy-start(f32[24,128]{1,0:T(8,128)} %get-tuple-element.15.scale_ref.s_ref) | copy-start | bytes 36868
  6.5 22.7 %copy-start.6 = (f32[32,3072]{1,0:T(8,128)S(1)}, f32[32,3072]{1,0:T(8,128)}, u32[]{:S(2)}) copy-start(f32[32,3072]{1,0:T(8,128)} %get-tuple-element.17.xs_ref) | copy-start | bytes 1179652
  6.5 21.8 %collective-permute-start = (f32[32,3072]{1,0:T(8,128)}, f32[32,3072]{1,0:T(8,128)S(1)}, u32[]{:S(2)}, u32[]{:S(2)}) collective-permute-start(f32[32,3072]{1,0:T(8,128)} %get-tuple-element.17.xs_ref), channel_id=1, source_target_pairs={{2,4},{4,2},{6,8},{8,6},{10,12},{12,10},{14,16},{16,14},{18,20},{2... | collective-permute-start | bytes 1179656 | tf_op jit(solution)/shard_map/ppermute | solution.py:35
  17.7 10.6 %collective-permute-start.1 = (f32[32,3072]{1,0:T(8,128)}, f32[32,3072]{1,0:T(8,128)S(1)}, u32[]{:S(2)}, u32[]{:S(2)}) collective-permute-start(f32[32,3072]{1,0:T(8,128)} %get-tuple-element.17.xs_ref), channel_id=1, source_target_pairs={{0,2},{2,0},{4,6},{6,4},{8,10},{10,8},{12,14},{14,12},{16,18},{18,... | collective-permute-start | bytes 1179656 | tf_op jit(solution)/shard_map/ppermute | solution.py:35
  26.6 16.8 %copy-start.1 = (f32[32,3072]{1,0:T(8,128)S(1)}, f32[32,3072]{1,0:T(8,128)}, u32[]{:S(2)}) copy-start(f32[32,3072]{1,0:T(8,128)} %p_ref.5) | copy-start | bytes 1179652
  26.6 16.8 %collective-permute-start.7 = (f32[32,3072]{1,0:T(8,128)}, f32[32,3072]{1,0:T(8,128)}, u32[]{:S(2)}, u32[]{:S(2)}) collective-permute-start(f32[32,3072]{1,0:T(8,128)} %get-tuple-element.21.ps_ref), channel_id=1, source_target_pairs={{2,4},{4,2},{6,8},{8,6},{10,12},{12,10},{14,16},{16,14},{18,20},{2... | collective-permute-start | bytes 1179656 | tf_op jit(solution)/shard_map/ppermute | solution.py:35
  27.3 16.7 %collective-permute-start.8 = (f32[32,3072]{1,0:T(8,128)}, f32[32,3072]{1,0:T(8,128)S(1)}, u32[]{:S(2)}, u32[]{:S(2)}) collective-permute-start(f32[32,3072]{1,0:T(8,128)} %get-tuple-element.21.ps_ref), channel_id=1, source_target_pairs={{0,2},{2,0},{4,6},{6,4},{8,10},{10,8},{12,14},{14,12},{16,18},{18,... | collective-permute-start | bytes 1179656 | tf_op jit(solution)/shard_map/ppermute | solution.py:35
  28.3 0.8 copy-start.21
  28.3 0.9 copy-start.22
  36.4 14.7 %copy-start.7 = (f32[32,3072]{1,0:T(8,128)}, f32[32,3072]{1,0:T(8,128)S(1)}, u32[]{:S(2)}) copy-start(f32[32,3072]{1,0:T(8,128)S(1)} %get-tuple-element.19.y_ref) | copy-start | bytes 1179652
  36.4 28.5 %copy-start.2 = (f32[32,3072]{1,0:T(8,128)S(1)}, f32[32,3072]{1,0:T(8,128)}, u32[]{:S(2)}) copy-start(f32[32,3072]{1,0:T(8,128)} %p_ref.5) | copy-start | bytes 1179652
  36.4 14.7 %collective-permute-start.5 = (f32[32,3072]{1,0:T(8,128)S(1)}, f32[32,3072]{1,0:T(8,128)}, u32[]{:S(2)}, u32[]{:S(2)}) collective-permute-start(f32[32,3072]{1,0:T(8,128)S(1)} %get-tuple-element.20.ys_ref), channel_id=1, source_target_pairs={{2,4},{4,2},{6,8},{8,6},{10,12},{12,10},{14,16},{16,14},{18,20},{2... | collective-permute-start | bytes 1179656 | tf_op jit(solution)/shard_map/ppermute | solution.py:35
  41.8 9.3 %collective-permute-start.6 = (f32[32,3072]{1,0:T(8,128)S(1)}, f32[32,3072]{1,0:T(8,128)}, u32[]{:S(2)}, u32[]{:S(2)}) collective-permute-start(f32[32,3072]{1,0:T(8,128)S(1)} %get-tuple-element.20.ys_ref), channel_id=1, source_target_pairs={{0,2},{2,0},{4,6},{6,4},{8,10},{10,8},{12,14},{14,12},{16,18},{18,... | collective-permute-start | bytes 1179656 | tf_op jit(solution)/shard_map/ppermute | solution.py:35
  41.8 17.9 %collective-permute-start.2 = (f32[32,3072]{1,0:T(8,128)S(1)}, f32[32,3072]{1,0:T(8,128)S(1)}, u32[]{:S(2)}, u32[]{:S(2)}) collective-permute-start(f32[32,3072]{1,0:T(8,128)S(1)} %copy-done), channel_id=1, source_target_pairs={{0,1},{1,0},{2,3},{3,2},{4,5},{5,4},{6,7},{7,6},{8,9},{9,8},{10,11... | collective-permute-start | bytes 1179656 | tf_op jit(solution)/shard_map/ppermute | solution.py:429
  43.4 17.1 %collective-permute-start.4 = (f32[32,3072]{1,0:T(8,128)S(1)}, f32[32,3072]{1,0:T(8,128)S(1)}, u32[]{:S(2)}, u32[]{:S(2)}) collective-permute-start(f32[32,3072]{1,0:T(8,128)S(1)} %copy-done.1), channel_id=1, source_target_pairs={{0,1},{1,0},{2,3},{3,2},{4,5},{5,4},{6,7},{7,6},{8,9},{9,8},{10,11... | collective-permute-start | bytes 1179656 | tf_op jit(solution)/shard_map/ppermute | solution.py:429
  44.0 0.8 copy-start.20
  44.7 19.4 %collective-permute-start.3 = (f32[32,3072]{1,0:T(8,128)S(1)}, f32[32,3072]{1,0:T(8,128)S(1)}, u32[]{:S(2)}, u32[]{:S(2)}) collective-permute-start(f32[32,3072]{1,0:T(8,128)S(1)} %get-tuple-element.19.y_ref), channel_id=1, source_target_pairs={{0,1},{1,0},{2,3},{3,2},{4,5},{5,4},{6,7},{7,6},{8,9},{9,8},{10,11... | collective-permute-start | bytes 1179656 | tf_op jit(solution)/shard_map/ppermute | solution.py:429
  44.7 18.8 %all-to-all-start = ((f32[256,1,128]{2,1,0:T(1,128)}), f32[256,1,128]{2,1,0:T(1,128)S(1)}, u32[]{:S(2)}, u32[]{:S(2)}) async-start(f32[256,1,128]{2,1,0:T(1,128)} %bitcast.5), calls=%async_computation | async-start | bytes 262144 | tf_op jit(solution)/shard_map/all_to_all | solution.py:453
  58.9 0.8 copy-start.18
  64.1 0.8 copy-start.13
  64.9 0.9 copy-start.4
  65.8 1.0 copy-start.8
  66.8 1.0 copy-start.10
  67.8 1.0 copy-start.12
  68.8 1.0 copy-start.14
  69.8 1.0 copy-start.17
  70.8 1.0 copy-start.19
  86.3 15.1 %all-to-all-start.2 = ((f32[8,24,128]{2,1,0:T(8,128)}), f32[8,24,128]{2,1,0:T(8,128)S(1)}, u32[]{:S(2)}, u32[]{:S(2)}) async-start(f32[8,24,128]{2,1,0:T(8,128)} %broadcast_in_dim.6), calls=%async_computation.2 | async-start | bytes 196608 | tf_op jit(solution)/shard_map/all_to_all | solution.py:51
  102.2 10.5 %all-to-all-start.3 = ((f32[16,24,128]{2,1,0:T(8,128)}), f32[16,24,128]{2,1,0:T(8,128)S(1)}, u32[]{:S(2)}, u32[]{:S(2)}) async-start(f32[16,24,128]{2,1,0:T(8,128)} %broadcast_in_dim.7), calls=%async_computation.3 | async-start | bytes 393216 | tf_op jit(solution)/shard_map/all_to_all | solution.py:51
  112.6 5.4 %collective-permute-start.9 = (f32[384,128]{1,0:T(8,128)S(1)}, f32[384,128]{1,0:T(8,128)S(1)}, u32[]{:S(2)}, u32[]{:S(2)}) collective-permute-start(f32[384,128]{1,0:T(8,128)S(1)} %bitcast.12), channel_id=1, source_target_pairs={{0,1},{1,0},{2,3},{3,2},{4,5},{5,4},{6,7},{7,6},{8,9},{9,8},{10,11... | collective-permute-start | bytes 589832 | tf_op jit(solution)/shard_map/ppermute | solution.py:429
  (4 other events, 2.9 us)

commit v10 on v9

--- a/solution.py
+++ b/solution.py
@@ -215,7 +215,7 @@
             pltpu.VMEM((3 * n, BLK, BLK), BF16),
             pltpu.SemaphoreType.DMA((n,)),
         ],
-        compiler_params=pltpu.CompilerParams(vmem_limit_bytes=52 * 2**20),
+        compiler_params=pltpu.CompilerParams(vmem_limit_bytes=60 * 2**20),
         cost_estimate=pl.CostEstimate(flops=4 * 10**9, bytes_accessed=11 * 10**6, transcendentals=0),
         name="first_image",
     )(info, pattern, split, x, xs, across_odd, across_even, s)
@@ -250,7 +250,7 @@
             pltpu.VMEM((3 * n, BLK, BLK), BF16),
             pltpu.SemaphoreType.DMA((n,)),
         ],
-        compiler_params=pltpu.CompilerParams(vmem_limit_bytes=52 * 2**20),
+        compiler_params=pltpu.CompilerParams(vmem_limit_bytes=60 * 2**20),
         cost_estimate=pl.CostEstimate(flops=4 * 10**9, bytes_accessed=14 * 10**6, transcendentals=0),
         name="second_image",
     )(info, pattern, split, ys, ys_odd, ys_even, ps, ps_odd, ps_even, s, y, p)
@@ -308,7 +308,7 @@
             pltpu.VMEM((384, CHUNK * BLK), BF16),
             pltpu.VMEM((384, 192), F32),
         ],
-        compiler_params=pltpu.CompilerParams(vmem_limit_bytes=24 * 2**20),
+        compiler_params=pltpu.CompilerParams(vmem_limit_bytes=60 * 2**20),
         cost_estimate=pl.CostEstimate(flops=2 * 10**9, bytes_accessed=6 * 10**6, transcendentals=0),
         name="products",
     )(info, sums, x, y, p, xo, yo, po, z, image)
@@ -419,7 +419,7 @@
         in_specs=memory(pltpu.SMEM, pltpu.VMEM, pltpu.VMEM, pltpu.VMEM, pl.ANY, pl.ANY),
         out_shape=[jax.ShapeDtypeStruct((32, high.shape[1]), F32)] * 2 + [jax.ShapeDtypeStruct((192, 192), F32)],
         scratch_shapes=[pltpu.VMEM(high.shape, BF16)] * 2 + [pltpu.VMEM((192, 192), F32)] * 3 + [pltpu.SemaphoreType.DMA((2,))],
-        compiler_params=pltpu.CompilerParams(vmem_limit_bytes=24 * 2**20),
+        compiler_params=pltpu.CompilerParams(vmem_limit_bytes=52 * 2**20),
         cost_estimate=pl.CostEstimate(flops=4 * 10**8, bytes_accessed=4 * 10**6, transcendentals=0),
         name="final",
     )(info, summed, theirs, chosen, high, low)

time: 129 us -> 124 us (0.961)
  local copies, waits for them, and re-layouts: 15.2 us -> 5.13 us
  Pallas kernels: 41.8 us -> 45.5 us
  waiting for transfers between devices: 17 us -> 19.7 us
    unnamed x46 -> x28, local copies, waits for them, and re-layouts: 13 us -> 3.71 us
    pallas_call x1, Pallas kernels: 3.13 us -> 5.04 us  [products(): pl.pallas_call(products_kernel, in_specs=memory(pltpu.SMEM, *[pltpu.VMEM]...]
  transfers between devices with their start and end apart: 13 -> 13, of which waited for: 5 -> 5; matrix products, arithmetic and copies ran while one was open for 1% -> 1% of each run, Pallas kernels for 18% -> 20%
where the time goes in v10:
time: 124 us; the launch traced here: 123 us
  Pallas kernels  45.5 us (37%)
  starting transfers between devices  40.8 us (33%)
  waiting for transfers between devices  19.7 us (16%)
  blocking collectives  10.4 us (8%)
  local copies, waits for them, and re-layouts  5.13 us (4%)
    ppermute x6, starting transfers between devices, from_neighbours(): return [lax.ppermute(x, 'rows', swaps(devices, first)) for first in (1, 0)]  18.2 us
    all_to_all x2, waiting for transfers between devices, exchange(): return lax.all_to_all(x, 'rows', 0, 0, axis_index_groups=groups)  14.5 us
    all_to_all x1, blocking collectives, exchange(): return lax.all_to_all(x, 'rows', 0, 0, axis_index_groups=groups)  10.4 us
    all_to_all x2, starting transfers between devices, exchange(): return lax.all_to_all(x, 'rows', 0, 0, axis_index_groups=groups)  10.4 us
    pallas_call x1, Pallas kernels, final(): pl.pallas_call(functools.partial(final_kernel, factor=factor), in_specs=m...  10.3 us
    pallas_call x1, Pallas kernels, split_affinity(): pl.pallas_call(split_kernel, in_specs=memory(pl.ANY, pltpu.VMEM, pltpu.VM...  8.89 us
    pallas_call x1, Pallas kernels, second_image(): pl.pallas_call(second_kernel, in_specs=memory(pltpu.SMEM, pltpu.SMEM, pl....  7.96 us
    pallas_call x1, Pallas kernels, first_image(): pl.pallas_call(first_kernel, in_specs=memory(pltpu.SMEM, pltpu.SMEM, pl.A...  7.48 us
  transfers between devices with their start and end apart: 13, of which 5 were waited for; matrix products, arithmetic and copies ran while one was open for 1% of the time, Pallas kernels for 20%

profile of v10, /device:TPU:1, one launch (start us, length us, event | category | flops | bytes accessed | tf_op | source)
XLA Modules:
  0.0 123.2 jit_solution(7562141701721668681)
XLA Ops:
  0.6 5.8 %degrees.1 = (f32[24,128]{1,0:T(8,128)}, f32[32,3072]{1,0:T(8,128)}) custom-call(f32[24,6,128,128]{3,2,1,0:T(8,128)} %a_hbm.3, f32[32,3072]{1,0:T(8,128)} %x_ref.5), custom_call_target="tpu_custom_call" | custom-call | flops 10000000 | bytes 10000000 | tf_op jit(solution)/shard_map/degrees/pallas_call | solution.py:96
  6.4 11.1 %collective-permute-start = (f32[32,3072]{1,0:T(8,128)}, f32[32,3072]{1,0:T(8,128)S(1)}, u32[]{:S(2)}, u32[]{:S(2)}) collective-permute-start(f32[32,3072]{1,0:T(8,128)} %get-tuple-element.17.xs_ref), channel_id=1, source_target_pairs={{2,4},{4,2},{6,8},{8,6},{10,12},{12,10},{14,16},{16,14},{18,20},{2... | collective-permute-start | bytes 1179656 | tf_op jit(solution)/shard_map/ppermute | solution.py:35
  17.6 8.9 %split.1 = (bf16[24,256,768]{2,1,0:T(8,128)(2,1)}, f32[32,3072]{1,0:T(8,128)}) custom-call(f32[24,6,128,128]{3,2,1,0:T(8,128)} %a_hbm.3, f32[24,128]{1,0:T(8,128)} %get-tuple-element.15.scale_ref.s_ref, f32[32,3072]{1,0:T(8,128)} %p_ref.5), custom_call_target="tpu_custom_call" | custom-call | flops 10000000 | bytes 19000000 | tf_op jit(solution)/shard_map/split/pallas_call | solution.py:130
  26.5 0.7 collective-permute-start.7
  27.2 0.9 collective-permute-start.8
  28.2 0.6 pad_add_fusion.info
  28.8 0.8 copy-done.8
  29.5 0.1 copy-done.9
  29.7 7.5 %first_image.1 = (f32[32,3072]{1,0:T(8,128)}, f32[32,3072]{1,0:T(8,128)}, f32[256,128]{1,0:T(8,128)}) custom-call(s32[4]{0:T(128)} %pad_add_fusion.info, s32[6,24]{1,0:T(8,128)} %bitcast.17, bf16[24,256,768]{2,1,0:T(8,128)(2,1)} %get-tuple-element.16.a_hbm, f32[32,3072]{1,0:T(8,128)} %x_ref.5, f32[32,3072]{1,0:T(8,128)} %get-tuple-element.17.xs_ref, ...), custom_call_target="tpu_custom_call" | custom-call | flops 4000000000 | bytes 11000000 | tf_op jit(solution)/shard_map/first_image/pallas_call | solution.py:205
  37.2 5.4 %collective-permute-start.5 = (f32[32,3072]{1,0:T(8,128)}, f32[32,3072]{1,0:T(8,128)S(1)}, u32[]{:S(2)}, u32[]{:S(2)}) collective-permute-start(f32[32,3072]{1,0:T(8,128)} %get-tuple-element.20.ys_ref), channel_id=1, source_target_pairs={{2,4},{4,2},{6,8},{8,6},{10,12},{12,10},{14,16},{16,14},{18,20},{2... | collective-permute-start | bytes 1179656 | tf_op jit(solution)/shard_map/ppermute | solution.py:35
  42.6 1.5 %collective-permute-start.2 = (f32[32,3072]{1,0:T(8,128)S(1)}, f32[32,3072]{1,0:T(8,128)S(1)}, u32[]{:S(2)}, u32[]{:S(2)}) collective-permute-start(f32[32,3072]{1,0:T(8,128)S(1)} %copy-done.2), channel_id=1, source_target_pairs={{0,1},{1,0},{2,3},{3,2},{4,5},{5,4},{6,7},{7,6},{8,9},{9,8},{10,11... | collective-permute-start | bytes 1179656 | tf_op jit(solution)/shard_map/ppermute | solution.py:429
  44.1 0.1 collective-permute-start.4
  44.3 0.5 collective-permute-start.3
  44.7 5.7 %all-to-all-start = ((f32[256,1,128]{2,1,0:T(1,128)}), f32[256,1,128]{2,1,0:T(1,128)S(1)}, u32[]{:S(2)}, u32[]{:S(2)}) async-start(f32[256,1,128]{2,1,0:T(1,128)} %bitcast.15), calls=%async_computation | async-start | bytes 262144 | tf_op jit(solution)/shard_map/all_to_all | solution.py:453
  50.5 1.5 %collective-permute-done.5.ys_odd_ref = f32[32,3072]{1,0:T(8,128)S(1)} collective-permute-done((f32[32,3072]{1,0:T(8,128)}, f32[32,3072]{1,0:T(8,128)S(1)}, u32[]{:S(2)}, u32[]{:S(2)}) %collective-permute-start.5) | collective-permute-done | bytes 393248 | tf_op jit(solution)/shard_map/ppermute | solution.py:35
  52.0 0.7 copy-done.13
  52.7 8.0 %second_image.1 = (f32[32,3072]{1,0:T(8,128)}, f32[32,3072]{1,0:T(8,128)}) custom-call(s32[4]{0:T(128)} %pad_add_fusion.info, s32[6,24]{1,0:T(8,128)} %bitcast.18, bf16[24,256,768]{2,1,0:T(8,128)(2,1)} %get-tuple-element.16.a_hbm, f32[32,3072]{1,0:T(8,128)} %get-tuple-element.20.ys_ref, f32[32,3072]{1,0:T(8,128)} %copy-done.13, ...), custom_call_target="tpu_custom_call" | custom-call | flops 4000000000 | bytes 14000000 | tf_op jit(solution)/shard_map/second_image/pallas_call | solution.py:244
  60.8 2.6 %all-to-all-done = f32[256,1,128]{2,1,0:T(1,128)S(1)} async-done(((f32[256,1,128]{2,1,0:T(1,128)}), f32[256,1,128]{2,1,0:T(1,128)S(1)}, u32[]{:S(2)}, u32[]{:S(2)}) %all-to-all-start) | async-done | bytes 131104 | tf_op jit(solution)/shard_map/all_to_all | solution.py:453
  63.4 0.6 copy-done.5
  64.0 0.1 copy-done.12
  64.2 5.0 %products.1 = (bf16[192,3072]{1,0:T(8,128)(2,1)}, bf16[192,3072]{1,0:T(8,128)(2,1)}, f32[384,128]{1,0:T(8,128)}) custom-call(s32[4]{0:T(128)} %pad_add_fusion.info, f32[256,128]{1,0:T(8,128)} %bitcast.16, f32[32,3072]{1,0:T(8,128)} %x_ref.5, f32[32,3072]{1,0:T(8,128)} %get-tuple-element.19.y_ref, f32[32,3072]{1,0:T(8,128)} %p_ref.5, f32[32,3072]{1,0:T(8,128)} %copy-done.10, ...), custom_call_target="tpu_custom_call" | custom-call | flops 2000000000 | bytes 6000000 | tf_op jit(solution)/shard_map/products/pallas_call | solution.py:302
  69.2 10.4 %all_to_all.20 = f32[16,24,128]{2,1,0:T(8,128)S(1)} all-to-all(f32[16,24,128]{2,1,0:T(8,128)} %bitcast.14), channel_id=1, replica_groups={{0,2,4,6,8,10,12,14,16,18,20,22,24,26,28,30},{32,34,36,38,40,42,44,46,4..., dimensions={0} | all-to-all | bytes 393216 | tf_op jit(solution)/shard_map/all_to_all | solution.py:51
  79.7 0.6 broadcast_in_dim.6
  80.3 6.9 %all-to-all-start.2 = ((f32[8,24,128]{2,1,0:T(8,128)}), f32[8,24,128]{2,1,0:T(8,128)S(1)}, u32[]{:S(2)}, u32[]{:S(2)}) async-start(f32[8,24,128]{2,1,0:T(8,128)} %broadcast_in_dim.6), calls=%async_computation.2 | async-start | bytes 196608 | tf_op jit(solution)/shard_map/all_to_all | solution.py:51
  87.2 7.6 %all-to-all-done.2 = f32[8,24,128]{2,1,0:T(8,128)S(1)} async-done(((f32[8,24,128]{2,1,0:T(8,128)}), f32[8,24,128]{2,1,0:T(8,128)S(1)}, u32[]{:S(2)}, u32[]{:S(2)}) %all-to-all-start.2) | async-done | bytes 98336 | tf_op jit(solution)/shard_map/all_to_all | solution.py:51
  94.9 0.7 broadcast_in_dim.7
  95.6 3.5 %all-to-all-start.3 = ((f32[16,24,128]{2,1,0:T(8,128)}), f32[16,24,128]{2,1,0:T(8,128)S(1)}, u32[]{:S(2)}, u32[]{:S(2)}) async-start(f32[16,24,128]{2,1,0:T(8,128)} %broadcast_in_dim.7), calls=%async_computation.3 | async-start | bytes 393216 | tf_op jit(solution)/shard_map/all_to_all | solution.py:51
  99.1 6.9 %all-to-all-done.3 = f32[16,24,128]{2,1,0:T(8,128)S(1)} async-done(((f32[16,24,128]{2,1,0:T(8,128)}), f32[16,24,128]{2,1,0:T(8,128)S(1)}, u32[]{:S(2)}, u32[]{:S(2)}) %all-to-all-start.3) | async-done | bytes 196640 | tf_op jit(solution)/shard_map/all_to_all | solution.py:51
  106.0 4.3 %collective-permute-start.9 = (f32[384,128]{1,0:T(8,128)S(1)}, f32[384,128]{1,0:T(8,128)S(1)}, u32[]{:S(2)}, u32[]{:S(2)}) collective-permute-start(f32[384,128]{1,0:T(8,128)S(1)} %bitcast.12), channel_id=1, source_target_pairs={{0,1},{1,0},{2,3},{3,2},{4,5},{5,4},{6,7},{7,6},{8,9},{9,8},{10,11... | collective-permute-start | bytes 589832 | tf_op jit(solution)/shard_map/ppermute | solution.py:429
  110.4 1.0 collective-permute-done.9.theirs_ref
  111.4 1.3 %copy-done = bf16[192,3072]{1,0:T(8,128)(2,1)S(1)} copy-done((bf16[192,3072]{1,0:T(8,128)(2,1)S(1)}, bf16[192,3072]{1,0:T(8,128)(2,1)}, u32[]{:S(2)}) %copy-start) | copy-done | bytes 1179672
  112.7 10.3 %final.1 = (f32[32,3072]{1,0:T(8,128)}, f32[32,3072]{1,0:T(8,128)}, f32[192,192]{1,0:T(8,128)}) custom-call(s32[4]{0:T(128)S(1)} %copy-done.1, f32[384,128]{1,0:T(8,128)S(1)} %bitcast.13, f32[384,128]{1,0:T(8,128)S(1)} %collective-permute-done.9.theirs_ref, f32[64,192]{1,0:T(8,128)S(1)} %maximum_bitcast_fusion.chosen_ref, bf16[192,3072]{1,0:T(8,128)(2,1)S(1)} %copy-done, ...), custom_call_target="tpu_custom_call" | custom-call | flops 400000000 | bytes 4000000 | tf_op jit(solution)/shard_map/final/pallas_call | solution.py:417
  (39 shorter events, 0.2 us)
Async XLA Ops:
  6.4 22.3 %collective-permute-start = (f32[32,3072]{1,0:T(8,128)}, f32[32,3072]{1,0:T(8,128)S(1)}, u32[]{:S(2)}, u32[]{:S(2)}) collective-permute-start(f32[32,3072]{1,0:T(8,128)} %get-tuple-element.17.xs_ref), channel_id=1, source_target_pairs={{2,4},{4,2},{6,8},{8,6},{10,12},{12,10},{14,16},{16,14},{18,20},{2... | collective-permute-start | bytes 1179656 | tf_op jit(solution)/shard_map/ppermute | solution.py:35
  17.6 11.2 %collective-permute-start.1 = (f32[32,3072]{1,0:T(8,128)}, f32[32,3072]{1,0:T(8,128)S(1)}, u32[]{:S(2)}, u32[]{:S(2)}) collective-permute-start(f32[32,3072]{1,0:T(8,128)} %get-tuple-element.17.xs_ref), channel_id=1, source_target_pairs={{0,2},{2,0},{4,6},{6,4},{8,10},{10,8},{12,14},{14,12},{16,18},{18,... | collective-permute-start | bytes 1179656 | tf_op jit(solution)/shard_map/ppermute | solution.py:35
  26.5 16.1 %copy-start.2 = (f32[32,3072]{1,0:T(8,128)S(1)}, f32[32,3072]{1,0:T(8,128)}, u32[]{:S(2)}) copy-start(f32[32,3072]{1,0:T(8,128)} %x_ref.5) | copy-start | bytes 1179652
  26.5 17.6 %copy-start.3 = (f32[32,3072]{1,0:T(8,128)S(1)}, f32[32,3072]{1,0:T(8,128)}, u32[]{:S(2)}) copy-start(f32[32,3072]{1,0:T(8,128)} %p_ref.5) | copy-start | bytes 1179652
  26.5 17.6 %collective-permute-start.7 = (f32[32,3072]{1,0:T(8,128)}, f32[32,3072]{1,0:T(8,128)S(1)}, u32[]{:S(2)}, u32[]{:S(2)}) collective-permute-start(f32[32,3072]{1,0:T(8,128)} %get-tuple-element.21.ps_ref), channel_id=1, source_target_pairs={{2,4},{4,2},{6,8},{8,6},{10,12},{12,10},{14,16},{16,14},{18,20},{2... | collective-permute-start | bytes 1179656 | tf_op jit(solution)/shard_map/ppermute | solution.py:35
  27.2 17.0 %collective-permute-start.8 = (f32[32,3072]{1,0:T(8,128)}, f32[32,3072]{1,0:T(8,128)S(1)}, u32[]{:S(2)}, u32[]{:S(2)}) collective-permute-start(f32[32,3072]{1,0:T(8,128)} %get-tuple-element.21.ps_ref), channel_id=1, source_target_pairs={{0,2},{2,0},{4,6},{6,4},{8,10},{10,8},{12,14},{14,12},{16,18},{18,... | collective-permute-start | bytes 1179656 | tf_op jit(solution)/shard_map/ppermute | solution.py:35
  28.8 0.8 copy-start.8
  28.8 0.9 copy-start.9
  37.2 14.8 %collective-permute-start.5 = (f32[32,3072]{1,0:T(8,128)}, f32[32,3072]{1,0:T(8,128)S(1)}, u32[]{:S(2)}, u32[]{:S(2)}) collective-permute-start(f32[32,3072]{1,0:T(8,128)} %get-tuple-element.20.ys_ref), channel_id=1, source_target_pairs={{2,4},{4,2},{6,8},{8,6},{10,12},{12,10},{14,16},{16,14},{18,20},{2... | collective-permute-start | bytes 1179656 | tf_op jit(solution)/shard_map/ppermute | solution.py:35
  42.6 9.4 %collective-permute-start.6 = (f32[32,3072]{1,0:T(8,128)}, f32[32,3072]{1,0:T(8,128)}, u32[]{:S(2)}, u32[]{:S(2)}) collective-permute-start(f32[32,3072]{1,0:T(8,128)} %get-tuple-element.20.ys_ref), channel_id=1, source_target_pairs={{0,2},{2,0},{4,6},{6,4},{8,10},{10,8},{12,14},{14,12},{16,18},{18,... | collective-permute-start | bytes 1179656 | tf_op jit(solution)/shard_map/ppermute | solution.py:35
  42.6 18.1 %collective-permute-start.2 = (f32[32,3072]{1,0:T(8,128)S(1)}, f32[32,3072]{1,0:T(8,128)S(1)}, u32[]{:S(2)}, u32[]{:S(2)}) collective-permute-start(f32[32,3072]{1,0:T(8,128)S(1)} %copy-done.2), channel_id=1, source_target_pairs={{0,1},{1,0},{2,3},{3,2},{4,5},{5,4},{6,7},{7,6},{8,9},{9,8},{10,11... | collective-permute-start | bytes 1179656 | tf_op jit(solution)/shard_map/ppermute | solution.py:429
  44.1 7.9 %copy-start.6 = (f32[32,3072]{1,0:T(8,128)}, f32[32,3072]{1,0:T(8,128)S(1)}, u32[]{:S(2)}) copy-start(f32[32,3072]{1,0:T(8,128)S(1)} %collective-permute-done.7.ps_odd_ref) | copy-start | bytes 1179652
  44.1 16.6 %collective-permute-start.4 = (f32[32,3072]{1,0:T(8,128)S(1)}, f32[32,3072]{1,0:T(8,128)S(1)}, u32[]{:S(2)}, u32[]{:S(2)}) collective-permute-start(f32[32,3072]{1,0:T(8,128)S(1)} %copy-done.3), channel_id=1, source_target_pairs={{0,1},{1,0},{2,3},{3,2},{4,5},{5,4},{6,7},{7,6},{8,9},{9,8},{10,11... | collective-permute-start | bytes 1179656 | tf_op jit(solution)/shard_map/ppermute | solution.py:429
  44.3 7.8 %copy-start.7 = (f32[32,3072]{1,0:T(8,128)}, f32[32,3072]{1,0:T(8,128)S(1)}, u32[]{:S(2)}) copy-start(f32[32,3072]{1,0:T(8,128)S(1)} %collective-permute-done.8.ps_even_ref) | copy-start | bytes 1179652
  44.3 19.1 %collective-permute-start.3 = (f32[32,3072]{1,0:T(8,128)}, f32[32,3072]{1,0:T(8,128)S(1)}, u32[]{:S(2)}, u32[]{:S(2)}) collective-permute-start(f32[32,3072]{1,0:T(8,128)} %get-tuple-element.19.y_ref), channel_id=1, source_target_pairs={{0,1},{1,0},{2,3},{3,2},{4,5},{5,4},{6,7},{7,6},{8,9},{9,8},{10,11... | collective-permute-start | bytes 1179656 | tf_op jit(solution)/shard_map/ppermute | solution.py:429
  44.7 18.6 %all-to-all-start = ((f32[256,1,128]{2,1,0:T(1,128)}), f32[256,1,128]{2,1,0:T(1,128)S(1)}, u32[]{:S(2)}, u32[]{:S(2)}) async-start(f32[256,1,128]{2,1,0:T(1,128)} %bitcast.15), calls=%async_computation | async-start | bytes 262144 | tf_op jit(solution)/shard_map/all_to_all | solution.py:453
  50.5 48.7 %copy-start.4 = (f32[192,64]{0,1:T(8,128)S(1)}, f32[192,64]{0,1:T(8,128)}, u32[]{:S(2)}) copy-start(f32[192,64]{0,1:T(8,128)} %param.9) | copy-start | bytes 147460
  50.5 60.9 %copy-start.1 = (s32[4]{0:T(128)S(1)}, s32[4]{0:T(128)}, u32[]{:S(2)}) copy-start(s32[4]{0:T(128)} %pad_add_fusion.info) | copy-start | bytes 52
  52.0 0.7 copy-start.13
  60.7 2.7 %copy-start.10 = (f32[32,3072]{1,0:T(8,128)}, f32[32,3072]{1,0:T(8,128)S(1)}, u32[]{:S(2)}) copy-start(f32[32,3072]{1,0:T(8,128)S(1)} %collective-permute-done.2.xo_ref) | copy-start | bytes 1179652
  60.7 2.7 %copy-start.11 = (f32[32,3072]{1,0:T(8,128)}, f32[32,3072]{1,0:T(8,128)S(1)}, u32[]{:S(2)}) copy-start(f32[32,3072]{1,0:T(8,128)S(1)} %collective-permute-done.4.po_ref) | copy-start | bytes 1179652
  63.4 0.6 copy-start.5
  63.4 0.8 copy-start.12
  80.3 14.5 %all-to-all-start.2 = ((f32[8,24,128]{2,1,0:T(8,128)}), f32[8,24,128]{2,1,0:T(8,128)S(1)}, u32[]{:S(2)}, u32[]{:S(2)}) async-start(f32[8,24,128]{2,1,0:T(8,128)} %broadcast_in_dim.6), calls=%async_computation.2 | async-start | bytes 196608 | tf_op jit(solution)/shard_map/all_to_all | solution.py:51
  95.6 10.5 %all-to-all-start.3 = ((f32[16,24,128]{2,1,0:T(8,128)}), f32[16,24,128]{2,1,0:T(8,128)S(1)}, u32[]{:S(2)}, u32[]{:S(2)}) async-start(f32[16,24,128]{2,1,0:T(8,128)} %broadcast_in_dim.7), calls=%async_computation.3 | async-start | bytes 393216 | tf_op jit(solution)/shard_map/all_to_all | solution.py:51
  106.0 5.4 %collective-permute-start.9 = (f32[384,128]{1,0:T(8,128)S(1)}, f32[384,128]{1,0:T(8,128)S(1)}, u32[]{:S(2)}, u32[]{:S(2)}) collective-permute-start(f32[384,128]{1,0:T(8,128)S(1)} %bitcast.12), channel_id=1, source_target_pairs={{0,1},{1,0},{2,3},{3,2},{4,5},{5,4},{6,7},{7,6},{8,9},{9,8},{10,11... | collective-permute-start | bytes 589832 | tf_op jit(solution)/shard_map/ppermute | solution.py:429
  111.4 1.3 %copy-start = (bf16[192,3072]{1,0:T(8,128)(2,1)S(1)}, bf16[192,3072]{1,0:T(8,128)(2,1)}, u32[]{:S(2)}) copy-start(bf16[192,3072]{1,0:T(8,128)(2,1)} %get-tuple-element.25.high_hbm) | copy-start | bytes 3538948
